TPU v7x, 128 devices: a whole 4x4x4 slice. The times are simulated.
128 devices in a mesh: lat: 32 (over z, x, core), lon: 4 (over y).
Axes of the slice: x: 4, y: 4, z: 4, core: 2. Of those that a mesh axis runs over, the one named last changes fastest.
Arguments:
- grid_latent: bfloat16 [262144, 256], P(('lat', 'lon')), may hold values from -6 to 6
- mesh_latent: bfloat16 [32768, 256], P(('lat', 'lon')), may hold values from -6 to 6
- encode_sends: int32 [384, 4, 128], P(('lat', 'lon')), may hold values from 0 to 2047
- encode_sources: int32 [524288], P(('lat', 'lon')), may hold values from 0 to 1535, as said below
- encode_targets: int32 [524288], P(('lat', 'lon')), may hold values from 0 to 256, as said below
- mesh_sources: int32 [262144], P(('lat', 'lon')), may hold values from 0 to 2303, as said below
- mesh_targets: int32 [262144], P(('lat', 'lon')), may hold values from 0 to 256, as said below
- decode_sources: int32 [262144, 3], P(('lat', 'lon')), may hold values from 0 to 3071, as said below
- encode_weights: bfloat16 [4, 256, 256], replicated, may hold values from -0.375 to 0.375
- process_weights: bfloat16 [8, 256, 256], replicated, may hold values from -0.375 to 0.375
- decode_weights: bfloat16 [4, 256, 256], replicated, may hold values from -0.375 to 0.375
- norm_gains: bfloat16 [4, 256], replicated, may hold values from 0.099609375 to 1.8984375
Outputs:
- grid_out: bfloat16 [262144, 256], P(('lat', 'lon'))
- mesh_out: bfloat16 [32768, 256], P(('lat', 'lon'))
Inputs may be any that keep to these rules, and one draw needn't show every extreme that they name: `encode_sources`: rows of encode_rows: a device of the first band uses none from the band below, one of the last band none from the band above. `encode_targets`: per device, 4096 edge slots; 256 marks padding, which comes after all live edges; devices of the first and last bands have no padding. `mesh_sources`: rows of the neighbourhood: a device of the first band uses none from the band below, one of the last band none from the band above. `mesh_targets`: per device, 2048 edge slots; 256 marks padding, which comes after all live edges; devices of the first and last bands have no padding. `decode_sources`: rows of band_table: a device of the first band uses none from the band below, one of the last band none from the band above.
All inputs are finite; a program needn't handle non-finite values.
Results may differ from a plain program's by a relative error of at most 0.013.
Values may be sent and summed in bfloat16 or wider, within the bound.
No kernel may reach another device: no remote copies, remote signals or barrier semaphores. Data moves between devices by JAX's collectives and lax.ppermute only.
A program may use at most 64 MiB of HBM per device.

v0:
```python
import jax
import jax.numpy as jnp
from jax import lax
from jax.sharding import PartitionSpec as P

STEPS = 2


epsilon = 1e-05


def shifted(x, axis, by):
    length = lax.axis_size(axis)
    pairs = [(i, i + by) for i in range(length) if 0 <= i + by < length]
    return lax.ppermute(x, axis, pairs)


def extended(cells, sides, width, closed):
    for axis, dim in sides:
        count = lax.axis_size(axis)
        ends = count if closed else count - 1
        head = lax.slice_in_dim(cells, 0, width, axis=dim)
        tail = lax.slice_in_dim(cells, cells.shape[dim] - width, cells.shape[dim], axis=dim)
        cells = jnp.concatenate(
            [
                lax.ppermute(tail, axis, [(i, (i + 1) % count) for i in range(ends)]),
                cells,
                lax.ppermute(head, axis, [((i + 1) % count, i) for i in range(ends)]),
            ],
            axis=dim,
        )
    return cells


def project(source_rows, weight):
    return jnp.dot(source_rows, weight, preferred_element_type=jnp.float32).astype(jnp.bfloat16)


def node_update(latent, summed, gain_row, node_weight):
    mean_square = jnp.mean(summed * summed, axis=-1, keepdims=True)
    scaled = (summed * lax.rsqrt(mean_square + epsilon) * gain_row.astype(jnp.float32)).astype(
        jnp.bfloat16
    )
    return (
        latent.astype(jnp.float32)
        + jnp.dot(scaled, node_weight, preferred_element_type=jnp.float32)
    ).astype(jnp.bfloat16)


def select_rows(table, indices):
    table_ids = lax.broadcasted_iota(jnp.int32, (indices.shape[0], table.shape[0]), 1)
    selector = (table_ids == indices[:, None]).astype(jnp.bfloat16)
    return jnp.dot(selector, table, preferred_element_type=jnp.float32)


def block_total(targets, block_rows):
    return targets.shape[0] // block_rows


def edge_sums(source_rows, target_proj, sources, targets, edge_weight):
    node_count = target_proj.shape[0]
    block_rows = 512
    node_ids = lax.broadcasted_iota(jnp.int32, (node_count, block_rows), 0)

    def one_block(block_index, summed):
        first_edge = block_index * block_rows
        edge_src = lax.dynamic_slice_in_dim(sources, first_edge, block_rows)
        edge_dst = lax.dynamic_slice_in_dim(targets, first_edge, block_rows)
        picked = select_rows(source_rows, edge_src)
        clamped = jnp.minimum(edge_dst, node_count - 1)
        pointer = (node_ids == clamped[None, :]).astype(jnp.float32)
        target_rows = lax.dot_general(
            pointer,
            target_proj,
            (((0,), (0,)), ((), ())),
            precision=lax.Precision.HIGHEST,
            preferred_element_type=jnp.float32,
        )
        hidden = jax.nn.silu(picked + target_rows).astype(jnp.bfloat16)
        message = jnp.dot(hidden, edge_weight, preferred_element_type=jnp.float32).astype(
            jnp.bfloat16
        )
        incidence = (node_ids == edge_dst[None, :]).astype(jnp.bfloat16)
        return summed + jnp.dot(incidence, message, preferred_element_type=jnp.float32)

    block_count = block_total(targets, block_rows)
    return lax.fori_loop(0, block_count, one_block, jnp.zeros(target_proj.shape, jnp.float32))


def shards(
    grid_latent,
    mesh_latent,
    encode_sends,
    encode_sources,
    encode_targets,
    mesh_sources,
    mesh_targets,
    decode_sources,
    encode_weights,
    process_weights,
    decode_weights,
    norm_gains,
):
    lon_count = lax.axis_size("lon")
    latent = grid_latent.shape[1]
    node_count = mesh_latent.shape[0]
    grid_count = grid_latent.shape[0]
    slot_count = encode_sends.shape[2]
    picked = (
        select_rows(grid_latent, encode_sends.reshape(-1))
        .astype(jnp.bfloat16)
        .reshape(3, lon_count, slot_count, latent)
    )
    banded = lax.all_to_all(picked, "lon", split_axis=1, concat_axis=1, tiled=True)
    from_lower = shifted(banded[2], "lat", 1)
    from_upper = shifted(banded[0], "lat", -1)
    arrived = jnp.stack([from_lower, banded[1], from_upper])
    arrived = arrived.reshape(3 * lon_count * slot_count, latent)
    source_rows = project(arrived, encode_weights[0])
    target_proj = jnp.dot(mesh_latent, encode_weights[1], preferred_element_type=jnp.float32)
    summed = edge_sums(source_rows, target_proj, encode_sources, encode_targets, encode_weights[2])
    mesh_now = node_update(mesh_latent, summed, norm_gains[0], encode_weights[3])
    for step_number in range(STEPS):
        weights_now = process_weights[4 * step_number : 4 * step_number + 4]
        sent_rows = mesh_now
        around_rows = extended(sent_rows[None], (("lon", 0),), 1, True)
        around_rows = extended(around_rows[None], (("lat", 0),), 1, False)
        around_rows = around_rows.reshape(9 * node_count, latent)
        halo_rows = project(around_rows, weights_now[0])
        target_proj = jnp.dot(mesh_now, weights_now[1], preferred_element_type=jnp.float32)
        summed = edge_sums(halo_rows, target_proj, mesh_sources, mesh_targets, weights_now[2])
        mesh_now = node_update(mesh_now, summed, norm_gains[1 + step_number], weights_now[3])
    whole_band = lax.all_gather(mesh_now, "lon", axis=0, tiled=True)
    near_rows = extended(whole_band[None], (("lat", 0),), 1, False)
    near_rows = near_rows.reshape(3 * lon_count * node_count, latent)
    band_table = project(near_rows, decode_weights[0])
    grid_proj = jnp.dot(grid_latent, decode_weights[1], preferred_element_type=jnp.float32)
    grid_block = 512
    block_count = grid_count // grid_block

    def decode_block(packed):
        block_sources, block_proj = packed
        gathered = select_rows(band_table, block_sources.reshape(-1)).reshape(grid_block, 3, latent)
        hidden = jax.nn.silu(gathered + block_proj[:, None, :]).astype(jnp.bfloat16)
        message = jnp.dot(
            hidden.reshape(3 * grid_block, latent),
            decode_weights[2],
            preferred_element_type=jnp.float32,
        ).astype(jnp.bfloat16)
        return jnp.sum(message.astype(jnp.float32).reshape(grid_block, 3, latent), axis=1)

    summed = lax.map(
        decode_block,
        (
            decode_sources.reshape(block_count, grid_block, 3),
            grid_proj.reshape(block_count, grid_block, latent),
        ),
    )
    summed = summed.reshape(grid_count, latent)
    grid_out = node_update(grid_latent, summed, norm_gains[STEPS + 1], decode_weights[3])
    return (grid_out, mesh_now)


def solution(mesh):
    placed = (
        P(("lat", "lon"), None),
        P(("lat", "lon"), None),
        P(("lat", "lon"), None, None),
        P(("lat", "lon")),
        P(("lat", "lon")),
        P(("lat", "lon")),
        P(("lat", "lon")),
        P(("lat", "lon"), None),
        P(),
        P(),
        P(),
        P(),
    )
    return jax.shard_map(
        shards,
        mesh=mesh,
        in_specs=placed,
        out_specs=(P(("lat", "lon"), None), P(("lat", "lon"), None)),
        check_vma=False,
    )
```

profile of v0, /device:TPU:39, one launch (start us, length us, event | category | flops | bytes accessed | tf_op | source)
XLA Modules:
  0.0 223.6 jit_solution(10807016673493038568)
XLA Ops:
  1.3 3.6 %fusion.41 = bf16[1536,256]{1,0:T(8,128)(2,1)S(1)} fusion(bf16[2048,256]{1,0:T(8,128)(2,1)} %param.20, s32[1536]{0:T(1024)S(1)} %eq.200), kind=kOutput, calls=%fused_computation.68 | convolution fusion | flops 1614151680 | bytes 1841152 | tf_op jit(solution)/shard_map/dot_general | solution.py:53
  5.9 4.3 %all-to-all-start = ((bf16[3,4,128,256]{3,2,0,1:T(8,128)(2,1)}), bf16[3,4,128,256]{3,2,0,1:T(8,128)(2,1)S(1)}, u32[]{:S(2)}, u32[]{:S(2)}) async-start(bf16[3,4,128,256]{3,2,0,1:T(8,128)(2,1)} %copy.16), calls=%async_computation | async-start | bytes 1572864 | tf_op jit(solution)/shard_map/all_to_all | solution.py:114
  10.2 11.4 %all-to-all-done = bf16[3,4,128,256]{3,2,0,1:T(8,128)(2,1)S(1)} async-done(((bf16[3,4,128,256]{3,2,0,1:T(8,128)(2,1)}), bf16[3,4,128,256]{3,2,0,1:T(8,128)(2,1)S(1)}, u32[]{:S(2)}, u32[]{:S(2)}) %all-to-all-start) | async-done | bytes 786464 | tf_op jit(solution)/shard_map/all_to_all | solution.py:114
  21.6 5.2 %collective-permute-start = (bf16[4,128,256]{2,1,0:T(8,128)(2,1)S(1)}, bf16[4,128,256]{2,1,0:T(8,128)(2,1)S(1)}, u32[]{:S(2)}, u32[]{:S(2)}) collective-permute-start(bf16[4,128,256]{2,1,0:T(8,128)(2,1)S(1)} %get-tuple-element.664), channel_id=1, source_target_pairs={{0,4},{4,8},{8,12},{12,16},{16,20},{20,24},{24,28},{28,32},{32,36}... | collective-permute-start | bytes 786440 | tf_op jit(solution)/shard_map/ppermute | solution.py:15
  26.8 1.9 collective-permute-start.1
  30.1 6.5 %collective-permute-done.1 = bf16[4,128,256]{2,1,0:T(8,128)(2,1)S(1)} collective-permute-done((bf16[4,128,256]{2,1,0:T(8,128)(2,1)S(1)}, bf16[4,128,256]{2,1,0:T(8,128)(2,1)S(1)}, u32[]{:S(2)}, u32[]{:S(2)}) %collective-permute-start.1) | collective-permute-done | bytes 262176 | tf_op jit(solution)/shard_map/ppermute | solution.py:15
  37.1 27.2 %while.56 = (s32[]{:T(128)}, f32[256,256]{1,0:T(8,128)S(1)}, s32[4096]{0:T(1024)}, s32[4096]{0:T(1024)}, bf16[1536,256]{1,0:T(8,128)(2,1)S(1)}, /*index=5*/f32[2...) while((s32[]{:T(128)}, f32[256,256]{1,0:T(8,128)S(1)}, ...), condition=%wide.region_1.2_spmd.clone.clone, body=%wide.region_0.1_spmd.clone.clone.sunk | while | flops 941621760 | bytes 3293357 | solution.py:87
  64.5 1.2 fusion.42
  66.1 2.4 %collective-permute-start.3 = (bf16[1,256,256]{2,1,0:T(8,128)(2,1)S(1)}, bf16[1,256,256]{2,1,0:T(8,128)(2,1)S(1)}, u32[]{:S(2)}, u32[]{:S(2)}) collective-permute-start(bf16[1,256,256]{2,1,0:T(8,128)(2,1)S(1)} %bitcast.149), channel_id=1, source_target_pairs={{1,0},{2,1},{3,2},{0,3},{5,4},{6,5},{7,6},{4,7},{9,8},{10,9},{11,1... | collective-permute-start | bytes 393224 | tf_op jit(solution)/shard_map/ppermute | solution.py:28
  68.5 2.4 %collective-permute-done.2 = bf16[1,256,256]{2,1,0:T(8,128)(2,1)S(1)} collective-permute-done((bf16[1,256,256]{2,1,0:T(8,128)(2,1)S(1)}, bf16[1,256,256]{2,1,0:T(8,128)(2,1)S(1)}, u32[]{:S(2)}, u32[]{:S(2)}) %collective-permute-start.2) | collective-permute-done | bytes 131104 | tf_op jit(solution)/shard_map/ppermute | solution.py:26
  70.9 3.0 %collective-permute-start.4 = (bf16[1,3,256,256]{3,2,1,0:T(8,128)(2,1)S(1)}, bf16[1,3,256,256]{3,2,1,0:T(8,128)(2,1)S(1)}, u32[]{:S(2)}, u32[]{:S(2)}) collective-permute-start(bf16[1,3,256,256]{3,2,1,0:T(8,128)(2,1)S(1)} %maximum_bitcast_fusion), channel_id=1, source_target_pairs={{0,4},{4,8},{8,12},{12,16},{16,20},{20,24},{24,28},{28,32},{32,36}... | collective-permute-start | bytes 1179656 | tf_op jit(solution)/shard_map/ppermute | solution.py:26
  73.9 1.9 collective-permute-start.5
  76.0 2.5 %collective-permute-done.4 = bf16[1,3,256,256]{3,2,1,0:T(8,128)(2,1)S(1)} collective-permute-done((bf16[1,3,256,256]{3,2,1,0:T(8,128)(2,1)S(1)}, bf16[1,3,256,256]{3,2,1,0:T(8,128)(2,1)S(1)}, u32[]{:S(2)}, u32[]{:S(2)}) %collective-permute-start.4) | collective-permute-done | bytes 393248 | tf_op jit(solution)/shard_map/ppermute | solution.py:26
  78.6 6.5 %collective-permute-done.5 = bf16[1,3,256,256]{3,2,1,0:T(8,128)(2,1)S(1)} collective-permute-done((bf16[1,3,256,256]{3,2,1,0:T(8,128)(2,1)S(1)}, bf16[1,3,256,256]{3,2,1,0:T(8,128)(2,1)S(1)}, u32[]{:S(2)}, u32[]{:S(2)}) %collective-permute-start.5) | collective-permute-done | bytes 393248 | tf_op jit(solution)/shard_map/ppermute | solution.py:28
  85.9 9.2 %while.57 = (s32[]{:T(128)}, f32[256,256]{1,0:T(8,128)S(1)}, s32[2048]{0:T(1024)S(1)}, s32[2048]{0:T(1024)S(1)}, bf16[2304,256]{1,0:T(8,128)(2,1)S(1)}, /*index=...) while((s32[]{:T(128)}, f32[256,256]{1,0:T(8,128)S(1)}, ...), condition=%wide.region_4.5_spmd.clone.clone, body=%wide.region_3.4_spmd.clone.clone.sunk | while | flops 1143341568 | bytes 3686573 | solution.py:87
  95.6 2.9 %collective-permute-start.7 = (bf16[1,256,256]{2,1,0:T(8,128)(2,1)S(1)}, bf16[1,256,256]{2,1,0:T(8,128)(2,1)S(1)}, u32[]{:S(2)}, u32[]{:S(2)}) collective-permute-start(bf16[1,256,256]{2,1,0:T(8,128)(2,1)S(1)} %bitcast.146), channel_id=1, source_target_pairs={{1,0},{2,1},{3,2},{0,3},{5,4},{6,5},{7,6},{4,7},{9,8},{10,9},{11,1... | collective-permute-start | bytes 393224 | tf_op jit(solution)/shard_map/ppermute | solution.py:28
  98.6 2.3 %collective-permute-done.6 = bf16[1,256,256]{2,1,0:T(8,128)(2,1)S(1)} collective-permute-done((bf16[1,256,256]{2,1,0:T(8,128)(2,1)S(1)}, bf16[1,256,256]{2,1,0:T(8,128)(2,1)S(1)}, u32[]{:S(2)}, u32[]{:S(2)}) %collective-permute-start.6) | collective-permute-done | bytes 131104 | tf_op jit(solution)/shard_map/ppermute | solution.py:26
  100.9 2.7 %collective-permute-start.8 = (bf16[1,3,256,256]{3,2,1,0:T(8,128)(2,1)S(1)}, bf16[1,3,256,256]{3,2,1,0:T(8,128)(2,1)S(1)}, u32[]{:S(2)}, u32[]{:S(2)}) collective-permute-start(bf16[1,3,256,256]{3,2,1,0:T(8,128)(2,1)S(1)} %maximum_bitcast_fusion.1), channel_id=1, source_target_pairs={{0,4},{4,8},{8,12},{12,16},{16,20},{20,24},{24,28},{28,32},{32,36}... | collective-permute-start | bytes 1179656 | tf_op jit(solution)/shard_map/ppermute | solution.py:26
  103.6 2.1 collective-permute-start.9
  105.9 2.4 %collective-permute-done.8 = bf16[1,3,256,256]{3,2,1,0:T(8,128)(2,1)S(1)} collective-permute-done((bf16[1,3,256,256]{3,2,1,0:T(8,128)(2,1)S(1)}, bf16[1,3,256,256]{3,2,1,0:T(8,128)(2,1)S(1)}, u32[]{:S(2)}, u32[]{:S(2)}) %collective-permute-start.8) | collective-permute-done | bytes 393248 | tf_op jit(solution)/shard_map/ppermute | solution.py:26
  108.3 6.5 %collective-permute-done.9 = bf16[1,3,256,256]{3,2,1,0:T(8,128)(2,1)S(1)} collective-permute-done((bf16[1,3,256,256]{3,2,1,0:T(8,128)(2,1)S(1)}, bf16[1,3,256,256]{3,2,1,0:T(8,128)(2,1)S(1)}, u32[]{:S(2)}, u32[]{:S(2)}) %collective-permute-start.9) | collective-permute-done | bytes 393248 | tf_op jit(solution)/shard_map/ppermute | solution.py:28
  115.4 9.3 %while.58 = (s32[]{:T(128)}, f32[256,256]{1,0:T(8,128)S(1)}, s32[2048]{0:T(1024)S(1)}, s32[2048]{0:T(1024)S(1)}, bf16[2304,256]{1,0:T(8,128)(2,1)S(1)}, /*index=...) while((s32[]{:T(128)}, f32[256,256]{1,0:T(8,128)S(1)}, ...), condition=%wide.region_7.8_spmd.clone.clone, body=%wide.region_6.7_spmd.clone.clone.sunk | while | flops 1143341568 | bytes 3686573 | solution.py:87
  125.1 11.8 %all_gather.3 = bf16[1024,256]{1,0:T(8,128)(2,1)S(1)} all-gather(bf16[256,256]{1,0:T(8,128)(2,1)S(1)} %fusion.44), channel_id=1, replica_groups=mesh['lat'=32,'lon'=4] {'lon'}, dimensions={0}, use_global_device_ids=true | all-gather | bytes 655360 | tf_op jit(solution)/shard_map/all_gather | solution.py:133
  136.9 3.7 %collective-permute-start.10 = (bf16[1,1024,256]{2,1,0:T(8,128)(2,1)S(1)}, bf16[1,1024,256]{2,1,0:T(8,128)(2,1)S(1)}, u32[]{:S(2)}, u32[]{:S(2)}) collective-permute-start(bf16[1,1024,256]{2,1,0:T(8,128)(2,1)S(1)} %bitcast.142), channel_id=1, source_target_pairs={{0,4},{4,8},{8,12},{12,16},{16,20},{20,24},{24,28},{28,32},{32,36}... | collective-permute-start | bytes 1572872 | tf_op jit(solution)/shard_map/ppermute | solution.py:26
  140.6 1.9 collective-permute-start.11
  142.6 2.1 copy.15
  144.7 1.8 fusion.46
  146.7 6.5 %collective-permute-done.11 = bf16[1,1024,256]{2,1,0:T(8,128)(2,1)S(1)} collective-permute-done((bf16[1,1024,256]{2,1,0:T(8,128)(2,1)S(1)}, bf16[1,1024,256]{2,1,0:T(8,128)(2,1)S(1)}, u32[]{:S(2)}, u32[]{:S(2)}) %collective-permute-start.11) | collective-permute-done | bytes 524320 | tf_op jit(solution)/shard_map/ppermute | solution.py:28
  153.4 1.8 convolution_convert_fusion.6
  155.2 63.6 %while.55 = (s32[]{:T(128)}, f32[4,512,256]{2,1,0:T(8,128)}, s32[4,512,3]{2,1,0:T(8,128)}, bf16[3072,256]{1,0:T(8,128)(2,1)}, f32[4,512,256]{2,1,0:T(8,128)}, /*...) while((s32[]{:T(128)}, f32[4,512,256]{2,1,0:T(8,128)}, s32[4,512,3]{2,1,0:T(8,128)}, ...), condition=%wide.region_11.12_spmd, body=%wide.region_9.11_spmd.sunk | while | flops 2625372160 | bytes 17465952 | solution.py:152
  156.6 1.7 add.307
  159.5 6.9 %fusion.125 = f32[1536,256]{1,0:T(8,128)} fusion(f32[1536,256]{1,0:T(8,128)} %add.307, bf16[3072,256]{1,0:T(8,128)(2,1)} %get-tuple-element.967, s32[1536]{0:T(1024)S(1)} %eq.368, bf16[4,256,256]{2,1,0:T(8,128)(2,1)S(1)} %get-tuple-element.969), kind=kOutput, calls=%fused_computation.8.clone.1 | convolution fusion | flops 2625110016 | bytes 4857856 | tf_op jit(solution)/shard_map/while/body/eval_jaxpr/dot_general | solution.py:145
  166.4 2.5 %reshape.113 = f32[512,3,256]{2,1,0:T(4,128)S(1)} reshape(f32[1536,256]{1,0:T(8,128)} %fusion.125) | data formatting | bytes 3145728 | tf_op jit(solution)/shard_map/while/body/eval_jaxpr/reshape | solution.py:150
  169.0 1.2 reduce_sum.54
  172.5 1.7 add.307
  175.4 6.9 %fusion.125 = f32[1536,256]{1,0:T(8,128)} fusion(f32[1536,256]{1,0:T(8,128)} %add.307, bf16[3072,256]{1,0:T(8,128)(2,1)} %get-tuple-element.967, s32[1536]{0:T(1024)S(1)} %eq.368, bf16[4,256,256]{2,1,0:T(8,128)(2,1)S(1)} %get-tuple-element.969), kind=kOutput, calls=%fused_computation.8.clone.1 | convolution fusion | flops 2625110016 | bytes 4857856 | tf_op jit(solution)/shard_map/while/body/eval_jaxpr/dot_general | solution.py:145
  182.3 2.5 %reshape.113 = f32[512,3,256]{2,1,0:T(4,128)S(1)} reshape(f32[1536,256]{1,0:T(8,128)} %fusion.125) | data formatting | bytes 3145728 | tf_op jit(solution)/shard_map/while/body/eval_jaxpr/reshape | solution.py:150
  184.9 1.2 reduce_sum.54
  188.4 1.7 add.307
  191.3 6.9 %fusion.125 = f32[1536,256]{1,0:T(8,128)} fusion(f32[1536,256]{1,0:T(8,128)} %add.307, bf16[3072,256]{1,0:T(8,128)(2,1)} %get-tuple-element.967, s32[1536]{0:T(1024)S(1)} %eq.368, bf16[4,256,256]{2,1,0:T(8,128)(2,1)S(1)} %get-tuple-element.969), kind=kOutput, calls=%fused_computation.8.clone.1 | convolution fusion | flops 2625110016 | bytes 4857856 | tf_op jit(solution)/shard_map/while/body/eval_jaxpr/dot_general | solution.py:145
  198.2 2.5 %reshape.113 = f32[512,3,256]{2,1,0:T(4,128)S(1)} reshape(f32[1536,256]{1,0:T(8,128)} %fusion.125) | data formatting | bytes 3145728 | tf_op jit(solution)/shard_map/while/body/eval_jaxpr/reshape | solution.py:150
  200.8 1.2 reduce_sum.54
  204.3 1.7 add.307
  207.2 6.9 %fusion.125 = f32[1536,256]{1,0:T(8,128)} fusion(f32[1536,256]{1,0:T(8,128)} %add.307, bf16[3072,256]{1,0:T(8,128)(2,1)} %get-tuple-element.967, s32[1536]{0:T(1024)S(1)} %eq.368, bf16[4,256,256]{2,1,0:T(8,128)(2,1)S(1)} %get-tuple-element.969), kind=kOutput, calls=%fused_computation.8.clone.1 | convolution fusion | flops 2625110016 | bytes 4857856 | tf_op jit(solution)/shard_map/while/body/eval_jaxpr/dot_general | solution.py:145
  214.1 2.5 %reshape.113 = f32[512,3,256]{2,1,0:T(4,128)S(1)} reshape(f32[1536,256]{1,0:T(8,128)} %fusion.125) | data formatting | bytes 3145728 | tf_op jit(solution)/shard_map/while/body/eval_jaxpr/reshape | solution.py:150
  216.7 1.2 reduce_sum.54
  218.8 2.1 multiply_reduce_fusion
  222.2 1.4 fusion.40
  (160 shorter events, 67.2 us)
Async XLA Ops:
  4.9 5.3 %copy-start.6 = (bf16[4,256,256]{2,1,0:T(8,128)(2,1)S(1)}, bf16[4,256,256]{2,1,0:T(8,128)(2,1)}, u32[]{:S(2)}) copy-start(bf16[4,256,256]{2,1,0:T(8,128)(2,1)} %param.28) | copy-start | bytes 1572868
  5.9 22.9 %copy-start.10 = (bf16[4,256]{1,0:T(4,128)(2,1)S(1)}, bf16[4,256]{1,0:T(4,128)(2,1)}, u32[]{:S(2)}) copy-start(bf16[4,256]{1,0:T(4,128)(2,1)} %param.31) | copy-start | bytes 6148
  5.9 22.9 %copy-start.5 = (bf16[256,256]{1,0:T(8,128)(2,1)S(1)}, bf16[256,256]{1,0:T(8,128)(2,1)}, u32[]{:S(2)}) copy-start(bf16[256,256]{1,0:T(8,128)(2,1)} %param.21) | copy-start | bytes 393220
  5.9 15.7 %all-to-all-start = ((bf16[3,4,128,256]{3,2,0,1:T(8,128)(2,1)}), bf16[3,4,128,256]{3,2,0,1:T(8,128)(2,1)S(1)}, u32[]{:S(2)}, u32[]{:S(2)}) async-start(bf16[3,4,128,256]{3,2,0,1:T(8,128)(2,1)} %copy.16), calls=%async_computation | async-start | bytes 1572864 | tf_op jit(solution)/shard_map/all_to_all | solution.py:114
  21.6 8.5 %collective-permute-start = (bf16[4,128,256]{2,1,0:T(8,128)(2,1)S(1)}, bf16[4,128,256]{2,1,0:T(8,128)(2,1)S(1)}, u32[]{:S(2)}, u32[]{:S(2)}) collective-permute-start(bf16[4,128,256]{2,1,0:T(8,128)(2,1)S(1)} %get-tuple-element.664), channel_id=1, source_target_pairs={{0,4},{4,8},{8,12},{12,16},{16,20},{20,24},{24,28},{28,32},{32,36}... | collective-permute-start | bytes 786440 | tf_op jit(solution)/shard_map/ppermute | solution.py:15
  26.8 9.8 %collective-permute-start.1 = (bf16[4,128,256]{2,1,0:T(8,128)(2,1)S(1)}, bf16[4,128,256]{2,1,0:T(8,128)(2,1)S(1)}, u32[]{:S(2)}, u32[]{:S(2)}) collective-permute-start(bf16[4,128,256]{2,1,0:T(8,128)(2,1)S(1)} %get-tuple-element.665), channel_id=1, source_target_pairs={{4,0},{8,4},{12,8},{16,12},{20,16},{24,20},{28,24},{32,28},{36,32}... | collective-permute-start | bytes 786440 | tf_op jit(solution)/shard_map/ppermute | solution.py:15
  64.4 11.5 %copy-start.3 = (bf16[8,256,256]{2,1,0:T(8,128)(2,1)S(1)}, bf16[8,256,256]{2,1,0:T(8,128)(2,1)}, u32[]{:S(2)}) copy-start(bf16[8,256,256]{2,1,0:T(8,128)(2,1)} %param.29) | copy-start | bytes 3145732
  65.7 5.1 %collective-permute-start.2 = (bf16[1,256,256]{2,1,0:T(8,128)(2,1)S(1)}, bf16[1,256,256]{2,1,0:T(8,128)(2,1)S(1)}, u32[]{:S(2)}, u32[]{:S(2)}) collective-permute-start(bf16[1,256,256]{2,1,0:T(8,128)(2,1)S(1)} %bitcast.148), channel_id=1, source_target_pairs={{0,1},{1,2},{2,3},{3,0},{4,5},{5,6},{6,7},{7,4},{8,9},{9,10},{10,1... | collective-permute-start | bytes 393224 | tf_op jit(solution)/shard_map/ppermute | solution.py:26
  66.1 4.7 %collective-permute-start.3 = (bf16[1,256,256]{2,1,0:T(8,128)(2,1)S(1)}, bf16[1,256,256]{2,1,0:T(8,128)(2,1)S(1)}, u32[]{:S(2)}, u32[]{:S(2)}) collective-permute-start(bf16[1,256,256]{2,1,0:T(8,128)(2,1)S(1)} %bitcast.149), channel_id=1, source_target_pairs={{1,0},{2,1},{3,2},{0,3},{5,4},{6,5},{7,6},{4,7},{9,8},{10,9},{11,1... | collective-permute-start | bytes 393224 | tf_op jit(solution)/shard_map/ppermute | solution.py:28
  70.9 7.7 %collective-permute-start.4 = (bf16[1,3,256,256]{3,2,1,0:T(8,128)(2,1)S(1)}, bf16[1,3,256,256]{3,2,1,0:T(8,128)(2,1)S(1)}, u32[]{:S(2)}, u32[]{:S(2)}) collective-permute-start(bf16[1,3,256,256]{3,2,1,0:T(8,128)(2,1)S(1)} %maximum_bitcast_fusion), channel_id=1, source_target_pairs={{0,4},{4,8},{8,12},{12,16},{16,20},{20,24},{24,28},{28,32},{32,36}... | collective-permute-start | bytes 1179656 | tf_op jit(solution)/shard_map/ppermute | solution.py:26
  73.9 11.2 %collective-permute-start.5 = (bf16[1,3,256,256]{3,2,1,0:T(8,128)(2,1)S(1)}, bf16[1,3,256,256]{3,2,1,0:T(8,128)(2,1)S(1)}, u32[]{:S(2)}, u32[]{:S(2)}) collective-permute-start(bf16[1,3,256,256]{3,2,1,0:T(8,128)(2,1)S(1)} %maximum_bitcast_fusion), channel_id=1, source_target_pairs={{4,0},{8,4},{12,8},{16,12},{20,16},{24,20},{28,24},{32,28},{36,32}... | collective-permute-start | bytes 1179656 | tf_op jit(solution)/shard_map/ppermute | solution.py:28
  85.2 0.7 copy-start.8
  85.2 0.7 copy-start.9
  95.6 5.3 %collective-permute-start.6 = (bf16[1,256,256]{2,1,0:T(8,128)(2,1)S(1)}, bf16[1,256,256]{2,1,0:T(8,128)(2,1)S(1)}, u32[]{:S(2)}, u32[]{:S(2)}) collective-permute-start(bf16[1,256,256]{2,1,0:T(8,128)(2,1)S(1)} %bitcast.145), channel_id=1, source_target_pairs={{0,1},{1,2},{2,3},{3,0},{4,5},{5,6},{6,7},{7,4},{8,9},{9,10},{10,1... | collective-permute-start | bytes 393224 | tf_op jit(solution)/shard_map/ppermute | solution.py:26
  95.6 5.2 %collective-permute-start.7 = (bf16[1,256,256]{2,1,0:T(8,128)(2,1)S(1)}, bf16[1,256,256]{2,1,0:T(8,128)(2,1)S(1)}, u32[]{:S(2)}, u32[]{:S(2)}) collective-permute-start(bf16[1,256,256]{2,1,0:T(8,128)(2,1)S(1)} %bitcast.146), channel_id=1, source_target_pairs={{1,0},{2,1},{3,2},{0,3},{5,4},{6,5},{7,6},{4,7},{9,8},{10,9},{11,1... | collective-permute-start | bytes 393224 | tf_op jit(solution)/shard_map/ppermute | solution.py:28
  100.9 7.4 %collective-permute-start.8 = (bf16[1,3,256,256]{3,2,1,0:T(8,128)(2,1)S(1)}, bf16[1,3,256,256]{3,2,1,0:T(8,128)(2,1)S(1)}, u32[]{:S(2)}, u32[]{:S(2)}) collective-permute-start(bf16[1,3,256,256]{3,2,1,0:T(8,128)(2,1)S(1)} %maximum_bitcast_fusion.1), channel_id=1, source_target_pairs={{0,4},{4,8},{8,12},{12,16},{16,20},{20,24},{24,28},{28,32},{32,36}... | collective-permute-start | bytes 1179656 | tf_op jit(solution)/shard_map/ppermute | solution.py:26
  103.6 11.2 %collective-permute-start.9 = (bf16[1,3,256,256]{3,2,1,0:T(8,128)(2,1)S(1)}, bf16[1,3,256,256]{3,2,1,0:T(8,128)(2,1)S(1)}, u32[]{:S(2)}, u32[]{:S(2)}) collective-permute-start(bf16[1,3,256,256]{3,2,1,0:T(8,128)(2,1)S(1)} %maximum_bitcast_fusion.1), channel_id=1, source_target_pairs={{4,0},{8,4},{12,8},{16,12},{20,16},{24,20},{28,24},{32,28},{36,32}... | collective-permute-start | bytes 1179656 | tf_op jit(solution)/shard_map/ppermute | solution.py:28
  124.7 20.0 %copy-start.1 = (bf16[2048,256]{1,0:T(8,128)(2,1)S(1)}, bf16[2048,256]{1,0:T(8,128)(2,1)}, u32[]{:S(2)}) copy-start(bf16[2048,256]{1,0:T(8,128)(2,1)} %param.20) | copy-start | bytes 3145732
  125.1 21.4 %copy-start.4 = (bf16[256,256]{1,0:T(8,128)(2,1)}, bf16[256,256]{1,0:T(8,128)(2,1)S(1)}, u32[]{:S(2)}) copy-start(bf16[256,256]{1,0:T(8,128)(2,1)S(1)} %fusion.44) | copy-start | bytes 393220
  125.1 19.6 %copy-start.7 = (bf16[4,256,256]{2,1,0:T(8,128)(2,1)S(1)}, bf16[4,256,256]{2,1,0:T(8,128)(2,1)}, u32[]{:S(2)}) copy-start(bf16[4,256,256]{2,1,0:T(8,128)(2,1)} %param.30) | copy-start | bytes 1572868
  136.9 9.8 %collective-permute-start.10 = (bf16[1,1024,256]{2,1,0:T(8,128)(2,1)S(1)}, bf16[1,1024,256]{2,1,0:T(8,128)(2,1)S(1)}, u32[]{:S(2)}, u32[]{:S(2)}) collective-permute-start(bf16[1,1024,256]{2,1,0:T(8,128)(2,1)S(1)} %bitcast.142), channel_id=1, source_target_pairs={{0,4},{4,8},{8,12},{12,16},{16,20},{20,24},{24,28},{28,32},{32,36}... | collective-permute-start | bytes 1572872 | tf_op jit(solution)/shard_map/ppermute | solution.py:26
  140.6 12.6 %collective-permute-start.11 = (bf16[1,1024,256]{2,1,0:T(8,128)(2,1)S(1)}, bf16[1,1024,256]{2,1,0:T(8,128)(2,1)S(1)}, u32[]{:S(2)}, u32[]{:S(2)}) collective-permute-start(bf16[1,1024,256]{2,1,0:T(8,128)(2,1)S(1)} %bitcast.143), channel_id=1, source_target_pairs={{4,0},{8,4},{12,8},{16,12},{20,16},{24,20},{28,24},{32,28},{36,32}... | collective-permute-start | bytes 1572872 | tf_op jit(solution)/shard_map/ppermute | solution.py:28
  218.8 2.2 copy-start
  221.0 1.2 copy-start.2
where the time goes:
time: 225 us; the launch traced here: 224 us
  matrix products  71.3 us (32%)
  waiting for transfers between devices  48.4 us (22%)
  local copies, waits for them, and re-layouts  42.5 us (19%)
  starting transfers between devices  32.6 us (14%)
  other arithmetic  15.1 us (7%)
  blocking collectives  11.8 us (5%)
    dot_general x4, matrix products, decode_block(): jnp.dot(hidden.reshape(3 * grid_block, latent), decode_weights[2], prefer...  27.8 us
    ppermute x5, waiting for transfers between devices, extended(): lax.ppermute(head, axis, [((i + 1) % count, i) for i in range(ends)])  19.5 us
    dot_general x17, matrix products, select_rows(): return jnp.dot(selector, table, preferred_element_type=jnp.float32)  17 us
    add x12, local copies, waits for them, and re-layouts, decode_block(): hidden = jax.nn.silu(gathered + block_proj[:, None, :]).astype(jnp.bfloat16)  12.6 us
    all_gather x1, blocking collectives, shards(): whole_band = lax.all_gather(mesh_now, 'lon', axis=0, tiled=True)  11.8 us
    all_to_all x1, waiting for transfers between devices, shards(): lax.all_to_all(picked, 'lon', split_axis=1, concat_axis=1, tiled=True)  11.4 us
    ppermute x5, starting transfers between devices, extended(): lax.ppermute(head, axis, [((i + 1) % count, i) for i in range(ends)])  11.2 us
    reshape x4, local copies, waits for them, and re-layouts, decode_block(): message.astype(jnp.float32).reshape(grid_block, 3, latent)  10.1 us
  transfers between devices with their start and end apart: 13, of which 11 were waited for; matrix products, arithmetic and copies ran while one was open for 2% of the time, Pallas kernels for 0%

commit v1 on v0

v1 whole, which is shorter than its diff:
```python
from functools import partial

import jax
import jax.numpy as jnp
from jax import lax
from jax.experimental import pallas as pl
from jax.experimental.pallas import tpu as pltpu
from jax.sharding import PartitionSpec as P

STEPS = 2
epsilon = 1e-05
VMEM = pl.BlockSpec(memory_space=pltpu.VMEM)
SMEM = pl.BlockSpec(memory_space=pltpu.SMEM)
params = pltpu.CompilerParams(vmem_limit_bytes=50 * 2**20)
f32, bf16 = jnp.float32, jnp.bfloat16


def dot(a, b):
    return jnp.dot(a, b, preferred_element_type=f32)


def silu(z):
    half = 0.5 * z
    return half + half * jnp.tanh(half)


def node_update(latent, summed, gain_row, node_weight):
    mean_square = jnp.mean(summed * summed, axis=-1, keepdims=True)
    scaled = (summed * lax.rsqrt(mean_square + epsilon) * gain_row).astype(bf16)
    return latent.astype(f32) + dot(scaled, node_weight)


def split_rows(x):
    return x.astype(f32).reshape(x.shape[0], 2, 128)


def pick_rows(table, out, read, start, count):
    rows = [table[read(start + u)] for u in range(count)]
    for u in range(count):
        out[start + u] = rows[u]


def lane_copies(row):
    return jnp.transpose(jnp.broadcast_to(row, (128, 128)))


def send_kernel(place, lists, grid, weight, chip_out, cross_out, own_out, table, picked):
    odd, lon = place[0], place[1]
    slots = 128
    table[...] = dot(grid[...], weight[...]).reshape(table.shape)
    for part, out in enumerate((chip_out, cross_out, own_out)):
        side = (2 - 2 * odd, 2 * odd, 1)[part]
        for k in range(4):
            first = (side * 4 + lax.rem(lon + k, 4)) * slots
            base = (part * 4 + k) * slots

            @pl.loop(0, slots // 32)
            def _(i):
                rows = [table[lists[first + i * 32 + u]] for u in range(32)]
                for u in range(32):
                    picked[base + i * 32 + u] = rows[u]

            out[k] = picked[base : base + slots].reshape(slots, 256).astype(bf16)


def edge_pass(table, picked, sources, target_rows, target_proj, rows_per_block):
    edges = target_rows.shape[0] * 128
    nodes = target_proj.shape[0]
    lanes = lax.broadcasted_iota(jnp.int32, (128, nodes), 1)
    node_ids = lax.broadcasted_iota(jnp.int32, (nodes, 128), 0)
    total = jnp.zeros((nodes, 256), f32)

    def block(j, total):
        start = pl.multiple_of(j * rows_per_block, rows_per_block)

        @pl.loop(0, rows_per_block // 32)
        def _(i):
            pick_rows(table, picked, lambda e: sources[e], start + i * 32, 32)

        gathered = picked[pl.ds(start, rows_per_block)].reshape(rows_per_block, 256)
        pointers, incidence = [], []
        for q in range(rows_per_block // 128):
            row = target_rows[pl.ds(j * (rows_per_block // 128) + q, 1), :]
            copies = lane_copies(row)
            pointers.append(
                (jnp.concatenate([copies] * (nodes // 128), 1) == lanes).astype(bf16)
            )
            incidence.append((node_ids == row).astype(bf16))
        z = gathered + dot(jnp.concatenate(pointers, 0), target_proj)
        return total + dot(jnp.concatenate(incidence, 1), silu(z).astype(bf16))

    return lax.fori_loop(0, edges // rows_per_block, block, total)


def mesh_kernel(fill, place, sources, targets, latent, gain, weights, next_weight, *rest):
    *parts, latent_out, sent_out, table, picked = rest
    fill(place, table, parts)
    target_proj = dot(latent[...], weights[1]).astype(bf16)
    hidden = edge_pass(table, picked, sources, targets, target_proj, 256)
    summed = dot(hidden.astype(bf16), weights[2])
    new = node_update(latent[...], summed, gain[...].astype(f32), weights[3]).astype(bf16)
    latent_out[...] = new
    sent_out[...] = dot(new, next_weight[...]).astype(bf16)


def fill_encode(place, table, parts):
    odd, lon = place[0], place[1]
    bands = (2 - 2 * odd, 2 * odd, 1)
    for k, part in enumerate(parts):
        column = lax.rem(lon + 4 - k, 4)
        for i in range(3):
            table[pl.ds((bands[i] * 4 + column) * 128, 128)] = split_rows(part[i])


def fill_halo(place, table, parts):
    odd = place[0]
    for band, part in zip((1, 2 - 2 * odd, 2 * odd), parts):
        for q in range(3):
            table[pl.ds((band * 3 + q) * 256, 256)] = split_rows(part[q])


def fill_bands(place, table, parts):
    odd, lon = place[0], place[1]
    for band, part in zip((1, 2 - 2 * odd, 2 * odd), parts):
        for k in range(4):
            column = lax.rem(lon + 4 - k, 4)
            table[pl.ds((band * 4 + column) * 256, 256)] = split_rows(part[k])


def decode_kernel(fill, place, sources, grid, gain, weights, *rest):
    *parts, out, table, picked = rest
    fill(place, table, parts)
    rows = 256

    @pl.loop(0, grid.shape[0] // rows)
    def _(j):
        start = pl.multiple_of(j * rows, rows)

        @pl.loop(0, rows // 16)
        def _(i):
            first = i * 16
            for k in range(3):
                got = [table[sources[3 * (start + first + u) + k]] for u in range(16)]
                for u in range(16):
                    picked[k, first + u] = got[u]

        latent = grid[pl.ds(start, rows), :]
        proj = dot(latent, weights[1])
        hidden = sum(silu(picked[k].reshape(rows, 256) + proj) for k in range(3))
        summed = dot(hidden.astype(bf16), weights[2])
        out[pl.ds(start, rows), :] = node_update(
            latent, summed, gain[...].astype(f32), weights[3]
        ).astype(bf16)


def shape(*dims, dtype=bf16):
    return jax.ShapeDtypeStruct(dims, dtype)


def call(kernel, specs, outs, scratch, cost):
    return pl.pallas_call(
        kernel,
        in_specs=specs,
        out_specs=tuple(VMEM for _ in outs),
        out_shape=tuple(outs),
        scratch_shapes=scratch,
        compiler_params=params,
        cost_estimate=pl.CostEstimate(flops=cost, bytes_accessed=2**20, transcendentals=0),
    )


def along(x, by):
    return lax.ppermute(x, "lon", [(i, (i + by) % 4) for i in range(4)])


def swap_chip(x):
    return lax.ppermute(x, "lat", [(i, i ^ 1) for i in range(32)])


def swap_cross(x):
    return lax.ppermute(x, "lat", [(i, ((i + 1) ^ 1) - 1) if 0 < i < 31 else (i, 31 - i) for i in range(32)])


def shards(
    grid_latent,
    mesh_latent,
    encode_sends,
    encode_sources,
    encode_targets,
    mesh_sources,
    mesh_targets,
    decode_sources,
    encode_weights,
    process_weights,
    decode_weights,
    norm_gains,
):
    grid_count, latent = grid_latent.shape
    nodes = mesh_latent.shape[0]
    place = jnp.stack([lax.axis_index("lat") % 2, lax.axis_index("lon")]).astype(jnp.int32)

    chip, cross, own = call(
        send_kernel,
        [SMEM, SMEM, VMEM, VMEM],
        [shape(4, 128, latent)] * 3,
        [pltpu.VMEM((grid_count, 2, 128), f32), pltpu.VMEM((1536, 2, 128), f32)],
        10**9,
    )(place, encode_sends.reshape(-1), grid_latent, encode_weights[0])
    stacked = jnp.stack([swap_chip(chip), swap_cross(cross), own])
    parts = [stacked[:, 0]] + [along(stacked[:, k], k) for k in (1, 2, 3)]

    def mesh_call(fill, rows, edges, part_count):
        return call(
            partial(mesh_kernel, fill),
            [SMEM, SMEM] + [VMEM] * (5 + part_count),
            [shape(nodes, latent)] * 2,
            [pltpu.VMEM((rows, 2, 128), f32), pltpu.VMEM((edges, 2, 128), f32)],
            10**9,
        )

    mesh_now, sent = mesh_call(fill_encode, 1536, 4096, 4)(
        place,
        encode_sources,
        encode_targets.reshape(-1, 128),
        mesh_latent,
        norm_gains[0:1],
        encode_weights,
        process_weights[0],
        *parts,
    )
    for step in range(STEPS):
        weights = process_weights[4 * step : 4 * step + 4]
        following = process_weights[4 * step + 4] if step + 1 < STEPS else decode_weights[0]
        around = jnp.stack([along(sent, 1), sent, along(sent, -1)])
        mesh_now, sent = mesh_call(fill_halo, 9 * nodes, mesh_sources.shape[0], 3)(
            place,
            mesh_sources,
            mesh_targets.reshape(-1, 128),
            mesh_now,
            norm_gains[1 + step : 2 + step],
            weights,
            following,
            around,
            swap_chip(around),
            swap_cross(around),
        )
    band = jnp.stack([sent] + [along(sent, k) for k in (1, 2, 3)])
    (grid_out,) = call(
        partial(decode_kernel, fill_bands),
        [SMEM, SMEM] + [VMEM] * 6,
        [shape(grid_count, latent)],
        [pltpu.VMEM((12 * nodes, 2, 128), f32), pltpu.VMEM((3, 256, 2, 128), f32)],
        10**9,
    )(
        place,
        decode_sources.reshape(-1),
        grid_latent,
        norm_gains[STEPS + 1 : STEPS + 2],
        decode_weights,
        band,
        swap_chip(band),
        swap_cross(band),
    )
    return grid_out, mesh_now


def solution(mesh):
    rows = P(("lat", "lon"), None)
    flat = P(("lat", "lon"))
    return jax.shard_map(
        shards,
        mesh=mesh,
        in_specs=(rows, rows, P(("lat", "lon"), None, None), flat, flat, flat, flat, rows, P(), P(), P(), P()),
        out_specs=(rows, rows),
        check_vma=False,
    )
```

time: 225 us -> 131 us (0.58)
  the two profiles are of different devices: /device:TPU:39 before, /device:TPU:0 now
where the time goes in v1:
time: 131 us
  Pallas kernels  50.1 us (38%)
  waiting for transfers between devices  37.6 us (29%)
  starting transfers between devices  36.8 us (28%)
  local copies, waits for them, and re-layouts  5.6 us (4%)
    ppermute x4, waiting for transfers between devices, swap_cross(): lax.ppermute(x, 'lat', [(i, (i + 1 ^ 1) - 1) if 0 < i < 31 else (i, 31 -...  22 us
    ppermute x4, starting transfers between devices, swap_cross(): lax.ppermute(x, 'lat', [(i, (i + 1 ^ 1) - 1) if 0 < i < 31 else (i, 31 -...  19.2 us
    ppermute x10, starting transfers between devices, along(): return lax.ppermute(x, 'lon', [(i, (i + by) % 4) for i in range(4)])  17.3 us
    pallas_call x1, Pallas kernels, shards(): call(partial(decode_kernel, fill_bands), [SMEM, SMEM] + [VMEM] * 6, [shap...  16.9 us
    pallas_call x2, Pallas kernels, shards(): mesh_call(fill_halo, 9 * nodes, mesh_sources.shape[0], 3)  15.9 us
    ppermute x10, waiting for transfers between devices, along(): return lax.ppermute(x, 'lon', [(i, (i + by) % 4) for i in range(4)])  15.5 us
    pallas_call x1, Pallas kernels, shards(): mesh_call(fill_encode, 1536, 4096, 4)  13.9 us
    pallas_call x1, Pallas kernels, shards(): call(send_kernel, [SMEM, SMEM, VMEM, VMEM], [shape(4, 128, latent)] * 3,...  3.32 us
  transfers between devices with their start and end apart: 18, of which 12 were waited for; matrix products, arithmetic and copies ran while one was open for 3% of the time, Pallas kernels for 0%

profile of v1, /device:TPU:0, one launch (start us, length us, event | category | flops | bytes accessed | tf_op | source)
XLA Modules:
  0.0 131.3 jit_solution(17048336941461438164)
XLA Ops:
  0.6 0.9 slice_bitcast_fusion.6.weight
  1.6 0.1 pad_add_fusion.place
  1.7 1.2 copy-done
  2.9 3.3 %shard_map.131 = (bf16[4,128,256]{2,1,0:T(8,128)(2,1)S(1)}, bf16[4,128,256]{2,1,0:T(8,128)(2,1)S(1)}, bf16[4,128,256]{2,1,0:T(8,128)(2,1)S(1)}) custom-call(s32[2]{0:T(128)S(1)} %pad_add_fusion.place, s32[1536]{0:T(1024)S(1)} %reshape.20.lists, bf16[2048,256]{1,0:T(8,128)(2,1)S(1)} %copy-done, bf16[256,256]{1,0:T(8,128)(2,1)S(1)} %slice_bitcast_fusion.6.weight), custom_call_target="tpu_custom_call" | custom-call | flops 1000000000 | bytes 1048576 | tf_op jit(solution)/shard_map/pallas_call | solution.py:202
  6.2 0.1 collective-permute-start
  6.3 6.4 %collective-permute-start.1 = (bf16[4,128,256]{2,1,0:T(8,128)(2,1)S(1)}, bf16[4,128,256]{2,1,0:T(8,128)(2,1)S(1)}, u32[]{:S(2)}, u32[]{:S(2)}) collective-permute-start(bf16[4,128,256]{2,1,0:T(8,128)(2,1)S(1)} %get-tuple-element.12), channel_id=1, source_target_pairs={{0,124},{4,8},{8,4},{12,16},{16,12},{20,24},{24,20},{28,32},{32,28... | collective-permute-start | bytes 786440 | tf_op jit(solution)/shard_map/ppermute | solution.py:181
  12.8 4.0 %collective-permute-done.1 = bf16[4,128,256]{2,1,0:T(8,128)(2,1)S(1)} collective-permute-done((bf16[4,128,256]{2,1,0:T(8,128)(2,1)S(1)}, bf16[4,128,256]{2,1,0:T(8,128)(2,1)S(1)}, u32[]{:S(2)}, u32[]{:S(2)}) %collective-permute-start.1) | collective-permute-done | bytes 262176 | tf_op jit(solution)/shard_map/ppermute | solution.py:181
  16.8 0.1 pad_maximum_fusion
  16.9 0.0 copy-start.11
  16.9 0.0 copy-start.3
  16.9 0.0 copy-start.4
  16.9 0.1 slice_bitcast_fusion
  17.0 1.6 %collective-permute-start.2 = (bf16[3,128,256]{2,1,0:T(8,128)(2,1)S(1)}, bf16[3,128,256]{2,1,0:T(8,128)(2,1)S(1)}, u32[]{:S(2)}, u32[]{:S(2)}) collective-permute-start(bf16[3,128,256]{2,1,0:T(8,128)(2,1)S(1)} %get-tuple-element.26), channel_id=1, source_target_pairs={{0,1},{1,2},{2,3},{3,0},{4,5},{5,6},{6,7},{7,4},{8,9},{9,10},{10,1... | collective-permute-start | bytes 589832 | tf_op jit(solution)/shard_map/ppermute | solution.py:173
  18.7 2.9 %collective-permute-start.3 = (bf16[3,128,256]{2,1,0:T(8,128)(2,1)S(1)}, bf16[3,128,256]{2,1,0:T(8,128)(2,1)S(1)}, u32[]{:S(2)}, u32[]{:S(2)}) collective-permute-start(bf16[3,128,256]{2,1,0:T(8,128)(2,1)S(1)} %get-tuple-element.25), channel_id=1, source_target_pairs={{0,2},{1,3},{2,0},{3,1},{4,6},{5,7},{6,4},{7,5},{8,10},{9,11},{10,... | collective-permute-start | bytes 589832 | tf_op jit(solution)/shard_map/ppermute | solution.py:173
  21.6 1.3 %collective-permute-start.4 = (bf16[3,128,256]{2,1,0:T(8,128)(2,1)S(1)}, bf16[3,128,256]{2,1,0:T(8,128)(2,1)S(1)}, u32[]{:S(2)}, u32[]{:S(2)}) collective-permute-start(bf16[3,128,256]{2,1,0:T(8,128)(2,1)S(1)} %get-tuple-element.24), channel_id=1, source_target_pairs={{0,3},{1,0},{2,1},{3,2},{4,7},{5,4},{6,5},{7,6},{8,11},{9,8},{10,9... | collective-permute-start | bytes 589832 | tf_op jit(solution)/shard_map/ppermute | solution.py:173
  22.9 1.4 %collective-permute-done.2.rest_1_ = bf16[3,128,256]{2,1,0:T(8,128)(2,1)S(1)} collective-permute-done((bf16[3,128,256]{2,1,0:T(8,128)(2,1)S(1)}, bf16[3,128,256]{2,1,0:T(8,128)(2,1)S(1)}, u32[]{:S(2)}, u32[]{:S(2)}) %collective-permute-start.2) | collective-permute-done | bytes 196640 | tf_op jit(solution)/shard_map/ppermute | solution.py:173
  24.3 3.0 %collective-permute-done.3.rest_2_ = bf16[3,128,256]{2,1,0:T(8,128)(2,1)S(1)} collective-permute-done((bf16[3,128,256]{2,1,0:T(8,128)(2,1)S(1)}, bf16[3,128,256]{2,1,0:T(8,128)(2,1)S(1)}, u32[]{:S(2)}, u32[]{:S(2)}) %collective-permute-start.3) | collective-permute-done | bytes 196640 | tf_op jit(solution)/shard_map/ppermute | solution.py:173
  27.3 13.9 %shard_map.132 = (bf16[256,256]{1,0:T(8,128)(2,1)S(1)}, bf16[256,256]{1,0:T(8,128)(2,1)S(1)}) custom-call(s32[2]{0:T(128)S(1)} %pad_add_fusion.place, s32[4096]{0:T(1024)S(1)} %copy-done.5, s32[32,128]{1,0:T(8,128)S(1)} %bitcast.39, bf16[256,256]{1,0:T(8,128)(2,1)S(1)} %copy-done.4, bf16[1,256]{1,0:T(2,128)(2,1)S(1)} %get-tuple-element.29.gain, ...), custom_call_target="tpu_custom_call" | custom-call | flops 1000000000 | bytes 1048576 | tf_op jit(solution)/shard_map/pallas_call | solution.py:221
  41.3 1.7 %collective-permute-start.5 = (bf16[256,256]{1,0:T(8,128)(2,1)S(1)}, bf16[256,256]{1,0:T(8,128)(2,1)S(1)}, u32[]{:S(2)}, u32[]{:S(2)}) collective-permute-start(bf16[256,256]{1,0:T(8,128)(2,1)S(1)} %get-tuple-element.15), channel_id=1, source_target_pairs={{0,1},{1,2},{2,3},{3,0},{4,5},{5,6},{6,7},{7,4},{8,9},{9,10},{10,1... | collective-permute-start | bytes 393224 | tf_op jit(solution)/shard_map/ppermute | solution.py:173
  43.0 1.6 %collective-permute-start.6 = (bf16[256,256]{1,0:T(8,128)(2,1)S(1)}, bf16[256,256]{1,0:T(8,128)(2,1)S(1)}, u32[]{:S(2)}, u32[]{:S(2)}) collective-permute-start(bf16[256,256]{1,0:T(8,128)(2,1)S(1)} %get-tuple-element.15), channel_id=1, source_target_pairs={{0,3},{1,0},{2,1},{3,2},{4,7},{5,4},{6,5},{7,6},{8,11},{9,8},{10,9... | collective-permute-start | bytes 393224 | tf_op jit(solution)/shard_map/ppermute | solution.py:173
  44.6 2.9 %collective-permute-done.5 = bf16[256,256]{1,0:T(8,128)(2,1)S(1)} collective-permute-done((bf16[256,256]{1,0:T(8,128)(2,1)S(1)}, bf16[256,256]{1,0:T(8,128)(2,1)S(1)}, u32[]{:S(2)}, u32[]{:S(2)}) %collective-permute-start.5) | collective-permute-done | bytes 131104 | tf_op jit(solution)/shard_map/ppermute | solution.py:173
  47.5 0.4 collective-permute-done.6
  48.0 0.1 collective-permute-start.7
  48.1 6.0 %collective-permute-start.8 = (bf16[3,256,256]{2,1,0:T(8,128)(2,1)S(1)}, bf16[3,256,256]{2,1,0:T(8,128)(2,1)S(1)}, u32[]{:S(2)}, u32[]{:S(2)}) collective-permute-start(bf16[3,256,256]{2,1,0:T(8,128)(2,1)S(1)} %pad_maximum_fusion.2.rest_0_), channel_id=1, source_target_pairs={{0,124},{4,8},{8,4},{12,16},{16,12},{20,24},{24,20},{28,32},{32,28... | collective-permute-start | bytes 1179656 | tf_op jit(solution)/shard_map/ppermute | solution.py:181
  54.1 0.1 fusion
  54.2 5.4 %collective-permute-done.8.rest_2_ = bf16[3,256,256]{2,1,0:T(8,128)(2,1)S(1)} collective-permute-done((bf16[3,256,256]{2,1,0:T(8,128)(2,1)S(1)}, bf16[3,256,256]{2,1,0:T(8,128)(2,1)S(1)}, u32[]{:S(2)}, u32[]{:S(2)}) %collective-permute-start.8) | collective-permute-done | bytes 393248 | tf_op jit(solution)/shard_map/ppermute | solution.py:181
  59.6 7.7 %shard_map.133 = (bf16[256,256]{1,0:T(8,128)(2,1)S(1)}, bf16[256,256]{1,0:T(8,128)(2,1)S(1)}) custom-call(s32[2]{0:T(128)S(1)} %pad_add_fusion.place, s32[2048]{0:T(1024)S(1)} %copy-done.7, s32[16,128]{1,0:T(8,128)S(1)} %bitcast.40, bf16[256,256]{1,0:T(8,128)(2,1)S(1)} %get-tuple-element.14.latent, bf16[1,256]{1,0:T(2,128)(2,1)S(1)} %get-tuple-element.31.gain, ...), custom_call_target="tpu_custom_call" | custom-call | flops 1000000000 | bytes 1048576 | tf_op jit(solution)/shard_map/pallas_call | solution.py:235
  67.3 0.6 collective-permute-start.9
  67.8 2.8 %collective-permute-start.10 = (bf16[256,256]{1,0:T(8,128)(2,1)S(1)}, bf16[256,256]{1,0:T(8,128)(2,1)S(1)}, u32[]{:S(2)}, u32[]{:S(2)}) collective-permute-start(bf16[256,256]{1,0:T(8,128)(2,1)S(1)} %get-tuple-element.17), channel_id=1, source_target_pairs={{0,3},{1,0},{2,1},{3,2},{4,7},{5,4},{6,5},{7,6},{8,11},{9,8},{10,9... | collective-permute-start | bytes 393224 | tf_op jit(solution)/shard_map/ppermute | solution.py:173
  70.6 2.9 %collective-permute-done.9 = bf16[256,256]{1,0:T(8,128)(2,1)S(1)} collective-permute-done((bf16[256,256]{1,0:T(8,128)(2,1)S(1)}, bf16[256,256]{1,0:T(8,128)(2,1)S(1)}, u32[]{:S(2)}, u32[]{:S(2)}) %collective-permute-start.9) | collective-permute-done | bytes 131104 | tf_op jit(solution)/shard_map/ppermute | solution.py:173
  73.6 0.1 collective-permute-start.11
  73.7 4.0 %collective-permute-start.12 = (bf16[3,256,256]{2,1,0:T(8,128)(2,1)S(1)}, bf16[3,256,256]{2,1,0:T(8,128)(2,1)S(1)}, u32[]{:S(2)}, u32[]{:S(2)}) collective-permute-start(bf16[3,256,256]{2,1,0:T(8,128)(2,1)S(1)} %pad_maximum_fusion.3.rest_0_), channel_id=1, source_target_pairs={{0,124},{4,8},{8,4},{12,16},{16,12},{20,24},{24,20},{28,32},{32,28... | collective-permute-start | bytes 1179656 | tf_op jit(solution)/shard_map/ppermute | solution.py:181
  77.7 6.6 %collective-permute-done.12.rest_2_ = bf16[3,256,256]{2,1,0:T(8,128)(2,1)S(1)} collective-permute-done((bf16[3,256,256]{2,1,0:T(8,128)(2,1)S(1)}, bf16[3,256,256]{2,1,0:T(8,128)(2,1)S(1)}, u32[]{:S(2)}, u32[]{:S(2)}) %collective-permute-start.12) | collective-permute-done | bytes 393248 | tf_op jit(solution)/shard_map/ppermute | solution.py:181
  84.3 8.2 %shard_map.134 = (bf16[256,256]{1,0:T(8,128)(2,1)}, bf16[256,256]{1,0:T(8,128)(2,1)S(1)}) custom-call(s32[2]{0:T(128)S(1)} %pad_add_fusion.place, s32[2048]{0:T(1024)S(1)} %copy-done.7, s32[16,128]{1,0:T(8,128)S(1)} %bitcast.41, bf16[256,256]{1,0:T(8,128)(2,1)S(1)} %get-tuple-element.16.latent, bf16[1,256]{1,0:T(2,128)(2,1)S(1)} %get-tuple-element.28.gain, ...), custom_call_target="tpu_custom_call" | custom-call | flops 1000000000 | bytes 1048576 | tf_op jit(solution)/shard_map/pallas_call | solution.py:235
  92.5 1.0 collective-permute-start.13
  93.5 3.7 %collective-permute-start.14 = (bf16[256,256]{1,0:T(8,128)(2,1)S(1)}, bf16[256,256]{1,0:T(8,128)(2,1)S(1)}, u32[]{:S(2)}, u32[]{:S(2)}) collective-permute-start(bf16[256,256]{1,0:T(8,128)(2,1)S(1)} %get-tuple-element.18), channel_id=1, source_target_pairs={{0,2},{1,3},{2,0},{3,1},{4,6},{5,7},{6,4},{7,5},{8,10},{9,11},{10,... | collective-permute-start | bytes 393224 | tf_op jit(solution)/shard_map/ppermute | solution.py:173
  97.2 0.1 collective-permute-start.15
  97.3 2.1 %collective-permute-done.13 = bf16[256,256]{1,0:T(8,128)(2,1)S(1)} collective-permute-done((bf16[256,256]{1,0:T(8,128)(2,1)S(1)}, bf16[256,256]{1,0:T(8,128)(2,1)S(1)}, u32[]{:S(2)}, u32[]{:S(2)}) %collective-permute-start.13) | collective-permute-done | bytes 131104 | tf_op jit(solution)/shard_map/ppermute | solution.py:173
  99.4 2.2 %collective-permute-done.14 = bf16[256,256]{1,0:T(8,128)(2,1)S(1)} collective-permute-done((bf16[256,256]{1,0:T(8,128)(2,1)S(1)}, bf16[256,256]{1,0:T(8,128)(2,1)S(1)}, u32[]{:S(2)}, u32[]{:S(2)}) %collective-permute-start.14) | collective-permute-done | bytes 131104 | tf_op jit(solution)/shard_map/ppermute | solution.py:173
  101.5 0.6 collective-permute-done.15
  102.2 0.1 pad_maximum_fusion.1.rest_0_
  102.2 0.0 copy-start.1
  102.3 0.1 collective-permute-start.16
  102.3 2.7 %collective-permute-start.17 = (bf16[4,256,256]{2,1,0:T(8,128)(2,1)S(1)}, bf16[4,256,256]{2,1,0:T(8,128)(2,1)S(1)}, u32[]{:S(2)}, u32[]{:S(2)}) collective-permute-start(bf16[4,256,256]{2,1,0:T(8,128)(2,1)S(1)} %pad_maximum_fusion.1.rest_0_), channel_id=1, source_target_pairs={{0,124},{4,8},{8,4},{12,16},{16,12},{20,24},{24,20},{28,32},{32,28... | collective-permute-start | bytes 1572872 | tf_op jit(solution)/shard_map/ppermute | solution.py:181
  105.1 1.3 %copy.14 = s32[2048,3]{1,0:T(8,128)} copy(s32[2048,3]{0,1:T(4,128)S(1)} %copy-done.10) | data formatting | bytes 49152 | tf_op args[7]
  106.4 1.9 %reshape.17.sources = s32[6144]{0:T(1024)S(1)} reshape(s32[2048,3]{1,0:T(8,128)} %copy.14) | data formatting | bytes 49152 | tf_op jit(solution)/shard_map/reshape | solution.py:256
  108.3 6.0 %collective-permute-done.17.rest_2_ = bf16[4,256,256]{2,1,0:T(8,128)(2,1)S(1)} collective-permute-done((bf16[4,256,256]{2,1,0:T(8,128)(2,1)S(1)}, bf16[4,256,256]{2,1,0:T(8,128)(2,1)S(1)}, u32[]{:S(2)}, u32[]{:S(2)}) %collective-permute-start.17) | collective-permute-done | bytes 524320 | tf_op jit(solution)/shard_map/ppermute | solution.py:181
  114.4 16.9 %shard_map.135 = bf16[2048,256]{1,0:T(8,128)(2,1)} custom-call(s32[2]{0:T(128)S(1)} %pad_add_fusion.place, s32[6144]{0:T(1024)S(1)} %reshape.17.sources, bf16[2048,256]{1,0:T(8,128)(2,1)S(1)} %copy-done.1, bf16[1,256]{1,0:T(2,128)(2,1)S(1)} %get-tuple-element.30.gain, bf16[4,256,256]{2,1,0:T(8,128)(2,1)S(1)} %copy-done.2, ...), custom_call_target="tpu_custom_call" | custom-call | flops 1000000000 | bytes 1048576 | tf_op jit(solution)/shard_map/pallas_call | solution.py:248
  (33 shorter events, 0.2 us)
Async XLA Ops:
  0.6 0.9 copy-start.12
  1.7 1.2 copy-start
  2.9 9.8 %copy-start.9 = (bf16[8,256,256]{2,1,0:T(8,128)(2,1)S(1)}, bf16[8,256,256]{2,1,0:T(8,128)(2,1)}, u32[]{:S(2)}) copy-start(bf16[8,256,256]{2,1,0:T(8,128)(2,1)} %param.21) | copy-start | bytes 3145732
  6.2 6.5 %collective-permute-start = (bf16[4,128,256]{2,1,0:T(8,128)(2,1)S(1)}, bf16[4,128,256]{2,1,0:T(8,128)(2,1)S(1)}, u32[]{:S(2)}, u32[]{:S(2)}) collective-permute-start(bf16[4,128,256]{2,1,0:T(8,128)(2,1)S(1)} %get-tuple-element.11), channel_id=1, source_target_pairs={{0,4},{4,0},{8,12},{12,8},{16,20},{20,16},{24,28},{28,24},{32,36},... | collective-permute-start | bytes 786440 | tf_op jit(solution)/shard_map/ppermute | solution.py:177
  6.3 10.5 %collective-permute-start.1 = (bf16[4,128,256]{2,1,0:T(8,128)(2,1)S(1)}, bf16[4,128,256]{2,1,0:T(8,128)(2,1)S(1)}, u32[]{:S(2)}, u32[]{:S(2)}) collective-permute-start(bf16[4,128,256]{2,1,0:T(8,128)(2,1)S(1)} %get-tuple-element.12), channel_id=1, source_target_pairs={{0,124},{4,8},{8,4},{12,16},{16,12},{20,24},{24,20},{28,32},{32,28... | collective-permute-start | bytes 786440 | tf_op jit(solution)/shard_map/ppermute | solution.py:181
  16.9 6.0 %copy-start.11 = (bf16[4,256]{1,0:T(4,128)(2,1)S(1)}, bf16[4,256]{1,0:T(4,128)(2,1)}, u32[]{:S(2)}) copy-start(bf16[4,256]{1,0:T(4,128)(2,1)} %param.23) | copy-start | bytes 6148
  16.9 10.4 %copy-start.3 = (bf16[4,256,256]{2,1,0:T(8,128)(2,1)S(1)}, bf16[4,256,256]{2,1,0:T(8,128)(2,1)}, u32[]{:S(2)}) copy-start(bf16[4,256,256]{2,1,0:T(8,128)(2,1)} %weights.2) | copy-start | bytes 1572868
  16.9 10.4 %copy-start.4 = (bf16[256,256]{1,0:T(8,128)(2,1)S(1)}, bf16[256,256]{1,0:T(8,128)(2,1)}, u32[]{:S(2)}) copy-start(bf16[256,256]{1,0:T(8,128)(2,1)} %latent.1) | copy-start | bytes 393220
  16.9 10.4 %copy-start.6 = (s32[4096]{0:T(1024)S(1)}, s32[4096]{0:T(1024)}, u32[]{:S(2)}) copy-start(s32[4096]{0:T(1024)} %param.16) | copy-start | bytes 49156
  17.0 10.3 %copy-start.5 = (s32[4096]{0:T(1024)S(1)}, s32[4096]{0:T(1024)}, u32[]{:S(2)}) copy-start(s32[4096]{0:T(1024)} %sources.3) | copy-start | bytes 49156
  17.0 7.3 %collective-permute-start.2 = (bf16[3,128,256]{2,1,0:T(8,128)(2,1)S(1)}, bf16[3,128,256]{2,1,0:T(8,128)(2,1)S(1)}, u32[]{:S(2)}, u32[]{:S(2)}) collective-permute-start(bf16[3,128,256]{2,1,0:T(8,128)(2,1)S(1)} %get-tuple-element.26), channel_id=1, source_target_pairs={{0,1},{1,2},{2,3},{3,0},{4,5},{5,6},{6,7},{7,4},{8,9},{9,10},{10,1... | collective-permute-start | bytes 589832 | tf_op jit(solution)/shard_map/ppermute | solution.py:173
  18.7 8.7 %collective-permute-start.3 = (bf16[3,128,256]{2,1,0:T(8,128)(2,1)S(1)}, bf16[3,128,256]{2,1,0:T(8,128)(2,1)S(1)}, u32[]{:S(2)}, u32[]{:S(2)}) collective-permute-start(bf16[3,128,256]{2,1,0:T(8,128)(2,1)S(1)} %get-tuple-element.25), channel_id=1, source_target_pairs={{0,2},{1,3},{2,0},{3,1},{4,6},{5,7},{6,4},{7,5},{8,10},{9,11},{10,... | collective-permute-start | bytes 589832 | tf_op jit(solution)/shard_map/ppermute | solution.py:173
  21.6 5.8 %collective-permute-start.4 = (bf16[3,128,256]{2,1,0:T(8,128)(2,1)S(1)}, bf16[3,128,256]{2,1,0:T(8,128)(2,1)S(1)}, u32[]{:S(2)}, u32[]{:S(2)}) collective-permute-start(bf16[3,128,256]{2,1,0:T(8,128)(2,1)S(1)} %get-tuple-element.24), channel_id=1, source_target_pairs={{0,3},{1,0},{2,1},{3,2},{4,7},{5,4},{6,5},{7,6},{8,11},{9,8},{10,9... | collective-permute-start | bytes 589832 | tf_op jit(solution)/shard_map/ppermute | solution.py:173
  41.3 6.2 %collective-permute-start.5 = (bf16[256,256]{1,0:T(8,128)(2,1)S(1)}, bf16[256,256]{1,0:T(8,128)(2,1)S(1)}, u32[]{:S(2)}, u32[]{:S(2)}) collective-permute-start(bf16[256,256]{1,0:T(8,128)(2,1)S(1)} %get-tuple-element.15), channel_id=1, source_target_pairs={{0,1},{1,2},{2,3},{3,0},{4,5},{5,6},{6,7},{7,4},{8,9},{9,10},{10,1... | collective-permute-start | bytes 393224 | tf_op jit(solution)/shard_map/ppermute | solution.py:173
  43.0 5.0 %collective-permute-start.6 = (bf16[256,256]{1,0:T(8,128)(2,1)S(1)}, bf16[256,256]{1,0:T(8,128)(2,1)S(1)}, u32[]{:S(2)}, u32[]{:S(2)}) collective-permute-start(bf16[256,256]{1,0:T(8,128)(2,1)S(1)} %get-tuple-element.15), channel_id=1, source_target_pairs={{0,3},{1,0},{2,1},{3,2},{4,7},{5,4},{6,5},{7,6},{8,11},{9,8},{10,9... | collective-permute-start | bytes 393224 | tf_op jit(solution)/shard_map/ppermute | solution.py:173
  48.0 6.2 %collective-permute-start.7 = (bf16[3,256,256]{2,1,0:T(8,128)(2,1)S(1)}, bf16[3,256,256]{2,1,0:T(8,128)(2,1)S(1)}, u32[]{:S(2)}, u32[]{:S(2)}) collective-permute-start(bf16[3,256,256]{2,1,0:T(8,128)(2,1)S(1)} %pad_maximum_fusion.2.rest_0_), channel_id=1, source_target_pairs={{0,4},{4,0},{8,12},{12,8},{16,20},{20,16},{24,28},{28,24},{32,36},... | collective-permute-start | bytes 1179656 | tf_op jit(solution)/shard_map/ppermute | solution.py:177
  48.1 11.5 %collective-permute-start.8 = (bf16[3,256,256]{2,1,0:T(8,128)(2,1)S(1)}, bf16[3,256,256]{2,1,0:T(8,128)(2,1)S(1)}, u32[]{:S(2)}, u32[]{:S(2)}) collective-permute-start(bf16[3,256,256]{2,1,0:T(8,128)(2,1)S(1)} %pad_maximum_fusion.2.rest_0_), channel_id=1, source_target_pairs={{0,124},{4,8},{8,4},{12,16},{16,12},{20,24},{24,20},{28,32},{32,28... | collective-permute-start | bytes 1179656 | tf_op jit(solution)/shard_map/ppermute | solution.py:181
  54.1 5.5 %copy-start.8 = (s32[2048]{0:T(1024)S(1)}, s32[2048]{0:T(1024)}, u32[]{:S(2)}) copy-start(s32[2048]{0:T(1024)} %param.18) | copy-start | bytes 24580
  54.2 5.4 %copy-start.7 = (s32[2048]{0:T(1024)S(1)}, s32[2048]{0:T(1024)}, u32[]{:S(2)}) copy-start(s32[2048]{0:T(1024)} %sources.5) | copy-start | bytes 24580
  67.3 10.4 %copy-start.2 = (bf16[4,256,256]{2,1,0:T(8,128)(2,1)S(1)}, bf16[4,256,256]{2,1,0:T(8,128)(2,1)}, u32[]{:S(2)}) copy-start(bf16[4,256,256]{2,1,0:T(8,128)(2,1)} %weights.3) | copy-start | bytes 1572868
  67.3 6.2 %collective-permute-start.9 = (bf16[256,256]{1,0:T(8,128)(2,1)S(1)}, bf16[256,256]{1,0:T(8,128)(2,1)S(1)}, u32[]{:S(2)}, u32[]{:S(2)}) collective-permute-start(bf16[256,256]{1,0:T(8,128)(2,1)S(1)} %get-tuple-element.17), channel_id=1, source_target_pairs={{0,1},{1,2},{2,3},{3,0},{4,5},{5,6},{6,7},{7,4},{8,9},{9,10},{10,1... | collective-permute-start | bytes 393224 | tf_op jit(solution)/shard_map/ppermute | solution.py:173
  67.8 5.7 %collective-permute-start.10 = (bf16[256,256]{1,0:T(8,128)(2,1)S(1)}, bf16[256,256]{1,0:T(8,128)(2,1)S(1)}, u32[]{:S(2)}, u32[]{:S(2)}) collective-permute-start(bf16[256,256]{1,0:T(8,128)(2,1)S(1)} %get-tuple-element.17), channel_id=1, source_target_pairs={{0,3},{1,0},{2,1},{3,2},{4,7},{5,4},{6,5},{7,6},{8,11},{9,8},{10,9... | collective-permute-start | bytes 393224 | tf_op jit(solution)/shard_map/ppermute | solution.py:173
  73.6 4.1 %collective-permute-start.11 = (bf16[3,256,256]{2,1,0:T(8,128)(2,1)S(1)}, bf16[3,256,256]{2,1,0:T(8,128)(2,1)S(1)}, u32[]{:S(2)}, u32[]{:S(2)}) collective-permute-start(bf16[3,256,256]{2,1,0:T(8,128)(2,1)S(1)} %pad_maximum_fusion.3.rest_0_), channel_id=1, source_target_pairs={{0,4},{4,0},{8,12},{12,8},{16,20},{20,16},{24,28},{28,24},{32,36},... | collective-permute-start | bytes 1179656 | tf_op jit(solution)/shard_map/ppermute | solution.py:177
  73.7 10.6 %collective-permute-start.12 = (bf16[3,256,256]{2,1,0:T(8,128)(2,1)S(1)}, bf16[3,256,256]{2,1,0:T(8,128)(2,1)S(1)}, u32[]{:S(2)}, u32[]{:S(2)}) collective-permute-start(bf16[3,256,256]{2,1,0:T(8,128)(2,1)S(1)} %pad_maximum_fusion.3.rest_0_), channel_id=1, source_target_pairs={{0,124},{4,8},{8,4},{12,16},{16,12},{20,24},{24,20},{28,32},{32,28... | collective-permute-start | bytes 1179656 | tf_op jit(solution)/shard_map/ppermute | solution.py:181
  92.5 6.9 %collective-permute-start.13 = (bf16[256,256]{1,0:T(8,128)(2,1)S(1)}, bf16[256,256]{1,0:T(8,128)(2,1)S(1)}, u32[]{:S(2)}, u32[]{:S(2)}) collective-permute-start(bf16[256,256]{1,0:T(8,128)(2,1)S(1)} %get-tuple-element.18), channel_id=1, source_target_pairs={{0,1},{1,2},{2,3},{3,0},{4,5},{5,6},{6,7},{7,4},{8,9},{9,10},{10,1... | collective-permute-start | bytes 393224 | tf_op jit(solution)/shard_map/ppermute | solution.py:173
  93.5 8.0 %collective-permute-start.14 = (bf16[256,256]{1,0:T(8,128)(2,1)S(1)}, bf16[256,256]{1,0:T(8,128)(2,1)S(1)}, u32[]{:S(2)}, u32[]{:S(2)}) collective-permute-start(bf16[256,256]{1,0:T(8,128)(2,1)S(1)} %get-tuple-element.18), channel_id=1, source_target_pairs={{0,2},{1,3},{2,0},{3,1},{4,6},{5,7},{6,4},{7,5},{8,10},{9,11},{10,... | collective-permute-start | bytes 393224 | tf_op jit(solution)/shard_map/ppermute | solution.py:173
  97.2 5.0 %collective-permute-start.15 = (bf16[256,256]{1,0:T(8,128)(2,1)S(1)}, bf16[256,256]{1,0:T(8,128)(2,1)S(1)}, u32[]{:S(2)}, u32[]{:S(2)}) collective-permute-start(bf16[256,256]{1,0:T(8,128)(2,1)S(1)} %get-tuple-element.18), channel_id=1, source_target_pairs={{0,3},{1,0},{2,1},{3,2},{4,7},{5,4},{6,5},{7,6},{8,11},{9,8},{10,9... | collective-permute-start | bytes 393224 | tf_op jit(solution)/shard_map/ppermute | solution.py:173
  102.2 2.9 %copy-start.10 = (s32[2048,3]{0,1:T(4,128)S(1)}, s32[2048,3]{0,1:T(4,128)}, u32[]{:S(2)}) copy-start(s32[2048,3]{0,1:T(4,128)} %param.19) | copy-start | bytes 73732
  102.2 12.1 %copy-start.1 = (bf16[2048,256]{1,0:T(8,128)(2,1)S(1)}, bf16[2048,256]{1,0:T(8,128)(2,1)}, u32[]{:S(2)}) copy-start(bf16[2048,256]{1,0:T(8,128)(2,1)} %grid.3) | copy-start | bytes 3145732
  102.3 6.1 %collective-permute-start.16 = (bf16[4,256,256]{2,1,0:T(8,128)(2,1)S(1)}, bf16[4,256,256]{2,1,0:T(8,128)(2,1)S(1)}, u32[]{:S(2)}, u32[]{:S(2)}) collective-permute-start(bf16[4,256,256]{2,1,0:T(8,128)(2,1)S(1)} %pad_maximum_fusion.1.rest_0_), channel_id=1, source_target_pairs={{0,4},{4,0},{8,12},{12,8},{16,20},{20,16},{24,28},{28,24},{32,36},... | collective-permute-start | bytes 1572872 | tf_op jit(solution)/shard_map/ppermute | solution.py:177
  102.3 12.0 %collective-permute-start.17 = (bf16[4,256,256]{2,1,0:T(8,128)(2,1)S(1)}, bf16[4,256,256]{2,1,0:T(8,128)(2,1)S(1)}, u32[]{:S(2)}, u32[]{:S(2)}) collective-permute-start(bf16[4,256,256]{2,1,0:T(8,128)(2,1)S(1)} %pad_maximum_fusion.1.rest_0_), channel_id=1, source_target_pairs={{0,124},{4,8},{8,4},{12,16},{16,12},{20,24},{24,20},{28,32},{32,28... | collective-permute-start | bytes 1572872 | tf_op jit(solution)/shard_map/ppermute | solution.py:181

commit v2 on v1

v2 whole, which is shorter than its diff:
```python
from functools import partial

import jax
import jax.numpy as jnp
from jax import lax
from jax.experimental import pallas as pl
from jax.experimental.pallas import tpu as pltpu
from jax.sharding import PartitionSpec as P

STEPS = 2
EDGE_BLOCK = 1024
GRID_BLOCK = 512
epsilon = 1e-05
VMEM = pl.BlockSpec(memory_space=pltpu.VMEM)
SMEM = pl.BlockSpec(memory_space=pltpu.SMEM)
params = pltpu.CompilerParams(vmem_limit_bytes=20 * 2**20)
f32, bf16, i16 = jnp.float32, jnp.bfloat16, jnp.int16


def dot(a, b):
    return jnp.dot(a, b, preferred_element_type=f32)


def silu(z):
    half = 0.5 * z
    return half + half * jnp.tanh(half)


def node_update(latent, summed, gain_row, node_weight):
    mean_square = jnp.mean(summed * summed, axis=-1, keepdims=True)
    scaled = (summed * lax.rsqrt(mean_square + epsilon) * gain_row).astype(bf16)
    return latent.astype(f32) + dot(scaled, node_weight)


def send_kernel(place, lists, grid, weights, out0, out1, out2, out3, table, picked):
    odd, lon = place[0], place[1]
    slots = 128
    table[...] = dot(grid[...], weights[0]).reshape(table.shape)
    for k, out in enumerate((out0, out1, out2, out3)):
        column = lax.rem(lon + k, 4)
        for part, side in enumerate((1, 2 - 2 * odd, 2 * odd)):
            base = (part * 4 + k) * slots
            first = (side * 4 + column) * slots

            @pl.loop(0, slots // 32)
            def _(i):
                rows = [table[lists[first + i * 32 + u]] for u in range(32)]
                for u in range(32):
                    picked[base + i * 32 + u] = rows[u]

            out[part] = picked[base : base + slots].reshape(slots, 256).astype(bf16)


def lane_copies(row):
    return jnp.transpose(jnp.broadcast_to(row, (128, 128))).astype(i16)


def lanes_kernel(indices, out):
    for q in range(indices.shape[0]):
        out[q * 128 : (q + 1) * 128, :] = lane_copies(indices[q : q + 1, :])


def edge_lanes_kernel(sources, targets, source_out, target_out, incidence_out):
    lanes_kernel(sources, source_out)
    lanes_kernel(targets, target_out)
    node_ids = lax.broadcasted_iota(jnp.int32, (incidence_out.shape[0], 128), 0)
    for q in range(targets.shape[0]):
        incidence_out[:, q * 128 : (q + 1) * 128] = (node_ids == targets[q : q + 1, :]).astype(bf16)


def pointers(copies, starts, width):
    lane = lax.broadcasted_iota(jnp.int32, (1, 128), 1)
    one, zero = jnp.ones((), bf16), jnp.zeros((), bf16)
    return jnp.concatenate(
        [
            jnp.where(copies == (lane + (start + offset)).astype(i16), one, zero)
            for start in starts
            for offset in range(0, width, 128)
        ],
        1,
    )


def received_starts(place, width):
    odd, lon = place[0], place[1]
    return [[(band * 4 + lax.rem(lon + 4 - k, 4)) * width for k in range(4)] for band in (1, 2 - 2 * odd, 2 * odd)]


def halo_starts(place, width):
    odd = place[0]
    return [[(band * 3 + q) * width for q in range(3)] for band in (1, 2 - 2 * odd, 2 * odd)]


def early_edges_kernel(starts, place, sources, targets, own, chip, latent, weights, out):
    width = own.shape[1]
    own_starts, chip_starts, _ = starts(place, width)
    target_proj = dot(latent[...], weights[1]).astype(bf16)
    tables = [x[...].reshape(-1, 256) for x in (own, chip)]
    size = min(EDGE_BLOCK, out.shape[0])
    for first in range(0, out.shape[0], size):
        here = slice(first, first + size)
        copies = sources[here, :]
        out[here, :] = (
            dot(pointers(targets[here, :], [0], 256), target_proj)
            + dot(pointers(copies, own_starts, width), tables[0])
            + dot(pointers(copies, chip_starts, width), tables[1])
        ).astype(bf16)


def late_edges_kernel(
    starts, place, sources, early, cross, incidence, latent, gain, weights, following, latent_out, sent_out, hidden
):
    width = cross.shape[1]
    cross_starts = starts(place, width)[2]
    table = cross[...].reshape(-1, 256)
    size = min(EDGE_BLOCK, hidden.shape[0])
    for first in range(0, hidden.shape[0], size):
        here = slice(first, first + size)
        z = early[here, :].astype(f32) + dot(pointers(sources[here, :], cross_starts, width), table)
        hidden[here, :] = silu(z).astype(bf16)
    summed = dot(incidence[...], hidden[...])
    summed = dot(summed.astype(bf16), weights[2])
    new = node_update(latent[...], summed, gain[...].astype(f32), weights[3]).astype(bf16)
    latent_out[...] = new
    sent_out[...] = dot(new, following[...]).astype(bf16)


def early_grid_kernel(place, sources, own, chip, out):
    width = own.shape[1]
    own_starts, chip_starts, _ = received_starts(place, width)
    tables = [x[...].reshape(-1, 256) for x in (own, chip)]

    @pl.loop(0, out.shape[0] // EDGE_BLOCK)
    def _(j):
        here = pl.ds(pl.multiple_of(j * EDGE_BLOCK, EDGE_BLOCK), EDGE_BLOCK)
        copies = sources[here, :]
        out[here, :] = (
            dot(pointers(copies, own_starts, width), tables[0]) + dot(pointers(copies, chip_starts, width), tables[1])
        ).astype(bf16)


def late_grid_kernel(place, sources, early, cross, grid, proj, gain, weights, out):
    width = cross.shape[1]
    cross_starts = received_starts(place, width)[2]
    table = cross[...].reshape(-1, 256)
    gains = gain[...].astype(f32)
    count = grid.shape[0]
    for first in range(0, count, GRID_BLOCK):
        here = slice(first, first + GRID_BLOCK)
        base = proj[here, :].astype(f32)
        hidden = jnp.zeros((GRID_BLOCK, 256), f32)
        for k in range(3):
            rows = slice(k * count + first, k * count + first + GRID_BLOCK)
            late = dot(pointers(sources[rows, :], cross_starts, width), table)
            hidden += silu(late + early[rows, :].astype(f32) + base)
        summed = dot(hidden.astype(bf16), weights[2])
        out[here, :] = node_update(grid[here, :], summed, gains, weights[3]).astype(bf16)


def project_kernel(rows, weights, out):
    out[...] = dot(rows[...], weights[1]).astype(bf16)


def shape(*dims, dtype=bf16):
    return jax.ShapeDtypeStruct(dims, dtype)


def call(kernel, specs, outs, scratch, cost):
    return pl.pallas_call(
        kernel,
        in_specs=specs,
        out_specs=tuple(VMEM for _ in outs),
        out_shape=tuple(outs),
        scratch_shapes=scratch,
        compiler_params=params,
        cost_estimate=pl.CostEstimate(flops=cost, bytes_accessed=2**20, transcendentals=0),
    )


def along(x, by):
    return lax.ppermute(x, "lon", [(i, (i + by) % 4) for i in range(4)])


def swap_chip(x):
    return lax.ppermute(x, "lat", [(i, i ^ 1) for i in range(32)])


def swap_cross(x):
    return lax.ppermute(x, "lat", [(i, ((i + 1) ^ 1) - 1) if 0 < i < 31 else (i, 31 - i) for i in range(32)])


def shards(
    grid_latent,
    mesh_latent,
    encode_sends,
    encode_sources,
    encode_targets,
    mesh_sources,
    mesh_targets,
    decode_sources,
    encode_weights,
    process_weights,
    decode_weights,
    norm_gains,
):
    grid_count, latent = grid_latent.shape
    nodes = mesh_latent.shape[0]
    place = jnp.stack([lax.axis_index("lat") % 2, lax.axis_index("lon")]).astype(jnp.int32)

    def edge_lanes(sources, targets):
        edges = sources.shape[0]
        return call(
            edge_lanes_kernel,
            [VMEM] * 2,
            [shape(edges, 128, dtype=i16)] * 2 + [shape(nodes, edges)],
            [],
            10**9,
        )(sources.reshape(-1, 128), targets.reshape(-1, 128))

    def edge_pass(starts, lanes, mesh_now, blocks, gain, weights, following):
        source_lanes, target_lanes, incidence = lanes
        edges = source_lanes.shape[0]
        chip, cross = swap_chip(blocks), swap_cross(blocks)
        rows = blocks.shape[0] * blocks.shape[1]
        (early,) = call(
            partial(early_edges_kernel, starts),
            [SMEM] + [VMEM] * 6,
            [shape(edges, latent)],
            [],
            2 * edges * 2 * rows * latent,
        )(place, source_lanes, target_lanes, blocks, chip, mesh_now, weights)
        return call(
            partial(late_edges_kernel, starts),
            [SMEM] + [VMEM] * 8,
            [shape(nodes, latent)] * 2,
            [pltpu.VMEM((edges, latent), bf16)],
            2 * edges * rows * latent,
        )(place, source_lanes, early, cross, incidence, mesh_now, gain, weights, following)

    outgoing = call(
        send_kernel,
        [SMEM, SMEM, VMEM, VMEM],
        [shape(3, 128, latent)] * 4,
        [pltpu.VMEM((grid_count, 2, 128), f32), pltpu.VMEM((1536, 2, 128), f32)],
        10**9,
    )(place, encode_sends.reshape(-1), grid_latent, encode_weights)
    encode_lanes = edge_lanes(encode_sources, encode_targets)
    mesh_lanes = edge_lanes(mesh_sources, mesh_targets)
    (grid_lanes,) = call(lanes_kernel, [VMEM], [shape(3 * grid_count, 128, dtype=i16)], [], 10**9)(
        decode_sources.T.reshape(-1, 128)
    )
    (grid_proj,) = call(project_kernel, [VMEM] * 2, [shape(grid_count, latent)], [], 10**9)(
        grid_latent, decode_weights
    )
    arrived = [outgoing[0]] + [along(outgoing[k], k) for k in (1, 2, 3)]
    own, chip, cross = (jnp.stack([x[part] for x in arrived]) for part in range(3))
    chip, cross, encode_lanes, mesh_lanes, grid_lanes, grid_proj = lax.optimization_barrier(
        (chip, cross, encode_lanes, mesh_lanes, grid_lanes, grid_proj)
    )
    chip, cross = swap_chip(chip), swap_cross(cross)
    source_lanes, target_lanes, incidence = encode_lanes
    edges = encode_sources.shape[0]
    (early,) = call(
        partial(early_edges_kernel, received_starts),
        [SMEM] + [VMEM] * 6,
        [shape(edges, latent)],
        [],
        2 * edges * 1024 * latent,
    )(place, source_lanes, target_lanes, own, chip, mesh_latent, encode_weights)
    mesh_now, sent = call(
        partial(late_edges_kernel, received_starts),
        [SMEM] + [VMEM] * 8,
        [shape(nodes, latent)] * 2,
        [pltpu.VMEM((edges, latent), bf16)],
        2 * edges * 512 * latent,
    )(place, source_lanes, early, cross, incidence, mesh_latent, norm_gains[0:1], encode_weights, process_weights[0])
    for step in range(STEPS):
        weights = process_weights[4 * step : 4 * step + 4]
        following = process_weights[4 * step + 4] if step + 1 < STEPS else decode_weights[0]
        around = jnp.stack([along(sent, 1), sent, along(sent, -1)])
        mesh_now, sent = edge_pass(
            halo_starts, mesh_lanes, mesh_now, around, norm_gains[1 + step : 2 + step], weights, following
        )
    band = jnp.stack([sent] + [along(sent, k) for k in (1, 2, 3)])
    chip, cross = swap_chip(band), swap_cross(band)
    (early,) = call(
        early_grid_kernel,
        [SMEM] + [VMEM] * 3,
        [shape(3 * grid_count, latent)],
        [],
        2 * 3 * grid_count * 8 * nodes * latent,
    )(place, grid_lanes, band, chip)
    (grid_out,) = call(
        late_grid_kernel,
        [SMEM] + [VMEM] * 7,
        [shape(grid_count, latent)],
        [],
        10**9,
    )(place, grid_lanes, early, cross, grid_latent, grid_proj, norm_gains[STEPS + 1 : STEPS + 2], decode_weights)
    return grid_out, mesh_now


def solution(mesh):
    rows = P(("lat", "lon"), None)
    flat = P(("lat", "lon"))
    return jax.shard_map(
        shards,
        mesh=mesh,
        in_specs=(rows, rows, P(("lat", "lon"), None, None), flat, flat, flat, flat, rows, P(), P(), P(), P()),
        out_specs=(rows, rows),
        check_vma=False,
    )
```

time: 131 us -> 107 us (0.82)
  waiting for transfers between devices: 37.6 us -> 28.8 us
  Pallas kernels: 50.1 us -> 41.7 us
  starting transfers between devices: 36.8 us -> 31 us
  local copies, waits for them, and re-layouts: 5.6 us -> 3.96 us
    ppermute x4, waiting for transfers between devices: 22 us -> 12.2 us  [swap_cross(): lax.ppermute(x, 'lat', [(i, (i + 1 ^ 1) - 1) if 0 < i < 31 else (i, 31 -...]
    pallas_call x5 -> x13, Pallas kernels: 50.1 us -> 41.7 us  [the longest x1 8.21 us: shards(): call(late_grid_kernel, [SMEM] + [VMEM] * 7, [shape(grid_count, latent)],...]
    ppermute x4, starting transfers between devices: 19.2 us -> 14.3 us  [swap_cross(): lax.ppermute(x, 'lat', [(i, (i + 1 ^ 1) - 1) if 0 < i < 31 else (i, 31 -...]
    reshape x1, local copies, waits for them, and re-layouts: 1.89 us -> 0.02 us  [shards(): decode_sources.T.reshape(-1, 128)]
    unnamed x27 -> x26, local copies, waits for them, and re-layouts: 2.63 us -> 3.08 us
  transfers between devices with their start and end apart: 18 -> 18, of which waited for: 12 -> 12; matrix products, arithmetic and copies ran while one was open for 3% -> 0% of each run, Pallas kernels for 0% -> 20%
where the time goes in v2:
time: 107 us
  Pallas kernels  41.7 us (39%)
  starting transfers between devices  31 us (29%)
  waiting for transfers between devices  28.8 us (27%)
  local copies, waits for them, and re-layouts  3.96 us (4%)
    ppermute x10, starting transfers between devices, along(): return lax.ppermute(x, 'lon', [(i, (i + by) % 4) for i in range(4)])  16.3 us
    ppermute x10, waiting for transfers between devices, along(): return lax.ppermute(x, 'lon', [(i, (i + by) % 4) for i in range(4)])  16.3 us
    ppermute x4, starting transfers between devices, swap_cross(): lax.ppermute(x, 'lat', [(i, (i + 1 ^ 1) - 1) if 0 < i < 31 else (i, 31 -...  14.3 us
    ppermute x4, waiting for transfers between devices, swap_cross(): lax.ppermute(x, 'lat', [(i, (i + 1 ^ 1) - 1) if 0 < i < 31 else (i, 31 -...  12.2 us
    pallas_call x1, Pallas kernels, shards(): call(late_grid_kernel, [SMEM] + [VMEM] * 7, [shape(grid_count, latent)],...  8.21 us
    pallas_call x1, Pallas kernels, shards(): call(early_grid_kernel, [SMEM] + [VMEM] * 3, [shape(3 * grid_count, laten...  8.18 us
    pallas_call x2, Pallas kernels, edge_pass(): call(partial(late_edges_kernel, starts), [SMEM] + [VMEM] * 8, [shape(node...  5.67 us
    pallas_call x2, Pallas kernels, edge_pass(): call(partial(early_edges_kernel, starts), [SMEM] + [VMEM] * 6, [shape(edg...  5.29 us
  transfers between devices with their start and end apart: 18, of which 12 were waited for; matrix products, arithmetic and copies ran while one was open for 0% of the time, Pallas kernels for 20%

profile of v2, /device:TPU:0, one launch (start us, length us, event | category | flops | bytes accessed | tf_op | source)
XLA Modules:
  0.0 106.8 jit_solution(9370907785437943324)
XLA Ops:
  0.6 0.7 reshape.22.lists
  1.3 0.1 pad_add_fusion.place
  1.4 1.2 %copy-done = bf16[2048,256]{1,0:T(8,128)(2,1)S(1)} copy-done((bf16[2048,256]{1,0:T(8,128)(2,1)S(1)}, bf16[2048,256]{1,0:T(8,128)(2,1)}, u32[]{:S(2)}) %copy-start) | copy-done | bytes 1048600
  2.7 1.0 copy-done.3
  3.7 3.3 %shard_map.131 = (bf16[3,128,256]{2,1,0:T(8,128)(2,1)S(1)}, bf16[3,128,256]{2,1,0:T(8,128)(2,1)S(1)}, bf16[3,128,256]{2,1,0:T(8,128)(2,1)S(1)}, bf16[3,128,256]{2,1,0:T(8,128)(2,1)S(1)}) custom-call(s32[2]{0:T(128)S(1)} %pad_add_fusion.place, s32[1536]{0:T(1024)S(1)} %reshape.22.lists, bf16[2048,256]{1,0:T(8,128)(2,1)S(1)} %copy-done, ...), custom_call_target="tpu_custom_call" | custom-call | flops 1000000000 | bytes 1048576 | tf_op jit(solution)/shard_map/pallas_call | solution.py:240
  7.0 1.7 %collective-permute-start = (bf16[3,128,256]{2,1,0:T(8,128)(2,1)S(1)}, bf16[3,128,256]{2,1,0:T(8,128)(2,1)S(1)}, u32[]{:S(2)}, u32[]{:S(2)}) collective-permute-start(bf16[3,128,256]{2,1,0:T(8,128)(2,1)S(1)} %get-tuple-element.29), channel_id=1, source_target_pairs={{0,1},{1,2},{2,3},{3,0},{4,5},{5,6},{6,7},{7,4},{8,9},{9,10},{10,1... | collective-permute-start | bytes 589832 | tf_op jit(solution)/shard_map/ppermute | solution.py:181
  8.8 2.9 %collective-permute-start.1 = (bf16[3,128,256]{2,1,0:T(8,128)(2,1)S(1)}, bf16[3,128,256]{2,1,0:T(8,128)(2,1)S(1)}, u32[]{:S(2)}, u32[]{:S(2)}) collective-permute-start(bf16[3,128,256]{2,1,0:T(8,128)(2,1)S(1)} %get-tuple-element.30), channel_id=1, source_target_pairs={{0,2},{1,3},{2,0},{3,1},{4,6},{5,7},{6,4},{7,5},{8,10},{9,11},{10,... | collective-permute-start | bytes 589832 | tf_op jit(solution)/shard_map/ppermute | solution.py:181
  11.7 1.3 %collective-permute-start.2 = (bf16[3,128,256]{2,1,0:T(8,128)(2,1)S(1)}, bf16[3,128,256]{2,1,0:T(8,128)(2,1)S(1)}, u32[]{:S(2)}, u32[]{:S(2)}) collective-permute-start(bf16[3,128,256]{2,1,0:T(8,128)(2,1)S(1)} %get-tuple-element.31), channel_id=1, source_target_pairs={{0,3},{1,0},{2,1},{3,2},{4,7},{5,4},{6,5},{7,6},{8,11},{9,8},{10,9... | collective-permute-start | bytes 589832 | tf_op jit(solution)/shard_map/ppermute | solution.py:181
  13.1 0.9 shard_map.134.sources
  14.0 0.4 shard_map.135.proj
  14.4 0.8 copy-done.10
  15.2 2.0 %shard_map.132 = (s16[4096,128]{1,0:T(8,128)(2,1)S(1)}, s16[4096,128]{1,0:T(8,128)(2,1)S(1)}, bf16[256,4096]{1,0:T(8,128)(2,1)S(1)}) custom-call(s32[32,128]{1,0:T(8,128)S(1)} %bitcast.28, s32[32,128]{1,0:T(8,128)S(1)} %bitcast.29), custom_call_target="tpu_custom_call" | custom-call | flops 1000000000 | bytes 1048576 | tf_op jit(solution)/shard_map/pallas_call | solution.py:212
  17.2 1.0 shard_map.133
  18.3 2.2 %collective-permute-done.1 = bf16[3,128,256]{2,1,0:T(8,128)(2,1)S(1)} collective-permute-done((bf16[3,128,256]{2,1,0:T(8,128)(2,1)S(1)}, bf16[3,128,256]{2,1,0:T(8,128)(2,1)S(1)}, u32[]{:S(2)}, u32[]{:S(2)}) %collective-permute-start.1) | collective-permute-done | bytes 196640 | tf_op jit(solution)/shard_map/ppermute | solution.py:181
  20.6 0.1 pad_maximum_fusion.3
  20.6 0.1 collective-permute-start.3
  20.7 6.4 %collective-permute-start.4 = (bf16[4,128,256]{2,1,0:T(8,128)(2,1)S(1)}, bf16[4,128,256]{2,1,0:T(8,128)(2,1)S(1)}, u32[]{:S(2)}, u32[]{:S(2)}) collective-permute-start(bf16[4,128,256]{2,1,0:T(8,128)(2,1)S(1)} %get-tuple-element.44), channel_id=1, source_target_pairs={{0,124},{4,8},{8,4},{12,16},{16,12},{20,24},{24,20},{28,32},{32,28... | collective-permute-start | bytes 786440 | tf_op jit(solution)/shard_map/ppermute | solution.py:189
  27.2 3.5 %shard_map.136.early = bf16[4096,256]{1,0:T(8,128)(2,1)S(1)} custom-call(s32[2]{0:T(128)S(1)} %pad_add_fusion.place, s16[4096,128]{1,0:T(8,128)(2,1)S(1)} %get-tuple-element.41.sources, s16[4096,128]{1,0:T(8,128)(2,1)S(1)} %get-tuple-element.42.targets, bf16[4,128,256]{2,1,0:T(8,128)(2,1)S(1)} %pad_maximum_fusion.5.own, ...), custom_call_target="tpu_custom_call" | custom-call | flops 2147483648 | bytes 1048576 | tf_op jit(solution)/shard_map/pallas_call | solution.py:263
  30.7 0.5 collective-permute-done.4.cross
  31.2 3.4 %shard_map.137 = (bf16[256,256]{1,0:T(8,128)(2,1)S(1)}, bf16[256,256]{1,0:T(8,128)(2,1)S(1)}) custom-call(s32[2]{0:T(128)S(1)} %pad_add_fusion.place, s16[4096,128]{1,0:T(8,128)(2,1)S(1)} %get-tuple-element.41.sources, bf16[4096,256]{1,0:T(8,128)(2,1)S(1)} %shard_map.136.early, bf16[4,128,256]{2,1,0:T(8,128)(2,1)S(1)} %collective-permute-done.4.cross, ...), custom_call_target="tpu_custom_call" | custom-call | flops 1073741824 | bytes 1048576 | tf_op jit(solution)/shard_map/pallas_call | solution.py:270
  34.6 2.4 %collective-permute-start.6 = (bf16[256,256]{1,0:T(8,128)(2,1)S(1)}, bf16[256,256]{1,0:T(8,128)(2,1)S(1)}, u32[]{:S(2)}, u32[]{:S(2)}) collective-permute-start(bf16[256,256]{1,0:T(8,128)(2,1)S(1)} %get-tuple-element.46), channel_id=1, source_target_pairs={{0,3},{1,0},{2,1},{3,2},{4,7},{5,4},{6,5},{7,6},{8,11},{9,8},{10,9... | collective-permute-start | bytes 393224 | tf_op jit(solution)/shard_map/ppermute | solution.py:181
  37.0 2.8 %collective-permute-done.6 = bf16[256,256]{1,0:T(8,128)(2,1)S(1)} collective-permute-done((bf16[256,256]{1,0:T(8,128)(2,1)S(1)}, bf16[256,256]{1,0:T(8,128)(2,1)S(1)}, u32[]{:S(2)}, u32[]{:S(2)}) %collective-permute-start.6) | collective-permute-done | bytes 131104 | tf_op jit(solution)/shard_map/ppermute | solution.py:181
  39.8 3.3 %collective-permute-done.5 = bf16[256,256]{1,0:T(8,128)(2,1)S(1)} collective-permute-done((bf16[256,256]{1,0:T(8,128)(2,1)S(1)}, bf16[256,256]{1,0:T(8,128)(2,1)S(1)}, u32[]{:S(2)}, u32[]{:S(2)}) %collective-permute-start.5) | collective-permute-done | bytes 131104 | tf_op jit(solution)/shard_map/ppermute | solution.py:181
  43.2 0.1 collective-permute-start.7
  43.3 3.7 %collective-permute-start.8 = (bf16[3,256,256]{2,1,0:T(8,128)(2,1)S(1)}, bf16[3,256,256]{2,1,0:T(8,128)(2,1)S(1)}, u32[]{:S(2)}, u32[]{:S(2)}) collective-permute-start(bf16[3,256,256]{2,1,0:T(8,128)(2,1)S(1)} %pad_maximum_fusion.1.own), channel_id=1, source_target_pairs={{0,124},{4,8},{8,4},{12,16},{16,12},{20,24},{24,20},{28,32},{32,28... | collective-permute-start | bytes 1179656 | tf_op jit(solution)/shard_map/ppermute | solution.py:189
  47.0 0.1 fusion
  47.1 2.7 %shard_map.138.early = bf16[2048,256]{1,0:T(8,128)(2,1)S(1)} custom-call(s32[2]{0:T(128)S(1)} %pad_add_fusion.place, s16[2048,128]{1,0:T(8,128)(2,1)S(1)} %get-tuple-element.39.sources, s16[2048,128]{1,0:T(8,128)(2,1)S(1)} %get-tuple-element.40.targets, bf16[3,256,256]{2,1,0:T(8,128)(2,1)S(1)} %pad_maximum_fusion.1.own, ...), custom_call_target="tpu_custom_call" | custom-call | flops 1610612736 | bytes 1048576 | tf_op jit(solution)/shard_map/pallas_call | solution.py:225
  49.7 4.2 %collective-permute-done.8.cross = bf16[3,256,256]{2,1,0:T(8,128)(2,1)S(1)} collective-permute-done((bf16[3,256,256]{2,1,0:T(8,128)(2,1)S(1)}, bf16[3,256,256]{2,1,0:T(8,128)(2,1)S(1)}, u32[]{:S(2)}, u32[]{:S(2)}) %collective-permute-start.8) | collective-permute-done | bytes 393248 | tf_op jit(solution)/shard_map/ppermute | solution.py:189
  53.9 2.6 %shard_map.139 = (bf16[256,256]{1,0:T(8,128)(2,1)S(1)}, bf16[256,256]{1,0:T(8,128)(2,1)S(1)}) custom-call(s32[2]{0:T(128)S(1)} %pad_add_fusion.place, s16[2048,128]{1,0:T(8,128)(2,1)S(1)} %get-tuple-element.39.sources, bf16[2048,256]{1,0:T(8,128)(2,1)S(1)} %shard_map.138.early, bf16[3,256,256]{2,1,0:T(8,128)(2,1)S(1)} %collective-permute-done.8.cross, ...), custom_call_target="tpu_custom_call" | custom-call | flops 805306368 | bytes 1048576 | tf_op jit(solution)/shard_map/pallas_call | solution.py:232
  56.5 0.1 collective-permute-start.9
  56.5 3.2 %collective-permute-start.10 = (bf16[256,256]{1,0:T(8,128)(2,1)S(1)}, bf16[256,256]{1,0:T(8,128)(2,1)S(1)}, u32[]{:S(2)}, u32[]{:S(2)}) collective-permute-start(bf16[256,256]{1,0:T(8,128)(2,1)S(1)} %get-tuple-element.49), channel_id=1, source_target_pairs={{0,3},{1,0},{2,1},{3,2},{4,7},{5,4},{6,5},{7,6},{8,11},{9,8},{10,9... | collective-permute-start | bytes 393224 | tf_op jit(solution)/shard_map/ppermute | solution.py:181
  59.8 2.9 %collective-permute-done.9 = bf16[256,256]{1,0:T(8,128)(2,1)S(1)} collective-permute-done((bf16[256,256]{1,0:T(8,128)(2,1)S(1)}, bf16[256,256]{1,0:T(8,128)(2,1)S(1)}, u32[]{:S(2)}, u32[]{:S(2)}) %collective-permute-start.9) | collective-permute-done | bytes 131104 | tf_op jit(solution)/shard_map/ppermute | solution.py:181
  62.8 0.1 collective-permute-start.11
  62.8 2.6 %collective-permute-start.12 = (bf16[3,256,256]{2,1,0:T(8,128)(2,1)S(1)}, bf16[3,256,256]{2,1,0:T(8,128)(2,1)S(1)}, u32[]{:S(2)}, u32[]{:S(2)}) collective-permute-start(bf16[3,256,256]{2,1,0:T(8,128)(2,1)S(1)} %pad_maximum_fusion.2.own), channel_id=1, source_target_pairs={{0,124},{4,8},{8,4},{12,16},{16,12},{20,24},{24,20},{28,32},{32,28... | collective-permute-start | bytes 1179656 | tf_op jit(solution)/shard_map/ppermute | solution.py:189
  65.5 2.6 %shard_map.140.early = bf16[2048,256]{1,0:T(8,128)(2,1)S(1)} custom-call(s32[2]{0:T(128)S(1)} %pad_add_fusion.place, s16[2048,128]{1,0:T(8,128)(2,1)S(1)} %get-tuple-element.39.sources, s16[2048,128]{1,0:T(8,128)(2,1)S(1)} %get-tuple-element.40.targets, bf16[3,256,256]{2,1,0:T(8,128)(2,1)S(1)} %pad_maximum_fusion.2.own, ...), custom_call_target="tpu_custom_call" | custom-call | flops 1610612736 | bytes 1048576 | tf_op jit(solution)/shard_map/pallas_call | solution.py:225
  68.1 5.3 %collective-permute-done.12.cross = bf16[3,256,256]{2,1,0:T(8,128)(2,1)S(1)} collective-permute-done((bf16[3,256,256]{2,1,0:T(8,128)(2,1)S(1)}, bf16[3,256,256]{2,1,0:T(8,128)(2,1)S(1)}, u32[]{:S(2)}, u32[]{:S(2)}) %collective-permute-start.12) | collective-permute-done | bytes 393248 | tf_op jit(solution)/shard_map/ppermute | solution.py:189
  73.4 3.1 %shard_map.141 = (bf16[256,256]{1,0:T(8,128)(2,1)}, bf16[256,256]{1,0:T(8,128)(2,1)S(1)}) custom-call(s32[2]{0:T(128)S(1)} %pad_add_fusion.place, s16[2048,128]{1,0:T(8,128)(2,1)S(1)} %get-tuple-element.39.sources, bf16[2048,256]{1,0:T(8,128)(2,1)S(1)} %shard_map.140.early, bf16[3,256,256]{2,1,0:T(8,128)(2,1)S(1)} %collective-permute-done.12.cross, ...), custom_call_target="tpu_custom_call" | custom-call | flops 805306368 | bytes 1048576 | tf_op jit(solution)/shard_map/pallas_call | solution.py:232
  76.6 4.7 %collective-permute-start.14 = (bf16[256,256]{1,0:T(8,128)(2,1)S(1)}, bf16[256,256]{1,0:T(8,128)(2,1)S(1)}, u32[]{:S(2)}, u32[]{:S(2)}) collective-permute-start(bf16[256,256]{1,0:T(8,128)(2,1)S(1)} %get-tuple-element.51), channel_id=1, source_target_pairs={{0,2},{1,3},{2,0},{3,1},{4,6},{5,7},{6,4},{7,5},{8,10},{9,11},{10,... | collective-permute-start | bytes 393224 | tf_op jit(solution)/shard_map/ppermute | solution.py:181
  81.3 2.2 %collective-permute-done.13 = bf16[256,256]{1,0:T(8,128)(2,1)S(1)} collective-permute-done((bf16[256,256]{1,0:T(8,128)(2,1)S(1)}, bf16[256,256]{1,0:T(8,128)(2,1)S(1)}, u32[]{:S(2)}, u32[]{:S(2)}) %collective-permute-start.13) | collective-permute-done | bytes 131104 | tf_op jit(solution)/shard_map/ppermute | solution.py:181
  83.4 2.2 %collective-permute-done.14 = bf16[256,256]{1,0:T(8,128)(2,1)S(1)} collective-permute-done((bf16[256,256]{1,0:T(8,128)(2,1)S(1)}, bf16[256,256]{1,0:T(8,128)(2,1)S(1)}, u32[]{:S(2)}, u32[]{:S(2)}) %collective-permute-start.14) | collective-permute-done | bytes 131104 | tf_op jit(solution)/shard_map/ppermute | solution.py:181
  85.6 0.6 collective-permute-done.15
  86.2 0.1 pad_maximum_fusion.own
  86.3 0.1 collective-permute-start.16
  86.4 1.6 %collective-permute-start.17 = (bf16[4,256,256]{2,1,0:T(8,128)(2,1)S(1)}, bf16[4,256,256]{2,1,0:T(8,128)(2,1)S(1)}, u32[]{:S(2)}, u32[]{:S(2)}) collective-permute-start(bf16[4,256,256]{2,1,0:T(8,128)(2,1)S(1)} %pad_maximum_fusion.own), channel_id=1, source_target_pairs={{0,124},{4,8},{8,4},{12,16},{16,12},{20,24},{24,20},{28,32},{32,28... | collective-permute-start | bytes 1572872 | tf_op jit(solution)/shard_map/ppermute | solution.py:189
  88.0 0.3 collective-permute-done.16.chip
  88.3 8.2 %shard_map.142.early = bf16[6144,256]{1,0:T(8,128)(2,1)S(1)} custom-call(s32[2]{0:T(128)S(1)} %pad_add_fusion.place, s16[6144,128]{1,0:T(8,128)(2,1)S(1)} %shard_map.134.sources, bf16[4,256,256]{2,1,0:T(8,128)(2,1)S(1)} %pad_maximum_fusion.own, bf16[4,256,256]{2,1,0:T(8,128)(2,1)S(1)} %collective-permute-done.16.chip), custom_call_target="tpu_custom_call" | custom-call | flops 6442450944 | bytes 1048576 | tf_op jit(solution)/shard_map/pallas_call | solution.py:286
  96.5 2.1 %collective-permute-done.17.cross = bf16[4,256,256]{2,1,0:T(8,128)(2,1)S(1)} collective-permute-done((bf16[4,256,256]{2,1,0:T(8,128)(2,1)S(1)}, bf16[4,256,256]{2,1,0:T(8,128)(2,1)S(1)}, u32[]{:S(2)}, u32[]{:S(2)}) %collective-permute-start.17) | collective-permute-done | bytes 524320 | tf_op jit(solution)/shard_map/ppermute | solution.py:189
  98.6 8.2 %shard_map.143 = bf16[2048,256]{1,0:T(8,128)(2,1)} custom-call(s32[2]{0:T(128)S(1)} %pad_add_fusion.place, s16[6144,128]{1,0:T(8,128)(2,1)S(1)} %shard_map.134.sources, bf16[6144,256]{1,0:T(8,128)(2,1)S(1)} %shard_map.142.early, bf16[4,256,256]{2,1,0:T(8,128)(2,1)S(1)} %collective-permute-done.17.cross, bf16[2048,256]{1,0:T(8,128)(2,1)S(1)} %copy-done.1, ...), custom_call_target="tpu_custom_call" | custom-call | flops 1000000000 | bytes 1048576 | tf_op jit(solution)/shard_map/pallas_call | solution.py:293
  (43 shorter events, 0.3 us)
Async XLA Ops:
  0.6 12.4 %copy-start.11 = (s32[2048,3]{0,1:T(4,128)S(1)}, s32[2048,3]{0,1:T(4,128)}, u32[]{:S(2)}) copy-start(s32[2048,3]{0,1:T(4,128)} %param.19) | copy-start | bytes 73732
  1.4 1.2 %copy-start = (bf16[2048,256]{1,0:T(8,128)(2,1)S(1)}, bf16[2048,256]{1,0:T(8,128)(2,1)}, u32[]{:S(2)}) copy-start(bf16[2048,256]{1,0:T(8,128)(2,1)} %grid.3) | copy-start | bytes 3145732
  2.6 1.0 copy-start.3
  7.0 6.9 %copy-start.1 = (bf16[2048,256]{1,0:T(8,128)(2,1)S(1)}, bf16[2048,256]{1,0:T(8,128)(2,1)}, u32[]{:S(2)}) copy-start(bf16[2048,256]{1,0:T(8,128)(2,1)} %grid.3) | copy-start | bytes 3145732
  7.0 6.9 %copy-start.2 = (bf16[4,256,256]{2,1,0:T(8,128)(2,1)S(1)}, bf16[4,256,256]{2,1,0:T(8,128)(2,1)}, u32[]{:S(2)}) copy-start(bf16[4,256,256]{2,1,0:T(8,128)(2,1)} %weights.9) | copy-start | bytes 1572868
  7.0 11.2 %collective-permute-start = (bf16[3,128,256]{2,1,0:T(8,128)(2,1)S(1)}, bf16[3,128,256]{2,1,0:T(8,128)(2,1)S(1)}, u32[]{:S(2)}, u32[]{:S(2)}) collective-permute-start(bf16[3,128,256]{2,1,0:T(8,128)(2,1)S(1)} %get-tuple-element.29), channel_id=1, source_target_pairs={{0,1},{1,2},{2,3},{3,0},{4,5},{5,6},{6,7},{7,4},{8,9},{9,10},{10,1... | collective-permute-start | bytes 589832 | tf_op jit(solution)/shard_map/ppermute | solution.py:181
  8.8 11.7 %collective-permute-start.1 = (bf16[3,128,256]{2,1,0:T(8,128)(2,1)S(1)}, bf16[3,128,256]{2,1,0:T(8,128)(2,1)S(1)}, u32[]{:S(2)}, u32[]{:S(2)}) collective-permute-start(bf16[3,128,256]{2,1,0:T(8,128)(2,1)S(1)} %get-tuple-element.30), channel_id=1, source_target_pairs={{0,2},{1,3},{2,0},{3,1},{4,6},{5,7},{6,4},{7,5},{8,10},{9,11},{10,... | collective-permute-start | bytes 589832 | tf_op jit(solution)/shard_map/ppermute | solution.py:181
  11.7 8.8 %collective-permute-start.2 = (bf16[3,128,256]{2,1,0:T(8,128)(2,1)S(1)}, bf16[3,128,256]{2,1,0:T(8,128)(2,1)S(1)}, u32[]{:S(2)}, u32[]{:S(2)}) collective-permute-start(bf16[3,128,256]{2,1,0:T(8,128)(2,1)S(1)} %get-tuple-element.31), channel_id=1, source_target_pairs={{0,3},{1,0},{2,1},{3,2},{4,7},{5,4},{6,5},{7,6},{8,11},{9,8},{10,9... | collective-permute-start | bytes 589832 | tf_op jit(solution)/shard_map/ppermute | solution.py:181
  14.0 1.2 %copy-start.10 = (bf16[8,256,256]{2,1,0:T(8,128)(2,1)S(1)}, bf16[8,256,256]{2,1,0:T(8,128)(2,1)}, u32[]{:S(2)}) copy-start(bf16[8,256,256]{2,1,0:T(8,128)(2,1)} %param.21) | copy-start | bytes 3145732
  14.0 1.2 %copy-start.6 = (s32[4096]{0:T(1024)S(1)}, s32[4096]{0:T(1024)}, u32[]{:S(2)}) copy-start(s32[4096]{0:T(1024)} %param.15) | copy-start | bytes 49156
  14.0 1.2 %copy-start.7 = (s32[4096]{0:T(1024)S(1)}, s32[4096]{0:T(1024)}, u32[]{:S(2)}) copy-start(s32[4096]{0:T(1024)} %param.16) | copy-start | bytes 49156
  15.2 2.0 %copy-start.8 = (s32[2048]{0:T(1024)S(1)}, s32[2048]{0:T(1024)}, u32[]{:S(2)}) copy-start(s32[2048]{0:T(1024)} %param.17) | copy-start | bytes 24580
  15.2 2.0 %copy-start.9 = (s32[2048]{0:T(1024)S(1)}, s32[2048]{0:T(1024)}, u32[]{:S(2)}) copy-start(s32[2048]{0:T(1024)} %param.18) | copy-start | bytes 24580
  18.2 2.5 %copy-start.12 = (bf16[4,256]{1,0:T(4,128)(2,1)S(1)}, bf16[4,256]{1,0:T(4,128)(2,1)}, u32[]{:S(2)}) copy-start(bf16[4,256]{1,0:T(4,128)(2,1)} %param.23) | copy-start | bytes 6148
  18.2 9.0 %copy-start.4 = (bf16[4,256,256]{2,1,0:T(8,128)(2,1)S(1)}, bf16[4,256,256]{2,1,0:T(8,128)(2,1)}, u32[]{:S(2)}) copy-start(bf16[4,256,256]{2,1,0:T(8,128)(2,1)} %weights.8) | copy-start | bytes 1572868
  18.2 9.0 %copy-start.5 = (bf16[256,256]{1,0:T(8,128)(2,1)S(1)}, bf16[256,256]{1,0:T(8,128)(2,1)}, u32[]{:S(2)}) copy-start(bf16[256,256]{1,0:T(8,128)(2,1)} %latent.3) | copy-start | bytes 393220
  20.6 6.6 %collective-permute-start.3 = (bf16[4,128,256]{2,1,0:T(8,128)(2,1)S(1)}, bf16[4,128,256]{2,1,0:T(8,128)(2,1)S(1)}, u32[]{:S(2)}, u32[]{:S(2)}) collective-permute-start(bf16[4,128,256]{2,1,0:T(8,128)(2,1)S(1)} %get-tuple-element.43), channel_id=1, source_target_pairs={{0,4},{4,0},{8,12},{12,8},{16,20},{20,16},{24,28},{28,24},{32,36},... | collective-permute-start | bytes 786440 | tf_op jit(solution)/shard_map/ppermute | solution.py:185
  20.7 10.5 %collective-permute-start.4 = (bf16[4,128,256]{2,1,0:T(8,128)(2,1)S(1)}, bf16[4,128,256]{2,1,0:T(8,128)(2,1)S(1)}, u32[]{:S(2)}, u32[]{:S(2)}) collective-permute-start(bf16[4,128,256]{2,1,0:T(8,128)(2,1)S(1)} %get-tuple-element.44), channel_id=1, source_target_pairs={{0,124},{4,8},{8,4},{12,16},{16,12},{20,24},{24,20},{28,32},{32,28... | collective-permute-start | bytes 786440 | tf_op jit(solution)/shard_map/ppermute | solution.py:189
  34.6 5.2 %collective-permute-start.6 = (bf16[256,256]{1,0:T(8,128)(2,1)S(1)}, bf16[256,256]{1,0:T(8,128)(2,1)S(1)}, u32[]{:S(2)}, u32[]{:S(2)}) collective-permute-start(bf16[256,256]{1,0:T(8,128)(2,1)S(1)} %get-tuple-element.46), channel_id=1, source_target_pairs={{0,3},{1,0},{2,1},{3,2},{4,7},{5,4},{6,5},{7,6},{8,11},{9,8},{10,9... | collective-permute-start | bytes 393224 | tf_op jit(solution)/shard_map/ppermute | solution.py:181
  37.0 6.2 %collective-permute-start.5 = (bf16[256,256]{1,0:T(8,128)(2,1)S(1)}, bf16[256,256]{1,0:T(8,128)(2,1)S(1)}, u32[]{:S(2)}, u32[]{:S(2)}) collective-permute-start(bf16[256,256]{1,0:T(8,128)(2,1)S(1)} %get-tuple-element.46), channel_id=1, source_target_pairs={{0,1},{1,2},{2,3},{3,0},{4,5},{5,6},{6,7},{7,4},{8,9},{9,10},{10,1... | collective-permute-start | bytes 393224 | tf_op jit(solution)/shard_map/ppermute | solution.py:181
  43.2 3.9 %collective-permute-start.7 = (bf16[3,256,256]{2,1,0:T(8,128)(2,1)S(1)}, bf16[3,256,256]{2,1,0:T(8,128)(2,1)S(1)}, u32[]{:S(2)}, u32[]{:S(2)}) collective-permute-start(bf16[3,256,256]{2,1,0:T(8,128)(2,1)S(1)} %pad_maximum_fusion.1.own), channel_id=1, source_target_pairs={{0,4},{4,0},{8,12},{12,8},{16,20},{20,16},{24,28},{28,24},{32,36},... | collective-permute-start | bytes 1179656 | tf_op jit(solution)/shard_map/ppermute | solution.py:185
  43.3 10.6 %collective-permute-start.8 = (bf16[3,256,256]{2,1,0:T(8,128)(2,1)S(1)}, bf16[3,256,256]{2,1,0:T(8,128)(2,1)S(1)}, u32[]{:S(2)}, u32[]{:S(2)}) collective-permute-start(bf16[3,256,256]{2,1,0:T(8,128)(2,1)S(1)} %pad_maximum_fusion.1.own), channel_id=1, source_target_pairs={{0,124},{4,8},{8,4},{12,16},{16,12},{20,24},{24,20},{28,32},{32,28... | collective-permute-start | bytes 1179656 | tf_op jit(solution)/shard_map/ppermute | solution.py:189
  56.5 6.2 %collective-permute-start.9 = (bf16[256,256]{1,0:T(8,128)(2,1)S(1)}, bf16[256,256]{1,0:T(8,128)(2,1)S(1)}, u32[]{:S(2)}, u32[]{:S(2)}) collective-permute-start(bf16[256,256]{1,0:T(8,128)(2,1)S(1)} %get-tuple-element.49), channel_id=1, source_target_pairs={{0,1},{1,2},{2,3},{3,0},{4,5},{5,6},{6,7},{7,4},{8,9},{9,10},{10,1... | collective-permute-start | bytes 393224 | tf_op jit(solution)/shard_map/ppermute | solution.py:181
  56.5 6.2 %collective-permute-start.10 = (bf16[256,256]{1,0:T(8,128)(2,1)S(1)}, bf16[256,256]{1,0:T(8,128)(2,1)S(1)}, u32[]{:S(2)}, u32[]{:S(2)}) collective-permute-start(bf16[256,256]{1,0:T(8,128)(2,1)S(1)} %get-tuple-element.49), channel_id=1, source_target_pairs={{0,3},{1,0},{2,1},{3,2},{4,7},{5,4},{6,5},{7,6},{8,11},{9,8},{10,9... | collective-permute-start | bytes 393224 | tf_op jit(solution)/shard_map/ppermute | solution.py:181
  62.8 2.7 %collective-permute-start.11 = (bf16[3,256,256]{2,1,0:T(8,128)(2,1)S(1)}, bf16[3,256,256]{2,1,0:T(8,128)(2,1)S(1)}, u32[]{:S(2)}, u32[]{:S(2)}) collective-permute-start(bf16[3,256,256]{2,1,0:T(8,128)(2,1)S(1)} %pad_maximum_fusion.2.own), channel_id=1, source_target_pairs={{0,4},{4,0},{8,12},{12,8},{16,20},{20,16},{24,28},{28,24},{32,36},... | collective-permute-start | bytes 1179656 | tf_op jit(solution)/shard_map/ppermute | solution.py:185
  62.8 10.6 %collective-permute-start.12 = (bf16[3,256,256]{2,1,0:T(8,128)(2,1)S(1)}, bf16[3,256,256]{2,1,0:T(8,128)(2,1)S(1)}, u32[]{:S(2)}, u32[]{:S(2)}) collective-permute-start(bf16[3,256,256]{2,1,0:T(8,128)(2,1)S(1)} %pad_maximum_fusion.2.own), channel_id=1, source_target_pairs={{0,124},{4,8},{8,4},{12,16},{16,12},{20,24},{24,20},{28,32},{32,28... | collective-permute-start | bytes 1179656 | tf_op jit(solution)/shard_map/ppermute | solution.py:189
  76.6 6.9 %collective-permute-start.13 = (bf16[256,256]{1,0:T(8,128)(2,1)S(1)}, bf16[256,256]{1,0:T(8,128)(2,1)S(1)}, u32[]{:S(2)}, u32[]{:S(2)}) collective-permute-start(bf16[256,256]{1,0:T(8,128)(2,1)S(1)} %get-tuple-element.51), channel_id=1, source_target_pairs={{0,1},{1,2},{2,3},{3,0},{4,5},{5,6},{6,7},{7,4},{8,9},{9,10},{10,1... | collective-permute-start | bytes 393224 | tf_op jit(solution)/shard_map/ppermute | solution.py:181
  76.6 9.0 %collective-permute-start.14 = (bf16[256,256]{1,0:T(8,128)(2,1)S(1)}, bf16[256,256]{1,0:T(8,128)(2,1)S(1)}, u32[]{:S(2)}, u32[]{:S(2)}) collective-permute-start(bf16[256,256]{1,0:T(8,128)(2,1)S(1)} %get-tuple-element.51), channel_id=1, source_target_pairs={{0,2},{1,3},{2,0},{3,1},{4,6},{5,7},{6,4},{7,5},{8,10},{9,11},{10,... | collective-permute-start | bytes 393224 | tf_op jit(solution)/shard_map/ppermute | solution.py:181
  81.2 5.0 %collective-permute-start.15 = (bf16[256,256]{1,0:T(8,128)(2,1)S(1)}, bf16[256,256]{1,0:T(8,128)(2,1)S(1)}, u32[]{:S(2)}, u32[]{:S(2)}) collective-permute-start(bf16[256,256]{1,0:T(8,128)(2,1)S(1)} %get-tuple-element.51), channel_id=1, source_target_pairs={{0,3},{1,0},{2,1},{3,2},{4,7},{5,4},{6,5},{7,6},{8,11},{9,8},{10,9... | collective-permute-start | bytes 393224 | tf_op jit(solution)/shard_map/ppermute | solution.py:181
  86.3 2.0 %collective-permute-start.16 = (bf16[4,256,256]{2,1,0:T(8,128)(2,1)S(1)}, bf16[4,256,256]{2,1,0:T(8,128)(2,1)S(1)}, u32[]{:S(2)}, u32[]{:S(2)}) collective-permute-start(bf16[4,256,256]{2,1,0:T(8,128)(2,1)S(1)} %pad_maximum_fusion.own), channel_id=1, source_target_pairs={{0,4},{4,0},{8,12},{12,8},{16,20},{20,16},{24,28},{28,24},{32,36},... | collective-permute-start | bytes 1572872 | tf_op jit(solution)/shard_map/ppermute | solution.py:185
  86.4 12.2 %collective-permute-start.17 = (bf16[4,256,256]{2,1,0:T(8,128)(2,1)S(1)}, bf16[4,256,256]{2,1,0:T(8,128)(2,1)S(1)}, u32[]{:S(2)}, u32[]{:S(2)}) collective-permute-start(bf16[4,256,256]{2,1,0:T(8,128)(2,1)S(1)} %pad_maximum_fusion.own), channel_id=1, source_target_pairs={{0,124},{4,8},{8,4},{12,16},{16,12},{20,24},{24,20},{28,32},{32,28... | collective-permute-start | bytes 1572872 | tf_op jit(solution)/shard_map/ppermute | solution.py:189

commit v3 on v2

v3 whole, which is shorter than its diff:
```python
from functools import partial

import jax
import jax.numpy as jnp
from jax import lax
from jax.experimental import pallas as pl
from jax.experimental.pallas import tpu as pltpu
from jax.sharding import PartitionSpec as P

STEPS = 2
EDGE_BLOCK = 1024
SEND_VMEM = 63
GRID_BLOCK = 1024
epsilon = 1e-05
VMEM = pl.BlockSpec(memory_space=pltpu.VMEM)
HBM = pl.BlockSpec(memory_space=pltpu.HBM)
f32, bf16, i16 = jnp.float32, jnp.bfloat16, jnp.int16


def dot(a, b):
    return jnp.dot(a, b, preferred_element_type=f32)


def silu(z):
    half = 0.5 * z
    return half + half * jnp.tanh(half)


def node_update(latent, summed, gain_row, node_weight):
    mean_square = jnp.mean(summed * summed, axis=-1, keepdims=True)
    scaled = (summed * lax.rsqrt(mean_square + epsilon) * gain_row).astype(bf16)
    return latent.astype(f32) + dot(scaled, node_weight)


def position():
    return lax.rem(lax.axis_index("lat"), 2), lax.axis_index("lon")


def send_kernel(lists, grid, weights, out0, out1, out2, out3, rows_in, weight, table, picked, wanted, sems):
    odd, lon = position()
    slots = 128
    parts = 4
    size = rows_in.shape[0] // parts
    fetch = [pltpu.make_async_copy(weights.at[0], weight, sems.at[0])]
    for n in range(parts):
        here = pl.ds(n * size, size)
        fetch.append(pltpu.make_async_copy(grid.at[here], rows_in.at[here], sems.at[1 + n]))
    for k in range(4):
        for part, side in enumerate((1, 2 - 2 * odd, 2 * odd)):
            n = 3 * k + part
            fetch.append(
                pltpu.make_async_copy(
                    lists.at[side, lax.rem(lon + k, 4)], wanted.at[pl.ds(n * slots, slots)], sems.at[1 + parts + n]
                )
            )
    for copy in fetch:
        copy.start()
    fetch[0].wait()
    for n in range(parts):
        fetch[1 + n].wait()
        here = pl.ds(n * size, size)
        table[here] = dot(rows_in[here, :], weight[...]).reshape(size, 2, 128)
    for copy in fetch[1 + parts :]:
        copy.wait()
    for k, out in enumerate((out0, out1, out2, out3)):
        for part in range(3):
            base = (3 * k + part) * slots

            @pl.loop(0, slots // 32)
            def _(i):
                rows = [table[wanted[base + i * 32 + u]] for u in range(32)]
                for u in range(32):
                    picked[base + i * 32 + u] = rows[u]

            out[part] = picked[base : base + slots].reshape(slots, 256).astype(bf16)


def lane_copies(row):
    return jnp.transpose(jnp.broadcast_to(row, (128, 128))).astype(i16)


def lanes_kernel(indices, out):
    for q in range(indices.shape[0]):
        out[q * 128 : (q + 1) * 128, :] = lane_copies(indices[q : q + 1, :])


def edge_lanes_kernel(sources, targets, source_out, target_out, incidence_out):
    lanes_kernel(sources, source_out)
    lanes_kernel(targets, target_out)
    node_ids = lax.broadcasted_iota(jnp.int32, (incidence_out.shape[0], 128), 0)
    for q in range(targets.shape[0]):
        incidence_out[:, q * 128 : (q + 1) * 128] = (node_ids == targets[q : q + 1, :]).astype(bf16)


def pointers(copies, starts, width):
    lane = lax.broadcasted_iota(jnp.int32, (1, 128), 1)
    one, zero = jnp.ones((), bf16), jnp.zeros((), bf16)
    return jnp.concatenate(
        [
            jnp.where(copies == (lane + (start + offset)).astype(i16), one, zero)
            for start in starts
            for offset in range(0, width, 128)
        ],
        1,
    )


def received_starts(width):
    odd, lon = position()
    return [[(band * 4 + lax.rem(lon + 4 - k, 4)) * width for k in range(4)] for band in (1, 2 - 2 * odd, 2 * odd)]


def halo_starts(width):
    odd, _ = position()
    return [[(band * 3 + q) * width for q in range(3)] for band in (1, 2 - 2 * odd, 2 * odd)]


def early_edges_kernel(starts, set_index, sources, targets, own, chip, latent, weights, out):
    width = own.shape[1]
    own_starts, chip_starts, _ = starts(width)
    target_proj = dot(latent[...], weights[4 * set_index + 1]).astype(bf16)
    tables = [x[...].reshape(-1, 256) for x in (own, chip)]
    size = min(EDGE_BLOCK, out.shape[0])
    for first in range(0, out.shape[0], size):
        here = slice(first, first + size)
        copies = sources[here, :]
        out[here, :] = (
            dot(pointers(targets[here, :], [0], 256), target_proj)
            + dot(pointers(copies, own_starts, width), tables[0])
            + dot(pointers(copies, chip_starts, width), tables[1])
        ).astype(bf16)


def late_edges_kernel(
    starts, set_index, stage, sources, early, cross, incidence, latent, gains, weights, following,
    latent_out, sent_out, hidden
):
    width = cross.shape[1]
    cross_starts = starts(width)[2]
    table = cross[...].reshape(-1, 256)
    size = min(EDGE_BLOCK, hidden.shape[0])
    for first in range(0, hidden.shape[0], size):
        here = slice(first, first + size)
        z = early[here, :].astype(f32) + dot(pointers(sources[here, :], cross_starts, width), table)
        hidden[here, :] = silu(z).astype(bf16)
    summed = dot(incidence[...], hidden[...])
    summed = dot(summed.astype(bf16), weights[4 * set_index + 2])
    gain = gains[stage : stage + 1, :].astype(f32)
    new = node_update(latent[...], summed, gain, weights[4 * set_index + 3]).astype(bf16)
    latent_out[...] = new
    sent_out[...] = dot(new, following[4 * (stage % STEPS)]).astype(bf16)


def own_grid_kernel(sources, own, out):
    width = own.shape[0]
    starts = received_starts(width)[0][:1]

    @pl.loop(0, out.shape[0] // EDGE_BLOCK)
    def _(j):
        here = pl.ds(pl.multiple_of(j * EDGE_BLOCK, EDGE_BLOCK), EDGE_BLOCK)
        out[here, :] = dot(pointers(sources[here, :], starts, width), own[...]).astype(bf16)


def early_grid_kernel(sources, before, own, chip, out):
    width = own.shape[1]
    own_starts, chip_starts, _ = received_starts(width)
    starts = own_starts[1:] + chip_starts
    table = jnp.concatenate([own[1:].reshape(-1, 256), chip[...].reshape(-1, 256)], 0)

    @pl.loop(0, out.shape[0] // EDGE_BLOCK)
    def _(j):
        here = pl.ds(pl.multiple_of(j * EDGE_BLOCK, EDGE_BLOCK), EDGE_BLOCK)
        found = dot(pointers(sources[here, :], starts, width), table)
        out[here, :] = (before[here, :].astype(f32) + found).astype(bf16)


def late_grid_kernel(sources, early, cross, grid, proj, gain, weights, out):
    width = cross.shape[1]
    cross_starts = received_starts(width)[2]
    table = cross[...].reshape(-1, 256)
    gains = gain[STEPS + 1 : STEPS + 2, :].astype(f32)
    count = grid.shape[0]
    @pl.loop(0, count // GRID_BLOCK)
    def _(j):
        first = pl.multiple_of(j * GRID_BLOCK, GRID_BLOCK)
        here = pl.ds(first, GRID_BLOCK)
        base = proj[here, :].astype(f32)
        hidden = jnp.zeros((GRID_BLOCK, 256), f32)
        for k in range(3):
            rows = pl.ds(pl.multiple_of(k * count + first, GRID_BLOCK), GRID_BLOCK)
            late = dot(pointers(sources[rows, :], cross_starts, width), table)
            hidden += silu(late + early[rows, :].astype(f32) + base)
        summed = dot(hidden.astype(bf16), weights[2])
        out[here, :] = node_update(grid[here, :], summed, gains, weights[3]).astype(bf16)


def project_kernel(rows, weights, out):
    out[...] = dot(rows[...], weights[1]).astype(bf16)


def shape(*dims, dtype=bf16):
    return jax.ShapeDtypeStruct(dims, dtype)


def call(kernel, specs, outs, scratch, cost, limit=20):
    return pl.pallas_call(
        kernel,
        in_specs=specs,
        out_specs=tuple(VMEM for _ in outs),
        out_shape=tuple(outs),
        scratch_shapes=scratch,
        compiler_params=pltpu.CompilerParams(vmem_limit_bytes=limit * 2**20),
        cost_estimate=pl.CostEstimate(flops=cost, bytes_accessed=2**20, transcendentals=0),
    )


def along(x, by):
    return lax.ppermute(x, "lon", [(i, (i + by) % 4) for i in range(4)])


def swap_chip(x):
    return lax.ppermute(x, "lat", [(i, i ^ 1) for i in range(32)])


def swap_cross(x):
    return lax.ppermute(x, "lat", [(i, ((i + 1) ^ 1) - 1) if 0 < i < 31 else (i, 31 - i) for i in range(32)])


def shards(
    grid_latent,
    mesh_latent,
    encode_sends,
    encode_sources,
    encode_targets,
    mesh_sources,
    mesh_targets,
    decode_sources,
    encode_weights,
    process_weights,
    decode_weights,
    norm_gains,
):
    grid_count, latent = grid_latent.shape
    nodes = mesh_latent.shape[0]

    def edge_lanes(sources, targets):
        edges = sources.shape[0]
        return call(
            edge_lanes_kernel,
            [VMEM] * 2,
            [shape(edges, 128, dtype=i16)] * 2 + [shape(nodes, edges)],
            [],
            10**9,
        )(sources.reshape(-1, 128), targets.reshape(-1, 128))

    def edge_pass(starts, stage, lanes, mesh_now, own, chip, cross):
        source_lanes, target_lanes, incidence = lanes
        edges = source_lanes.shape[0]
        rows = own.shape[0] * own.shape[1]
        weights = process_weights if stage else encode_weights
        following = process_weights if stage < STEPS else decode_weights
        set_index = stage - 1 if stage else 0
        chip, cross = swap_chip(chip), swap_cross(cross)
        (early,) = call(
            partial(early_edges_kernel, starts, set_index),
            [VMEM] * 6,
            [shape(edges, latent)],
            [],
            2 * edges * 2 * rows * latent,
        )(source_lanes, target_lanes, own, chip, mesh_now, weights)
        return call(
            partial(late_edges_kernel, starts, set_index, stage),
            [VMEM] * 8,
            [shape(nodes, latent)] * 2,
            [pltpu.VMEM((edges, latent), bf16)],
            2 * edges * rows * latent,
        )(source_lanes, early, cross, incidence, mesh_now, norm_gains, weights, following)

    outgoing = call(
        send_kernel,
        [HBM] * 3,
        [shape(3, 128, latent)] * 4,
        [
            pltpu.VMEM((grid_count, latent), bf16),
            pltpu.VMEM((latent, latent), bf16),
            pltpu.VMEM((grid_count, 2, 128), f32),
            pltpu.VMEM((1536, 2, 128), f32),
            pltpu.SMEM((1536,), jnp.int32),
            pltpu.SemaphoreType.DMA((17,)),
        ],
        10**9,
        SEND_VMEM,
    )(encode_sends, grid_latent, encode_weights)
    encode_lanes = edge_lanes(encode_sources, encode_targets)
    mesh_lanes = edge_lanes(mesh_sources, mesh_targets)
    (grid_lanes,) = call(lanes_kernel, [VMEM], [shape(3 * grid_count, 128, dtype=i16)], [], 10**9)(
        decode_sources.T.reshape(-1, 128)
    )
    (grid_proj,) = call(project_kernel, [VMEM] * 2, [shape(grid_count, latent)], [], 10**9)(
        grid_latent, decode_weights
    )
    arrived = [outgoing[0]] + [along(outgoing[k], k) for k in (1, 2, 3)]
    own, chip, cross = (jnp.stack([x[part] for x in arrived]) for part in range(3))
    chip, cross, encode_lanes, mesh_lanes, grid_lanes, grid_proj = lax.optimization_barrier(
        (chip, cross, encode_lanes, mesh_lanes, grid_lanes, grid_proj)
    )
    mesh_now, sent = edge_pass(received_starts, 0, encode_lanes, mesh_latent, own, chip, cross)
    for step in range(STEPS):
        around = jnp.stack([along(sent, 1), sent, along(sent, -1)])
        mesh_now, sent = edge_pass(halo_starts, step + 1, mesh_lanes, mesh_now, around, around, around)
    beside = [along(sent, k) for k in (1, 2, 3)]
    (before,) = call(
        own_grid_kernel,
        [VMEM] * 2,
        [shape(3 * grid_count, latent)],
        [],
        2 * 3 * grid_count * nodes * latent,
    )(grid_lanes, sent)
    band = jnp.stack([sent] + beside)
    band, before = lax.optimization_barrier((band, before))
    chip, cross = swap_chip(band), swap_cross(band)
    (early,) = call(
        early_grid_kernel,
        [VMEM] * 4,
        [shape(3 * grid_count, latent)],
        [],
        2 * 3 * grid_count * 7 * nodes * latent,
    )(grid_lanes, before, band, chip)
    (grid_out,) = call(
        late_grid_kernel,
        [VMEM] * 7,
        [shape(grid_count, latent)],
        [],
        10**9,
    )(grid_lanes, early, cross, grid_latent, grid_proj, norm_gains, decode_weights)
    return grid_out, mesh_now


def solution(mesh):
    rows = P(("lat", "lon"), None)
    flat = P(("lat", "lon"))
    return jax.shard_map(
        shards,
        mesh=mesh,
        in_specs=(rows, rows, P(("lat", "lon"), None, None), flat, flat, flat, flat, rows, P(), P(), P(), P()),
        out_specs=(rows, rows),
        check_vma=False,
    )
```

time: 107 us -> 102 us (0.953)
  waiting for transfers between devices: 28.8 us -> 32.2 us
  starting transfers between devices: 31 us -> 27.9 us
  local copies, waits for them, and re-layouts: 3.96 us -> 1.37 us
  Pallas kernels: 41.7 us -> 39.5 us
    ppermute x4, waiting for transfers between devices: 12.2 us -> 15.2 us  [swap_cross(): lax.ppermute(x, 'lat', [(i, (i + 1 ^ 1) - 1) if 0 < i < 31 else (i, 31 -...]
    ppermute x10, starting transfers between devices: 16.3 us -> 13.2 us  [along(): return lax.ppermute(x, 'lon', [(i, (i + by) % 4) for i in range(4)])]
    pallas_call x9 -> x10, Pallas kernels: 37.5 us -> 35.3 us  [the longest x3 7.31 us: edge_pass(): call(partial(late_edges_kernel, starts, set_index, stage), [VMEM] * 8, [s...]
    unnamed x26, local copies, waits for them, and re-layouts: 3.08 us -> 1.29 us
  transfers between devices with their start and end apart: 18 -> 18, of which waited for: 12 -> 13; matrix products, arithmetic and copies ran while one was open for 0% -> 0% of each run, Pallas kernels for 20% -> 20%
where the time goes in v3:
time: 102 us
  Pallas kernels  39.5 us (39%)
  waiting for transfers between devices  32.2 us (32%)
  starting transfers between devices  27.9 us (27%)
  local copies, waits for them, and re-layouts  1.37 us (1%)
  between operations  1.02 us (1%)
    ppermute x10, waiting for transfers between devices, along(): return lax.ppermute(x, 'lon', [(i, (i + by) % 4) for i in range(4)])  16.7 us
    ppermute x4, waiting for transfers between devices, swap_cross(): lax.ppermute(x, 'lat', [(i, (i + 1 ^ 1) - 1) if 0 < i < 31 else (i, 31 -...  15.2 us
    ppermute x4, starting transfers between devices, swap_cross(): lax.ppermute(x, 'lat', [(i, (i + 1 ^ 1) - 1) if 0 < i < 31 else (i, 31 -...  14.3 us
    ppermute x10, starting transfers between devices, along(): return lax.ppermute(x, 'lon', [(i, (i + by) % 4) for i in range(4)])  13.2 us
    pallas_call x3, Pallas kernels, edge_pass(): call(partial(late_edges_kernel, starts, set_index, stage), [VMEM] * 8, [s...  7.31 us
    pallas_call x3, Pallas kernels, edge_pass(): call(partial(early_edges_kernel, starts, set_index), [VMEM] * 6, [shape(e...  7.11 us
    pallas_call x1, Pallas kernels, shards(): call(early_grid_kernel, [VMEM] * 4, [shape(3 * grid_count, latent)], [],...  6.83 us
    pallas_call x1, Pallas kernels, shards(): call(late_grid_kernel, [VMEM] * 7, [shape(grid_count, latent)], [], 10 ** 9)  6.67 us
  transfers between devices with their start and end apart: 18, of which 13 were waited for; matrix products, arithmetic and copies ran while one was open for 0% of the time, Pallas kernels for 20%

profile of v3, /device:TPU:0, one launch (start us, length us, event | category | flops | bytes accessed | tf_op | source)
XLA Modules:
  0.0 102.3 jit_solution(184708931920755336)
XLA Ops:
  0.7 5.6 %shard_map.131 = (bf16[3,128,256]{2,1,0:T(8,128)(2,1)}, bf16[3,128,256]{2,1,0:T(8,128)(2,1)}, bf16[3,128,256]{2,1,0:T(8,128)(2,1)}, bf16[3,128,256]{2,1,0:T(8,128)(2,1)}) custom-call(s32[3,4,128]{2,1,0:T(4,128)} %lists.1, bf16[2048,256]{1,0:T(8,128)(2,1)} %grid.3, bf16[4,256,256]{2,1,0:T(8,128)(2,1)} %weights.12), custom_call_target="tpu_custom_call" | custom-call | flops 1000000000 | bytes 1048576 | tf_op jit(solution)/shard_map/pallas_call | solution.py:279
  6.2 1.7 %collective-permute-start = (bf16[3,128,256]{2,1,0:T(8,128)(2,1)}, bf16[3,128,256]{2,1,0:T(8,128)(2,1)S(1)}, u32[]{:S(2)}, u32[]{:S(2)}) collective-permute-start(bf16[3,128,256]{2,1,0:T(8,128)(2,1)} %get-tuple-element.31), channel_id=1, source_target_pairs={{0,1},{1,2},{2,3},{3,0},{4,5},{5,6},{6,7},{7,4},{8,9},{9,10},{10,1... | collective-permute-start | bytes 589832 | tf_op jit(solution)/shard_map/ppermute | solution.py:218
  7.9 2.9 %collective-permute-start.1 = (bf16[3,128,256]{2,1,0:T(8,128)(2,1)}, bf16[3,128,256]{2,1,0:T(8,128)(2,1)S(1)}, u32[]{:S(2)}, u32[]{:S(2)}) collective-permute-start(bf16[3,128,256]{2,1,0:T(8,128)(2,1)} %get-tuple-element.32), channel_id=1, source_target_pairs={{0,2},{1,3},{2,0},{3,1},{4,6},{5,7},{6,4},{7,5},{8,10},{9,11},{10,... | collective-permute-start | bytes 589832 | tf_op jit(solution)/shard_map/ppermute | solution.py:218
  10.8 1.3 %collective-permute-start.2 = (bf16[3,128,256]{2,1,0:T(8,128)(2,1)}, bf16[3,128,256]{2,1,0:T(8,128)(2,1)S(1)}, u32[]{:S(2)}, u32[]{:S(2)}) collective-permute-start(bf16[3,128,256]{2,1,0:T(8,128)(2,1)} %get-tuple-element.33), channel_id=1, source_target_pairs={{0,3},{1,0},{2,1},{3,2},{4,7},{5,4},{6,5},{7,6},{8,11},{9,8},{10,9... | collective-permute-start | bytes 589832 | tf_op jit(solution)/shard_map/ppermute | solution.py:218
  12.2 0.0 copy-start.2
  12.2 1.2 %copy-done.2 = bf16[2048,256]{1,0:T(8,128)(2,1)S(1)} copy-done((bf16[2048,256]{1,0:T(8,128)(2,1)S(1)}, bf16[2048,256]{1,0:T(8,128)(2,1)}, u32[]{:S(2)}) %copy-start.2) | copy-done | bytes 1048600
  13.5 0.4 shard_map.135.proj
  13.9 0.0 copy-start.10
  13.9 0.9 shard_map.134.sources
  14.8 0.0 copy-start.7
  14.8 1.0 shard_map.133
  15.8 2.0 %shard_map.132 = (s16[4096,128]{1,0:T(8,128)(2,1)S(1)}, s16[4096,128]{1,0:T(8,128)(2,1)S(1)}, bf16[256,4096]{1,0:T(8,128)(2,1)S(1)}) custom-call(s32[32,128]{1,0:T(8,128)S(1)} %bitcast.18, s32[32,128]{1,0:T(8,128)S(1)} %bitcast.19), custom_call_target="tpu_custom_call" | custom-call | flops 1000000000 | bytes 1048576 | tf_op jit(solution)/shard_map/pallas_call | solution.py:248
  17.9 2.0 %collective-permute-done.1 = bf16[3,128,256]{2,1,0:T(8,128)(2,1)S(1)} collective-permute-done((bf16[3,128,256]{2,1,0:T(8,128)(2,1)}, bf16[3,128,256]{2,1,0:T(8,128)(2,1)S(1)}, u32[]{:S(2)}, u32[]{:S(2)}) %collective-permute-start.1) | collective-permute-done | bytes 196640 | tf_op jit(solution)/shard_map/ppermute | solution.py:218
  19.9 0.1 pad_maximum_fusion.3
  20.0 0.1 collective-permute-start.3
  20.1 6.3 %collective-permute-start.4 = (bf16[4,128,256]{2,1,0:T(8,128)(2,1)S(1)}, bf16[4,128,256]{2,1,0:T(8,128)(2,1)S(1)}, u32[]{:S(2)}, u32[]{:S(2)}) collective-permute-start(bf16[4,128,256]{2,1,0:T(8,128)(2,1)S(1)} %get-tuple-element.46), channel_id=1, source_target_pairs={{0,124},{4,8},{8,4},{12,16},{16,12},{20,24},{24,20},{28,32},{32,28... | collective-permute-start | bytes 786440 | tf_op jit(solution)/shard_map/ppermute | solution.py:226
  26.5 2.9 %shard_map.136.early = bf16[4096,256]{1,0:T(8,128)(2,1)S(1)} custom-call(s16[4096,128]{1,0:T(8,128)(2,1)S(1)} %get-tuple-element.43.sources, s16[4096,128]{1,0:T(8,128)(2,1)S(1)} %get-tuple-element.44.targets, bf16[4,128,256]{2,1,0:T(8,128)(2,1)S(1)} %pad_maximum_fusion.5.own, bf16[4,128,256]{2,1,0:T(8,128)(2,1)S(1)} %collective-permute-done.3.chip, ...), custom_call_target="tpu_custom_call" | custom-call | flops 2147483648 | bytes 1048576 | tf_op jit(solution)/shard_map/pallas_call | solution.py:264
  29.5 1.0 %collective-permute-done.4.cross = bf16[4,128,256]{2,1,0:T(8,128)(2,1)S(1)} collective-permute-done((bf16[4,128,256]{2,1,0:T(8,128)(2,1)S(1)}, bf16[4,128,256]{2,1,0:T(8,128)(2,1)S(1)}, u32[]{:S(2)}, u32[]{:S(2)}) %collective-permute-start.4) | collective-permute-done | bytes 262176 | tf_op jit(solution)/shard_map/ppermute | solution.py:226
  30.5 2.7 %shard_map.137 = (bf16[256,256]{1,0:T(8,128)(2,1)S(1)}, bf16[256,256]{1,0:T(8,128)(2,1)S(1)}) custom-call(s16[4096,128]{1,0:T(8,128)(2,1)S(1)} %get-tuple-element.43.sources, bf16[4096,256]{1,0:T(8,128)(2,1)S(1)} %shard_map.136.early, bf16[4,128,256]{2,1,0:T(8,128)(2,1)S(1)} %collective-permute-done.4.cross, ...), custom_call_target="tpu_custom_call" | custom-call | flops 1073741824 | bytes 1048576 | tf_op jit(solution)/shard_map/pallas_call | solution.py:271
  33.2 2.4 %collective-permute-start.6 = (bf16[256,256]{1,0:T(8,128)(2,1)S(1)}, bf16[256,256]{1,0:T(8,128)(2,1)S(1)}, u32[]{:S(2)}, u32[]{:S(2)}) collective-permute-start(bf16[256,256]{1,0:T(8,128)(2,1)S(1)} %get-tuple-element.48), channel_id=1, source_target_pairs={{0,3},{1,0},{2,1},{3,2},{4,7},{5,4},{6,5},{7,6},{8,11},{9,8},{10,9... | collective-permute-start | bytes 393224 | tf_op jit(solution)/shard_map/ppermute | solution.py:218
  35.6 2.8 %collective-permute-done.6 = bf16[256,256]{1,0:T(8,128)(2,1)S(1)} collective-permute-done((bf16[256,256]{1,0:T(8,128)(2,1)S(1)}, bf16[256,256]{1,0:T(8,128)(2,1)S(1)}, u32[]{:S(2)}, u32[]{:S(2)}) %collective-permute-start.6) | collective-permute-done | bytes 131104 | tf_op jit(solution)/shard_map/ppermute | solution.py:218
  38.5 3.3 %collective-permute-done.5 = bf16[256,256]{1,0:T(8,128)(2,1)S(1)} collective-permute-done((bf16[256,256]{1,0:T(8,128)(2,1)S(1)}, bf16[256,256]{1,0:T(8,128)(2,1)S(1)}, u32[]{:S(2)}, u32[]{:S(2)}) %collective-permute-start.5) | collective-permute-done | bytes 131104 | tf_op jit(solution)/shard_map/ppermute | solution.py:218
  41.8 0.1 collective-permute-start.7
  41.9 3.7 %collective-permute-start.8 = (bf16[3,256,256]{2,1,0:T(8,128)(2,1)S(1)}, bf16[3,256,256]{2,1,0:T(8,128)(2,1)S(1)}, u32[]{:S(2)}, u32[]{:S(2)}) collective-permute-start(bf16[3,256,256]{2,1,0:T(8,128)(2,1)S(1)} %pad_maximum_fusion.1.own), channel_id=1, source_target_pairs={{0,124},{4,8},{8,4},{12,16},{16,12},{20,24},{24,20},{28,32},{32,28... | collective-permute-start | bytes 1179656 | tf_op jit(solution)/shard_map/ppermute | solution.py:226
  45.7 2.1 %shard_map.138.early = bf16[2048,256]{1,0:T(8,128)(2,1)S(1)} custom-call(s16[2048,128]{1,0:T(8,128)(2,1)S(1)} %get-tuple-element.41.sources, s16[2048,128]{1,0:T(8,128)(2,1)S(1)} %get-tuple-element.42.targets, bf16[3,256,256]{2,1,0:T(8,128)(2,1)S(1)} %pad_maximum_fusion.1.own, bf16[3,256,256]{2,1,0:T(8,128)(2,1)S(1)} %collective-permute-done.7.chip, ...), custom_call_target="tpu_custom_call" | custom-call | flops 1610612736 | bytes 1048576 | tf_op jit(solution)/shard_map/pallas_call | solution.py:264
  47.8 4.8 %collective-permute-done.8.cross = bf16[3,256,256]{2,1,0:T(8,128)(2,1)S(1)} collective-permute-done((bf16[3,256,256]{2,1,0:T(8,128)(2,1)S(1)}, bf16[3,256,256]{2,1,0:T(8,128)(2,1)S(1)}, u32[]{:S(2)}, u32[]{:S(2)}) %collective-permute-start.8) | collective-permute-done | bytes 393248 | tf_op jit(solution)/shard_map/ppermute | solution.py:226
  52.5 2.0 %shard_map.139 = (bf16[256,256]{1,0:T(8,128)(2,1)S(1)}, bf16[256,256]{1,0:T(8,128)(2,1)S(1)}) custom-call(s16[2048,128]{1,0:T(8,128)(2,1)S(1)} %get-tuple-element.41.sources, bf16[2048,256]{1,0:T(8,128)(2,1)S(1)} %shard_map.138.early, bf16[3,256,256]{2,1,0:T(8,128)(2,1)S(1)} %collective-permute-done.8.cross, ...), custom_call_target="tpu_custom_call" | custom-call | flops 805306368 | bytes 1048576 | tf_op jit(solution)/shard_map/pallas_call | solution.py:271
  54.6 0.1 collective-permute-start.10
  54.6 2.0 %collective-permute-start.9 = (bf16[256,256]{1,0:T(8,128)(2,1)S(1)}, bf16[256,256]{1,0:T(8,128)(2,1)S(1)}, u32[]{:S(2)}, u32[]{:S(2)}) collective-permute-start(bf16[256,256]{1,0:T(8,128)(2,1)S(1)} %get-tuple-element.51), channel_id=1, source_target_pairs={{0,1},{1,2},{2,3},{3,0},{4,5},{5,6},{6,7},{7,4},{8,9},{9,10},{10,1... | collective-permute-start | bytes 393224 | tf_op jit(solution)/shard_map/ppermute | solution.py:218
  56.7 2.9 %collective-permute-done.10 = bf16[256,256]{1,0:T(8,128)(2,1)S(1)} collective-permute-done((bf16[256,256]{1,0:T(8,128)(2,1)S(1)}, bf16[256,256]{1,0:T(8,128)(2,1)S(1)}, u32[]{:S(2)}, u32[]{:S(2)}) %collective-permute-start.10) | collective-permute-done | bytes 131104 | tf_op jit(solution)/shard_map/ppermute | solution.py:218
  59.6 1.3 %collective-permute-done.9 = bf16[256,256]{1,0:T(8,128)(2,1)S(1)} collective-permute-done((bf16[256,256]{1,0:T(8,128)(2,1)S(1)}, bf16[256,256]{1,0:T(8,128)(2,1)S(1)}, u32[]{:S(2)}, u32[]{:S(2)}) %collective-permute-start.9) | collective-permute-done | bytes 131104 | tf_op jit(solution)/shard_map/ppermute | solution.py:218
  60.9 0.1 collective-permute-start.11
  61.0 2.6 %collective-permute-start.12 = (bf16[3,256,256]{2,1,0:T(8,128)(2,1)S(1)}, bf16[3,256,256]{2,1,0:T(8,128)(2,1)S(1)}, u32[]{:S(2)}, u32[]{:S(2)}) collective-permute-start(bf16[3,256,256]{2,1,0:T(8,128)(2,1)S(1)} %pad_maximum_fusion.2.own), channel_id=1, source_target_pairs={{0,124},{4,8},{8,4},{12,16},{16,12},{20,24},{24,20},{28,32},{32,28... | collective-permute-start | bytes 1179656 | tf_op jit(solution)/shard_map/ppermute | solution.py:226
  63.6 2.1 %shard_map.140.early = bf16[2048,256]{1,0:T(8,128)(2,1)S(1)} custom-call(s16[2048,128]{1,0:T(8,128)(2,1)S(1)} %get-tuple-element.41.sources, s16[2048,128]{1,0:T(8,128)(2,1)S(1)} %get-tuple-element.42.targets, bf16[3,256,256]{2,1,0:T(8,128)(2,1)S(1)} %pad_maximum_fusion.2.own, bf16[3,256,256]{2,1,0:T(8,128)(2,1)S(1)} %collective-permute-done.11.chip, ...), custom_call_target="tpu_custom_call" | custom-call | flops 1610612736 | bytes 1048576 | tf_op jit(solution)/shard_map/pallas_call | solution.py:264
  65.7 5.9 %collective-permute-done.12.cross = bf16[3,256,256]{2,1,0:T(8,128)(2,1)S(1)} collective-permute-done((bf16[3,256,256]{2,1,0:T(8,128)(2,1)S(1)}, bf16[3,256,256]{2,1,0:T(8,128)(2,1)S(1)}, u32[]{:S(2)}, u32[]{:S(2)}) %collective-permute-start.12) | collective-permute-done | bytes 393248 | tf_op jit(solution)/shard_map/ppermute | solution.py:226
  71.6 2.6 %shard_map.141 = (bf16[256,256]{1,0:T(8,128)(2,1)}, bf16[256,256]{1,0:T(8,128)(2,1)S(1)}) custom-call(s16[2048,128]{1,0:T(8,128)(2,1)S(1)} %get-tuple-element.41.sources, bf16[2048,256]{1,0:T(8,128)(2,1)S(1)} %shard_map.140.early, bf16[3,256,256]{2,1,0:T(8,128)(2,1)S(1)} %collective-permute-done.12.cross, bf16[256,2048]{1,0:T(8,128)(2,1)S(1)} %get-tuple-element.50.incidence, ...), custom_call_target="tpu_custom_call" | custom-call | flops 805306368 | bytes 1048576 | tf_op jit(solution)/shard_map/pallas_call | solution.py:271
  74.2 2.8 %collective-permute-start.14 = (bf16[256,256]{1,0:T(8,128)(2,1)S(1)}, bf16[256,256]{1,0:T(8,128)(2,1)S(1)}, u32[]{:S(2)}, u32[]{:S(2)}) collective-permute-start(bf16[256,256]{1,0:T(8,128)(2,1)S(1)} %get-tuple-element.53.own), channel_id=1, source_target_pairs={{0,2},{1,3},{2,0},{3,1},{4,6},{5,7},{6,4},{7,5},{8,10},{9,11},{10,... | collective-permute-start | bytes 393224 | tf_op jit(solution)/shard_map/ppermute | solution.py:218
  77.0 1.8 %shard_map.142.before = bf16[6144,256]{1,0:T(8,128)(2,1)S(1)} custom-call(s16[6144,128]{1,0:T(8,128)(2,1)S(1)} %shard_map.134.sources, bf16[256,256]{1,0:T(8,128)(2,1)S(1)} %get-tuple-element.53.own), custom_call_target="tpu_custom_call" | custom-call | flops 805306368 | bytes 1048576 | tf_op jit(solution)/shard_map/pallas_call | solution.py:312
  78.8 0.3 collective-permute-done.15
  79.2 1.5 %collective-permute-done.14 = bf16[256,256]{1,0:T(8,128)(2,1)S(1)} collective-permute-done((bf16[256,256]{1,0:T(8,128)(2,1)S(1)}, bf16[256,256]{1,0:T(8,128)(2,1)S(1)}, u32[]{:S(2)}, u32[]{:S(2)}) %collective-permute-start.14) | collective-permute-done | bytes 131104 | tf_op jit(solution)/shard_map/ppermute | solution.py:218
  80.7 2.5 %collective-permute-done.13 = bf16[256,256]{1,0:T(8,128)(2,1)S(1)} collective-permute-done((bf16[256,256]{1,0:T(8,128)(2,1)S(1)}, bf16[256,256]{1,0:T(8,128)(2,1)S(1)}, u32[]{:S(2)}, u32[]{:S(2)}) %collective-permute-start.13) | collective-permute-done | bytes 131104 | tf_op jit(solution)/shard_map/ppermute | solution.py:218
  83.2 0.1 pad_maximum_fusion.own
  83.3 0.1 collective-permute-start.16
  83.4 1.7 %collective-permute-start.17 = (bf16[4,256,256]{2,1,0:T(8,128)(2,1)S(1)}, bf16[4,256,256]{2,1,0:T(8,128)(2,1)S(1)}, u32[]{:S(2)}, u32[]{:S(2)}) collective-permute-start(bf16[4,256,256]{2,1,0:T(8,128)(2,1)S(1)} %pad_maximum_fusion.own), channel_id=1, source_target_pairs={{0,124},{4,8},{8,4},{12,16},{16,12},{20,24},{24,20},{28,32},{32,28... | collective-permute-start | bytes 1572872 | tf_op jit(solution)/shard_map/ppermute | solution.py:226
  85.1 0.2 collective-permute-done.16.chip
  85.3 6.8 %shard_map.143.early = bf16[6144,256]{1,0:T(8,128)(2,1)S(1)} custom-call(s16[6144,128]{1,0:T(8,128)(2,1)S(1)} %shard_map.134.sources, bf16[6144,256]{1,0:T(8,128)(2,1)S(1)} %shard_map.142.before, bf16[4,256,256]{2,1,0:T(8,128)(2,1)S(1)} %pad_maximum_fusion.own, bf16[4,256,256]{2,1,0:T(8,128)(2,1)S(1)} %collective-permute-done.16.chip), custom_call_target="tpu_custom_call" | custom-call | flops 5637144576 | bytes 1048576 | tf_op jit(solution)/shard_map/pallas_call | solution.py:322
  92.1 3.5 %collective-permute-done.17.cross = bf16[4,256,256]{2,1,0:T(8,128)(2,1)S(1)} collective-permute-done((bf16[4,256,256]{2,1,0:T(8,128)(2,1)S(1)}, bf16[4,256,256]{2,1,0:T(8,128)(2,1)S(1)}, u32[]{:S(2)}, u32[]{:S(2)}) %collective-permute-start.17) | collective-permute-done | bytes 524320 | tf_op jit(solution)/shard_map/ppermute | solution.py:226
  95.6 6.7 %shard_map.144 = bf16[2048,256]{1,0:T(8,128)(2,1)} custom-call(s16[6144,128]{1,0:T(8,128)(2,1)S(1)} %shard_map.134.sources, bf16[6144,256]{1,0:T(8,128)(2,1)S(1)} %shard_map.143.early, bf16[4,256,256]{2,1,0:T(8,128)(2,1)S(1)} %collective-permute-done.17.cross, bf16[2048,256]{1,0:T(8,128)(2,1)S(1)} %copy-done.3, bf16[2048,256]{1,0:T(8,128)(2,1)S(1)} %shard_map.135.proj, ...), custom_call_target="tpu_custom_call" | custom-call | flops 1000000000 | bytes 1048576 | tf_op jit(solution)/shard_map/pallas_call | solution.py:329
  (38 shorter events, 0.3 us)
Async XLA Ops:
  0.6 11.6 %copy-start.12 = (s32[2048,3]{0,1:T(4,128)S(1)}, s32[2048,3]{0,1:T(4,128)}, u32[]{:S(2)}) copy-start(s32[2048,3]{0,1:T(4,128)} %param.19) | copy-start | bytes 73732
  0.6 11.6 %copy-start.1 = (bf16[4,256,256]{2,1,0:T(8,128)(2,1)S(1)}, bf16[4,256,256]{2,1,0:T(8,128)(2,1)}, u32[]{:S(2)}) copy-start(bf16[4,256,256]{2,1,0:T(8,128)(2,1)} %weights.17) | copy-start | bytes 1572868
  6.2 11.7 %collective-permute-start = (bf16[3,128,256]{2,1,0:T(8,128)(2,1)}, bf16[3,128,256]{2,1,0:T(8,128)(2,1)S(1)}, u32[]{:S(2)}, u32[]{:S(2)}) collective-permute-start(bf16[3,128,256]{2,1,0:T(8,128)(2,1)} %get-tuple-element.31), channel_id=1, source_target_pairs={{0,1},{1,2},{2,3},{3,0},{4,5},{5,6},{6,7},{7,4},{8,9},{9,10},{10,1... | collective-permute-start | bytes 589832 | tf_op jit(solution)/shard_map/ppermute | solution.py:218
  7.9 11.9 %collective-permute-start.1 = (bf16[3,128,256]{2,1,0:T(8,128)(2,1)}, bf16[3,128,256]{2,1,0:T(8,128)(2,1)S(1)}, u32[]{:S(2)}, u32[]{:S(2)}) collective-permute-start(bf16[3,128,256]{2,1,0:T(8,128)(2,1)} %get-tuple-element.32), channel_id=1, source_target_pairs={{0,2},{1,3},{2,0},{3,1},{4,6},{5,7},{6,4},{7,5},{8,10},{9,11},{10,... | collective-permute-start | bytes 589832 | tf_op jit(solution)/shard_map/ppermute | solution.py:218
  10.8 9.1 %collective-permute-start.2 = (bf16[3,128,256]{2,1,0:T(8,128)(2,1)}, bf16[3,128,256]{2,1,0:T(8,128)(2,1)S(1)}, u32[]{:S(2)}, u32[]{:S(2)}) collective-permute-start(bf16[3,128,256]{2,1,0:T(8,128)(2,1)} %get-tuple-element.33), channel_id=1, source_target_pairs={{0,3},{1,0},{2,1},{3,2},{4,7},{5,4},{6,5},{7,6},{8,11},{9,8},{10,9... | collective-permute-start | bytes 589832 | tf_op jit(solution)/shard_map/ppermute | solution.py:218
  12.2 1.2 %copy-start.2 = (bf16[2048,256]{1,0:T(8,128)(2,1)S(1)}, bf16[2048,256]{1,0:T(8,128)(2,1)}, u32[]{:S(2)}) copy-start(bf16[2048,256]{1,0:T(8,128)(2,1)} %grid.3) | copy-start | bytes 3145732
  13.9 0.9 copy-start.9
  13.9 0.9 copy-start.10
  14.8 1.0 copy-start.7
  14.8 1.0 copy-start.8
  15.8 2.0 %copy-start.11 = (bf16[3,128,256]{2,1,0:T(8,128)(2,1)S(1)}, bf16[3,128,256]{2,1,0:T(8,128)(2,1)}, u32[]{:S(2)}) copy-start(bf16[3,128,256]{2,1,0:T(8,128)(2,1)} %get-tuple-element.30) | copy-start | bytes 589828
  17.8 8.7 %copy-start.4 = (bf16[4,256,256]{2,1,0:T(8,128)(2,1)S(1)}, bf16[4,256,256]{2,1,0:T(8,128)(2,1)}, u32[]{:S(2)}) copy-start(bf16[4,256,256]{2,1,0:T(8,128)(2,1)} %weights.12) | copy-start | bytes 1572868
  17.8 8.7 %copy-start.5 = (bf16[256,256]{1,0:T(8,128)(2,1)S(1)}, bf16[256,256]{1,0:T(8,128)(2,1)}, u32[]{:S(2)}) copy-start(bf16[256,256]{1,0:T(8,128)(2,1)} %latent.3) | copy-start | bytes 393220
  20.0 6.5 %collective-permute-start.3 = (bf16[4,128,256]{2,1,0:T(8,128)(2,1)S(1)}, bf16[4,128,256]{2,1,0:T(8,128)(2,1)S(1)}, u32[]{:S(2)}, u32[]{:S(2)}) collective-permute-start(bf16[4,128,256]{2,1,0:T(8,128)(2,1)S(1)} %get-tuple-element.45), channel_id=1, source_target_pairs={{0,4},{4,0},{8,12},{12,8},{16,20},{20,16},{24,28},{28,24},{32,36},... | collective-permute-start | bytes 786440 | tf_op jit(solution)/shard_map/ppermute | solution.py:222
  20.1 10.4 %collective-permute-start.4 = (bf16[4,128,256]{2,1,0:T(8,128)(2,1)S(1)}, bf16[4,128,256]{2,1,0:T(8,128)(2,1)S(1)}, u32[]{:S(2)}, u32[]{:S(2)}) collective-permute-start(bf16[4,128,256]{2,1,0:T(8,128)(2,1)S(1)} %get-tuple-element.46), channel_id=1, source_target_pairs={{0,124},{4,8},{8,4},{12,16},{16,12},{20,24},{24,20},{28,32},{32,28... | collective-permute-start | bytes 786440 | tf_op jit(solution)/shard_map/ppermute | solution.py:226
  26.5 4.0 %copy-start = (bf16[8,256,256]{2,1,0:T(8,128)(2,1)S(1)}, bf16[8,256,256]{2,1,0:T(8,128)(2,1)}, u32[]{:S(2)}) copy-start(bf16[8,256,256]{2,1,0:T(8,128)(2,1)} %weights.16) | copy-start | bytes 3145732
  26.5 4.0 %copy-start.6 = (bf16[4,256]{1,0:T(4,128)(2,1)S(1)}, bf16[4,256]{1,0:T(4,128)(2,1)}, u32[]{:S(2)}) copy-start(bf16[4,256]{1,0:T(4,128)(2,1)} %gain.1) | copy-start | bytes 6148
  33.2 5.2 %collective-permute-start.6 = (bf16[256,256]{1,0:T(8,128)(2,1)S(1)}, bf16[256,256]{1,0:T(8,128)(2,1)S(1)}, u32[]{:S(2)}, u32[]{:S(2)}) collective-permute-start(bf16[256,256]{1,0:T(8,128)(2,1)S(1)} %get-tuple-element.48), channel_id=1, source_target_pairs={{0,3},{1,0},{2,1},{3,2},{4,7},{5,4},{6,5},{7,6},{8,11},{9,8},{10,9... | collective-permute-start | bytes 393224 | tf_op jit(solution)/shard_map/ppermute | solution.py:218
  35.6 6.2 %collective-permute-start.5 = (bf16[256,256]{1,0:T(8,128)(2,1)S(1)}, bf16[256,256]{1,0:T(8,128)(2,1)S(1)}, u32[]{:S(2)}, u32[]{:S(2)}) collective-permute-start(bf16[256,256]{1,0:T(8,128)(2,1)S(1)} %get-tuple-element.48), channel_id=1, source_target_pairs={{0,1},{1,2},{2,3},{3,0},{4,5},{5,6},{6,7},{7,4},{8,9},{9,10},{10,1... | collective-permute-start | bytes 393224 | tf_op jit(solution)/shard_map/ppermute | solution.py:218
  41.8 3.8 %collective-permute-start.7 = (bf16[3,256,256]{2,1,0:T(8,128)(2,1)S(1)}, bf16[3,256,256]{2,1,0:T(8,128)(2,1)S(1)}, u32[]{:S(2)}, u32[]{:S(2)}) collective-permute-start(bf16[3,256,256]{2,1,0:T(8,128)(2,1)S(1)} %pad_maximum_fusion.1.own), channel_id=1, source_target_pairs={{0,4},{4,0},{8,12},{12,8},{16,20},{20,16},{24,28},{28,24},{32,36},... | collective-permute-start | bytes 1179656 | tf_op jit(solution)/shard_map/ppermute | solution.py:222
  41.9 10.6 %collective-permute-start.8 = (bf16[3,256,256]{2,1,0:T(8,128)(2,1)S(1)}, bf16[3,256,256]{2,1,0:T(8,128)(2,1)S(1)}, u32[]{:S(2)}, u32[]{:S(2)}) collective-permute-start(bf16[3,256,256]{2,1,0:T(8,128)(2,1)S(1)} %pad_maximum_fusion.1.own), channel_id=1, source_target_pairs={{0,124},{4,8},{8,4},{12,16},{16,12},{20,24},{24,20},{28,32},{32,28... | collective-permute-start | bytes 1179656 | tf_op jit(solution)/shard_map/ppermute | solution.py:226
  54.6 5.0 %collective-permute-start.10 = (bf16[256,256]{1,0:T(8,128)(2,1)S(1)}, bf16[256,256]{1,0:T(8,128)(2,1)S(1)}, u32[]{:S(2)}, u32[]{:S(2)}) collective-permute-start(bf16[256,256]{1,0:T(8,128)(2,1)S(1)} %get-tuple-element.51), channel_id=1, source_target_pairs={{0,3},{1,0},{2,1},{3,2},{4,7},{5,4},{6,5},{7,6},{8,11},{9,8},{10,9... | collective-permute-start | bytes 393224 | tf_op jit(solution)/shard_map/ppermute | solution.py:218
  54.6 6.2 %collective-permute-start.9 = (bf16[256,256]{1,0:T(8,128)(2,1)S(1)}, bf16[256,256]{1,0:T(8,128)(2,1)S(1)}, u32[]{:S(2)}, u32[]{:S(2)}) collective-permute-start(bf16[256,256]{1,0:T(8,128)(2,1)S(1)} %get-tuple-element.51), channel_id=1, source_target_pairs={{0,1},{1,2},{2,3},{3,0},{4,5},{5,6},{6,7},{7,4},{8,9},{9,10},{10,1... | collective-permute-start | bytes 393224 | tf_op jit(solution)/shard_map/ppermute | solution.py:218
  60.9 2.7 %collective-permute-start.11 = (bf16[3,256,256]{2,1,0:T(8,128)(2,1)S(1)}, bf16[3,256,256]{2,1,0:T(8,128)(2,1)S(1)}, u32[]{:S(2)}, u32[]{:S(2)}) collective-permute-start(bf16[3,256,256]{2,1,0:T(8,128)(2,1)S(1)} %pad_maximum_fusion.2.own), channel_id=1, source_target_pairs={{0,4},{4,0},{8,12},{12,8},{16,20},{20,16},{24,28},{28,24},{32,36},... | collective-permute-start | bytes 1179656 | tf_op jit(solution)/shard_map/ppermute | solution.py:222
  61.0 10.6 %collective-permute-start.12 = (bf16[3,256,256]{2,1,0:T(8,128)(2,1)S(1)}, bf16[3,256,256]{2,1,0:T(8,128)(2,1)S(1)}, u32[]{:S(2)}, u32[]{:S(2)}) collective-permute-start(bf16[3,256,256]{2,1,0:T(8,128)(2,1)S(1)} %pad_maximum_fusion.2.own), channel_id=1, source_target_pairs={{0,124},{4,8},{8,4},{12,16},{16,12},{20,24},{24,20},{28,32},{32,28... | collective-permute-start | bytes 1179656 | tf_op jit(solution)/shard_map/ppermute | solution.py:226
  74.2 5.0 %collective-permute-start.15 = (bf16[256,256]{1,0:T(8,128)(2,1)S(1)}, bf16[256,256]{1,0:T(8,128)(2,1)S(1)}, u32[]{:S(2)}, u32[]{:S(2)}) collective-permute-start(bf16[256,256]{1,0:T(8,128)(2,1)S(1)} %get-tuple-element.53.own), channel_id=1, source_target_pairs={{0,3},{1,0},{2,1},{3,2},{4,7},{5,4},{6,5},{7,6},{8,11},{9,8},{10,9... | collective-permute-start | bytes 393224 | tf_op jit(solution)/shard_map/ppermute | solution.py:218
  74.2 6.5 %collective-permute-start.14 = (bf16[256,256]{1,0:T(8,128)(2,1)S(1)}, bf16[256,256]{1,0:T(8,128)(2,1)S(1)}, u32[]{:S(2)}, u32[]{:S(2)}) collective-permute-start(bf16[256,256]{1,0:T(8,128)(2,1)S(1)} %get-tuple-element.53.own), channel_id=1, source_target_pairs={{0,2},{1,3},{2,0},{3,1},{4,6},{5,7},{6,4},{7,5},{8,10},{9,11},{10,... | collective-permute-start | bytes 393224 | tf_op jit(solution)/shard_map/ppermute | solution.py:218
  77.0 6.2 %collective-permute-start.13 = (bf16[256,256]{1,0:T(8,128)(2,1)S(1)}, bf16[256,256]{1,0:T(8,128)(2,1)S(1)}, u32[]{:S(2)}, u32[]{:S(2)}) collective-permute-start(bf16[256,256]{1,0:T(8,128)(2,1)S(1)} %get-tuple-element.53.own), channel_id=1, source_target_pairs={{0,1},{1,2},{2,3},{3,0},{4,5},{5,6},{6,7},{7,4},{8,9},{9,10},{10,1... | collective-permute-start | bytes 393224 | tf_op jit(solution)/shard_map/ppermute | solution.py:218
  83.3 12.3 %copy-start.3 = (bf16[2048,256]{1,0:T(8,128)(2,1)S(1)}, bf16[2048,256]{1,0:T(8,128)(2,1)}, u32[]{:S(2)}) copy-start(bf16[2048,256]{1,0:T(8,128)(2,1)} %grid.3) | copy-start | bytes 3145732
  83.3 2.0 %collective-permute-start.16 = (bf16[4,256,256]{2,1,0:T(8,128)(2,1)S(1)}, bf16[4,256,256]{2,1,0:T(8,128)(2,1)S(1)}, u32[]{:S(2)}, u32[]{:S(2)}) collective-permute-start(bf16[4,256,256]{2,1,0:T(8,128)(2,1)S(1)} %pad_maximum_fusion.own), channel_id=1, source_target_pairs={{0,4},{4,0},{8,12},{12,8},{16,20},{20,16},{24,28},{28,24},{32,36},... | collective-permute-start | bytes 1572872 | tf_op jit(solution)/shard_map/ppermute | solution.py:222
  83.4 12.2 %collective-permute-start.17 = (bf16[4,256,256]{2,1,0:T(8,128)(2,1)S(1)}, bf16[4,256,256]{2,1,0:T(8,128)(2,1)S(1)}, u32[]{:S(2)}, u32[]{:S(2)}) collective-permute-start(bf16[4,256,256]{2,1,0:T(8,128)(2,1)S(1)} %pad_maximum_fusion.own), channel_id=1, source_target_pairs={{0,124},{4,8},{8,4},{12,16},{16,12},{20,24},{24,20},{28,32},{32,28... | collective-permute-start | bytes 1572872 | tf_op jit(solution)/shard_map/ppermute | solution.py:226

commit v4 on v3

--- a/solution.py
+++ b/solution.py
@@ -9,7 +9,7 @@
 
 STEPS = 2
 EDGE_BLOCK = 1024
-SEND_VMEM = 63
+SEND_VMEM = 62
 GRID_BLOCK = 1024
 epsilon = 1e-05
 VMEM = pl.BlockSpec(memory_space=pltpu.VMEM)
@@ -36,8 +36,14 @@
     return lax.rem(lax.axis_index("lat"), 2), lax.axis_index("lon")
 
 
+def columns():
+    _, lon = position()
+    step = 1 - 2 * lax.rem(lon, 2)
+    return [lon] + [lax.rem(lon + by + 4, 4) for by in (step, -step, 2)]
+
+
 def send_kernel(lists, grid, weights, out0, out1, out2, out3, rows_in, weight, table, picked, wanted, sems):
-    odd, lon = position()
+    odd, _ = position()
     slots = 128
     parts = 4
     size = rows_in.shape[0] // parts
@@ -50,7 +56,7 @@
             n = 3 * k + part
             fetch.append(
                 pltpu.make_async_copy(
-                    lists.at[side, lax.rem(lon + k, 4)], wanted.at[pl.ds(n * slots, slots)], sems.at[1 + parts + n]
+                    lists.at[side, columns()[k]], wanted.at[pl.ds(n * slots, slots)], sems.at[1 + parts + n]
                 )
             )
     for copy in fetch:
@@ -106,13 +112,14 @@
 
 
 def received_starts(width):
+    odd, _ = position()
+    return [[(band * 4 + column) * width for column in columns()] for band in (1, 2 - 2 * odd, 2 * odd)]
+
+
+def halo_starts(width):
     odd, lon = position()
-    return [[(band * 4 + lax.rem(lon + 4 - k, 4)) * width for k in range(4)] for band in (1, 2 - 2 * odd, 2 * odd)]
-
-
-def halo_starts(width):
-    odd, _ = position()
-    return [[(band * 3 + q) * width for q in range(3)] for band in (1, 2 - 2 * odd, 2 * odd)]
+    step = 1 - 2 * lax.rem(lon, 2)
+    return [[(band * 3 + q) * width for q in (1 + step, 1, 1 - step)] for band in (1, 2 - 2 * odd, 2 * odd)]
 
 
 def early_edges_kernel(starts, set_index, sources, targets, own, chip, latent, weights, out):
@@ -214,8 +221,9 @@
     )
 
 
-def along(x, by):
-    return lax.ppermute(x, "lon", [(i, (i + by) % 4) for i in range(4)])
+def along(x, k):
+    to = ((0, 1, 2, 3), (1, 0, 3, 2), (3, 2, 1, 0), (2, 3, 0, 1))[k]
+    return lax.ppermute(x, "lon", list(enumerate(to)))
 
 
 def swap_chip(x):
@@ -306,7 +314,7 @@
     )
     mesh_now, sent = edge_pass(received_starts, 0, encode_lanes, mesh_latent, own, chip, cross)
     for step in range(STEPS):
-        around = jnp.stack([along(sent, 1), sent, along(sent, -1)])
+        around = jnp.stack([along(sent, 1), sent, along(sent, 2)])
         mesh_now, sent = edge_pass(halo_starts, step + 1, mesh_lanes, mesh_now, around, around, around)
     beside = [along(sent, k) for k in (1, 2, 3)]
     (before,) = call(

time: 102 us -> 100 us (0.980)
  local copies, waits for them, and re-layouts: 1.37 us -> 0.15 us
    ppermute x10, starting transfers between devices: 13.2 us -> 11.9 us  [along(): return lax.ppermute(x, 'lon', list(enumerate(to)))]
    unnamed x26 -> x24, local copies, waits for them, and re-layouts: 1.29 us -> 0.07 us
  transfers between devices with their start and end apart: 18 -> 18, of which waited for: 13 -> 11; matrix products, arithmetic and copies ran while one was open for 0% -> 0% of each run, Pallas kernels for 20% -> 20%
where the time goes in v4:
time: 100 us
  Pallas kernels  39.6 us (40%)
  waiting for transfers between devices  32.2 us (32%)
  starting transfers between devices  26.9 us (27%)
  between operations  1 us (1%)
    ppermute x10, waiting for transfers between devices, along(): return lax.ppermute(x, 'lon', list(enumerate(to)))  17.1 us
    ppermute x4, waiting for transfers between devices, swap_cross(): lax.ppermute(x, 'lat', [(i, (i + 1 ^ 1) - 1) if 0 < i < 31 else (i, 31 -...  15.1 us
    ppermute x4, starting transfers between devices, swap_cross(): lax.ppermute(x, 'lat', [(i, (i + 1 ^ 1) - 1) if 0 < i < 31 else (i, 31 -...  14.7 us
    ppermute x10, starting transfers between devices, along(): return lax.ppermute(x, 'lon', list(enumerate(to)))  11.9 us
    pallas_call x3, Pallas kernels, edge_pass(): call(partial(late_edges_kernel, starts, set_index, stage), [VMEM] * 8, [s...  7.3 us
    pallas_call x3, Pallas kernels, edge_pass(): call(partial(early_edges_kernel, starts, set_index), [VMEM] * 6, [shape(e...  7.09 us
    pallas_call x1, Pallas kernels, shards(): call(early_grid_kernel, [VMEM] * 4, [shape(3 * grid_count, latent)], [],...  6.83 us
    pallas_call x1, Pallas kernels, shards(): call(late_grid_kernel, [VMEM] * 7, [shape(grid_count, latent)], [], 10 ** 9)  6.66 us
  transfers between devices with their start and end apart: 18, of which 11 were waited for; matrix products, arithmetic and copies ran while one was open for 0% of the time, Pallas kernels for 20%

profile of v4, /device:TPU:0, one launch (start us, length us, event | category | flops | bytes accessed | tf_op | source)
XLA Modules:
  0.0 100.1 jit_solution(5797962990222316534)
XLA Ops:
  0.7 5.6 %shard_map.131 = (bf16[3,128,256]{2,1,0:T(8,128)(2,1)}, bf16[3,128,256]{2,1,0:T(8,128)(2,1)}, bf16[3,128,256]{2,1,0:T(8,128)(2,1)}, bf16[3,128,256]{2,1,0:T(8,128)(2,1)}) custom-call(s32[3,4,128]{2,1,0:T(4,128)} %lists.1, bf16[2048,256]{1,0:T(8,128)(2,1)} %grid.3, bf16[4,256,256]{2,1,0:T(8,128)(2,1)} %weights.12), custom_call_target="tpu_custom_call" | custom-call | flops 1000000000 | bytes 1048576 | tf_op jit(solution)/shard_map/pallas_call | solution.py:287
  6.3 1.7 %collective-permute-start = (bf16[3,128,256]{2,1,0:T(8,128)(2,1)}, bf16[3,128,256]{2,1,0:T(8,128)(2,1)S(1)}, u32[]{:S(2)}, u32[]{:S(2)}) collective-permute-start(bf16[3,128,256]{2,1,0:T(8,128)(2,1)} %get-tuple-element.31), channel_id=1, source_target_pairs={{0,1},{1,0},{2,3},{3,2},{4,5},{5,4},{6,7},{7,6},{8,9},{9,8},{10,11... | collective-permute-start | bytes 589832 | tf_op jit(solution)/shard_map/ppermute | solution.py:226
  8.0 2.2 %collective-permute-start.1 = (bf16[3,128,256]{2,1,0:T(8,128)(2,1)}, bf16[3,128,256]{2,1,0:T(8,128)(2,1)S(1)}, u32[]{:S(2)}, u32[]{:S(2)}) collective-permute-start(bf16[3,128,256]{2,1,0:T(8,128)(2,1)} %get-tuple-element.32), channel_id=1, source_target_pairs={{0,3},{1,2},{2,1},{3,0},{4,7},{5,6},{6,5},{7,4},{8,11},{9,10},{10,... | collective-permute-start | bytes 589832 | tf_op jit(solution)/shard_map/ppermute | solution.py:226
  10.2 0.7 collective-permute-start.2
  11.0 0.4 shard_map.135.proj
  11.4 0.0 copy-start.8
  11.4 0.9 shard_map.134.sources
  12.3 0.0 copy-start.6
  12.3 0.0 copy-start.7
  12.4 1.0 shard_map.133
  13.3 0.0 copy-start.10
  13.4 2.0 %shard_map.132 = (s16[4096,128]{1,0:T(8,128)(2,1)S(1)}, s16[4096,128]{1,0:T(8,128)(2,1)S(1)}, bf16[256,4096]{1,0:T(8,128)(2,1)S(1)}) custom-call(s32[32,128]{1,0:T(8,128)S(1)} %bitcast.18, s32[32,128]{1,0:T(8,128)S(1)} %bitcast.19), custom_call_target="tpu_custom_call" | custom-call | flops 1000000000 | bytes 1048576 | tf_op jit(solution)/shard_map/pallas_call | solution.py:256
  15.3 0.0 copy-start.3
  15.4 3.2 %collective-permute-done.1 = bf16[3,128,256]{2,1,0:T(8,128)(2,1)S(1)} collective-permute-done((bf16[3,128,256]{2,1,0:T(8,128)(2,1)}, bf16[3,128,256]{2,1,0:T(8,128)(2,1)S(1)}, u32[]{:S(2)}, u32[]{:S(2)}) %collective-permute-start.1) | collective-permute-done | bytes 196640 | tf_op jit(solution)/shard_map/ppermute | solution.py:226
  18.6 1.4 %collective-permute-done.2 = bf16[3,128,256]{2,1,0:T(8,128)(2,1)S(1)} collective-permute-done((bf16[3,128,256]{2,1,0:T(8,128)(2,1)}, bf16[3,128,256]{2,1,0:T(8,128)(2,1)S(1)}, u32[]{:S(2)}, u32[]{:S(2)}) %collective-permute-start.2) | collective-permute-done | bytes 196640 | tf_op jit(solution)/shard_map/ppermute | solution.py:226
  20.0 0.1 pad_maximum_fusion.3
  20.1 0.1 collective-permute-start.3
  20.2 6.3 %collective-permute-start.4 = (bf16[4,128,256]{2,1,0:T(8,128)(2,1)S(1)}, bf16[4,128,256]{2,1,0:T(8,128)(2,1)S(1)}, u32[]{:S(2)}, u32[]{:S(2)}) collective-permute-start(bf16[4,128,256]{2,1,0:T(8,128)(2,1)S(1)} %get-tuple-element.46), channel_id=1, source_target_pairs={{0,124},{4,8},{8,4},{12,16},{16,12},{20,24},{24,20},{28,32},{32,28... | collective-permute-start | bytes 786440 | tf_op jit(solution)/shard_map/ppermute | solution.py:234
  26.6 2.9 %shard_map.136.early = bf16[4096,256]{1,0:T(8,128)(2,1)S(1)} custom-call(s16[4096,128]{1,0:T(8,128)(2,1)S(1)} %get-tuple-element.43.sources, s16[4096,128]{1,0:T(8,128)(2,1)S(1)} %get-tuple-element.44.targets, bf16[4,128,256]{2,1,0:T(8,128)(2,1)S(1)} %pad_maximum_fusion.5.own, bf16[4,128,256]{2,1,0:T(8,128)(2,1)S(1)} %collective-permute-done.3.chip, ...), custom_call_target="tpu_custom_call" | custom-call | flops 2147483648 | bytes 1048576 | tf_op jit(solution)/shard_map/pallas_call | solution.py:272
  29.6 1.0 %collective-permute-done.4.cross = bf16[4,128,256]{2,1,0:T(8,128)(2,1)S(1)} collective-permute-done((bf16[4,128,256]{2,1,0:T(8,128)(2,1)S(1)}, bf16[4,128,256]{2,1,0:T(8,128)(2,1)S(1)}, u32[]{:S(2)}, u32[]{:S(2)}) %collective-permute-start.4) | collective-permute-done | bytes 262176 | tf_op jit(solution)/shard_map/ppermute | solution.py:234
  30.6 2.7 %shard_map.137 = (bf16[256,256]{1,0:T(8,128)(2,1)S(1)}, bf16[256,256]{1,0:T(8,128)(2,1)S(1)}) custom-call(s16[4096,128]{1,0:T(8,128)(2,1)S(1)} %get-tuple-element.43.sources, bf16[4096,256]{1,0:T(8,128)(2,1)S(1)} %shard_map.136.early, bf16[4,128,256]{2,1,0:T(8,128)(2,1)S(1)} %collective-permute-done.4.cross, ...), custom_call_target="tpu_custom_call" | custom-call | flops 1073741824 | bytes 1048576 | tf_op jit(solution)/shard_map/pallas_call | solution.py:279
  33.3 2.5 %collective-permute-start.6 = (bf16[256,256]{1,0:T(8,128)(2,1)S(1)}, bf16[256,256]{1,0:T(8,128)(2,1)S(1)}, u32[]{:S(2)}, u32[]{:S(2)}) collective-permute-start(bf16[256,256]{1,0:T(8,128)(2,1)S(1)} %get-tuple-element.48), channel_id=1, source_target_pairs={{0,3},{1,2},{2,1},{3,0},{4,7},{5,6},{6,5},{7,4},{8,11},{9,10},{10,... | collective-permute-start | bytes 393224 | tf_op jit(solution)/shard_map/ppermute | solution.py:226
  35.8 4.0 %collective-permute-done.6 = bf16[256,256]{1,0:T(8,128)(2,1)S(1)} collective-permute-done((bf16[256,256]{1,0:T(8,128)(2,1)S(1)}, bf16[256,256]{1,0:T(8,128)(2,1)S(1)}, u32[]{:S(2)}, u32[]{:S(2)}) %collective-permute-start.6) | collective-permute-done | bytes 131104 | tf_op jit(solution)/shard_map/ppermute | solution.py:226
  39.8 1.0 %collective-permute-done.5 = bf16[256,256]{1,0:T(8,128)(2,1)S(1)} collective-permute-done((bf16[256,256]{1,0:T(8,128)(2,1)S(1)}, bf16[256,256]{1,0:T(8,128)(2,1)S(1)}, u32[]{:S(2)}, u32[]{:S(2)}) %collective-permute-start.5) | collective-permute-done | bytes 131104 | tf_op jit(solution)/shard_map/ppermute | solution.py:226
  40.8 0.1 collective-permute-start.7
  40.9 3.7 %collective-permute-start.8 = (bf16[3,256,256]{2,1,0:T(8,128)(2,1)S(1)}, bf16[3,256,256]{2,1,0:T(8,128)(2,1)S(1)}, u32[]{:S(2)}, u32[]{:S(2)}) collective-permute-start(bf16[3,256,256]{2,1,0:T(8,128)(2,1)S(1)} %pad_maximum_fusion.1.own), channel_id=1, source_target_pairs={{0,124},{4,8},{8,4},{12,16},{16,12},{20,24},{24,20},{28,32},{32,28... | collective-permute-start | bytes 1179656 | tf_op jit(solution)/shard_map/ppermute | solution.py:234
  44.6 2.1 %shard_map.138.early = bf16[2048,256]{1,0:T(8,128)(2,1)S(1)} custom-call(s16[2048,128]{1,0:T(8,128)(2,1)S(1)} %get-tuple-element.41.sources, s16[2048,128]{1,0:T(8,128)(2,1)S(1)} %get-tuple-element.42.targets, bf16[3,256,256]{2,1,0:T(8,128)(2,1)S(1)} %pad_maximum_fusion.1.own, bf16[3,256,256]{2,1,0:T(8,128)(2,1)S(1)} %collective-permute-done.7.chip, ...), custom_call_target="tpu_custom_call" | custom-call | flops 1610612736 | bytes 1048576 | tf_op jit(solution)/shard_map/pallas_call | solution.py:272
  46.7 4.8 %collective-permute-done.8.cross = bf16[3,256,256]{2,1,0:T(8,128)(2,1)S(1)} collective-permute-done((bf16[3,256,256]{2,1,0:T(8,128)(2,1)S(1)}, bf16[3,256,256]{2,1,0:T(8,128)(2,1)S(1)}, u32[]{:S(2)}, u32[]{:S(2)}) %collective-permute-start.8) | collective-permute-done | bytes 393248 | tf_op jit(solution)/shard_map/ppermute | solution.py:234
  51.5 2.0 %shard_map.139 = (bf16[256,256]{1,0:T(8,128)(2,1)S(1)}, bf16[256,256]{1,0:T(8,128)(2,1)S(1)}) custom-call(s16[2048,128]{1,0:T(8,128)(2,1)S(1)} %get-tuple-element.41.sources, bf16[2048,256]{1,0:T(8,128)(2,1)S(1)} %shard_map.138.early, bf16[3,256,256]{2,1,0:T(8,128)(2,1)S(1)} %collective-permute-done.8.cross, ...), custom_call_target="tpu_custom_call" | custom-call | flops 805306368 | bytes 1048576 | tf_op jit(solution)/shard_map/pallas_call | solution.py:279
  53.5 1.3 %collective-permute-start.10 = (bf16[256,256]{1,0:T(8,128)(2,1)S(1)}, bf16[256,256]{1,0:T(8,128)(2,1)S(1)}, u32[]{:S(2)}, u32[]{:S(2)}) collective-permute-start(bf16[256,256]{1,0:T(8,128)(2,1)S(1)} %get-tuple-element.51), channel_id=1, source_target_pairs={{0,3},{1,2},{2,1},{3,0},{4,7},{5,6},{6,5},{7,4},{8,11},{9,10},{10,... | collective-permute-start | bytes 393224 | tf_op jit(solution)/shard_map/ppermute | solution.py:226
  54.8 5.0 %collective-permute-done.10 = bf16[256,256]{1,0:T(8,128)(2,1)S(1)} collective-permute-done((bf16[256,256]{1,0:T(8,128)(2,1)S(1)}, bf16[256,256]{1,0:T(8,128)(2,1)S(1)}, u32[]{:S(2)}, u32[]{:S(2)}) %collective-permute-start.10) | collective-permute-done | bytes 131104 | tf_op jit(solution)/shard_map/ppermute | solution.py:226
  59.9 0.1 collective-permute-start.11
  60.0 2.6 %collective-permute-start.12 = (bf16[3,256,256]{2,1,0:T(8,128)(2,1)S(1)}, bf16[3,256,256]{2,1,0:T(8,128)(2,1)S(1)}, u32[]{:S(2)}, u32[]{:S(2)}) collective-permute-start(bf16[3,256,256]{2,1,0:T(8,128)(2,1)S(1)} %pad_maximum_fusion.2.own), channel_id=1, source_target_pairs={{0,124},{4,8},{8,4},{12,16},{16,12},{20,24},{24,20},{28,32},{32,28... | collective-permute-start | bytes 1179656 | tf_op jit(solution)/shard_map/ppermute | solution.py:234
  62.5 2.1 %shard_map.140.early = bf16[2048,256]{1,0:T(8,128)(2,1)S(1)} custom-call(s16[2048,128]{1,0:T(8,128)(2,1)S(1)} %get-tuple-element.41.sources, s16[2048,128]{1,0:T(8,128)(2,1)S(1)} %get-tuple-element.42.targets, bf16[3,256,256]{2,1,0:T(8,128)(2,1)S(1)} %pad_maximum_fusion.2.own, bf16[3,256,256]{2,1,0:T(8,128)(2,1)S(1)} %collective-permute-done.11.chip, ...), custom_call_target="tpu_custom_call" | custom-call | flops 1610612736 | bytes 1048576 | tf_op jit(solution)/shard_map/pallas_call | solution.py:272
  64.6 5.9 %collective-permute-done.12.cross = bf16[3,256,256]{2,1,0:T(8,128)(2,1)S(1)} collective-permute-done((bf16[3,256,256]{2,1,0:T(8,128)(2,1)S(1)}, bf16[3,256,256]{2,1,0:T(8,128)(2,1)S(1)}, u32[]{:S(2)}, u32[]{:S(2)}) %collective-permute-start.12) | collective-permute-done | bytes 393248 | tf_op jit(solution)/shard_map/ppermute | solution.py:234
  70.6 2.6 %shard_map.141 = (bf16[256,256]{1,0:T(8,128)(2,1)}, bf16[256,256]{1,0:T(8,128)(2,1)S(1)}) custom-call(s16[2048,128]{1,0:T(8,128)(2,1)S(1)} %get-tuple-element.41.sources, bf16[2048,256]{1,0:T(8,128)(2,1)S(1)} %shard_map.140.early, bf16[3,256,256]{2,1,0:T(8,128)(2,1)S(1)} %collective-permute-done.12.cross, bf16[256,2048]{1,0:T(8,128)(2,1)S(1)} %get-tuple-element.50.incidence, ...), custom_call_target="tpu_custom_call" | custom-call | flops 805306368 | bytes 1048576 | tf_op jit(solution)/shard_map/pallas_call | solution.py:279
  73.1 1.5 %collective-permute-start.15 = (bf16[256,256]{1,0:T(8,128)(2,1)S(1)}, bf16[256,256]{1,0:T(8,128)(2,1)S(1)}, u32[]{:S(2)}, u32[]{:S(2)}) collective-permute-start(bf16[256,256]{1,0:T(8,128)(2,1)S(1)} %get-tuple-element.53.own), channel_id=1, source_target_pairs={{0,2},{1,3},{2,0},{3,1},{4,6},{5,7},{6,4},{7,5},{8,10},{9,11},{10,... | collective-permute-start | bytes 393224 | tf_op jit(solution)/shard_map/ppermute | solution.py:226
  74.6 1.2 %collective-permute-start.14 = (bf16[256,256]{1,0:T(8,128)(2,1)S(1)}, bf16[256,256]{1,0:T(8,128)(2,1)S(1)}, u32[]{:S(2)}, u32[]{:S(2)}) collective-permute-start(bf16[256,256]{1,0:T(8,128)(2,1)S(1)} %get-tuple-element.53.own), channel_id=1, source_target_pairs={{0,3},{1,2},{2,1},{3,0},{4,7},{5,6},{6,5},{7,4},{8,11},{9,10},{10,... | collective-permute-start | bytes 393224 | tf_op jit(solution)/shard_map/ppermute | solution.py:226
  75.8 0.8 collective-permute-start.13
  76.6 1.8 %shard_map.142.before = bf16[6144,256]{1,0:T(8,128)(2,1)S(1)} custom-call(s16[6144,128]{1,0:T(8,128)(2,1)S(1)} %shard_map.134.sources, bf16[256,256]{1,0:T(8,128)(2,1)S(1)} %get-tuple-element.53.own), custom_call_target="tpu_custom_call" | custom-call | flops 805306368 | bytes 1048576 | tf_op jit(solution)/shard_map/pallas_call | solution.py:320
  78.4 1.2 %collective-permute-done.15 = bf16[256,256]{1,0:T(8,128)(2,1)S(1)} collective-permute-done((bf16[256,256]{1,0:T(8,128)(2,1)S(1)}, bf16[256,256]{1,0:T(8,128)(2,1)S(1)}, u32[]{:S(2)}, u32[]{:S(2)}) %collective-permute-start.15) | collective-permute-done | bytes 131104 | tf_op jit(solution)/shard_map/ppermute | solution.py:226
  79.6 1.4 %collective-permute-done.14 = bf16[256,256]{1,0:T(8,128)(2,1)S(1)} collective-permute-done((bf16[256,256]{1,0:T(8,128)(2,1)S(1)}, bf16[256,256]{1,0:T(8,128)(2,1)S(1)}, u32[]{:S(2)}, u32[]{:S(2)}) %collective-permute-start.14) | collective-permute-done | bytes 131104 | tf_op jit(solution)/shard_map/ppermute | solution.py:226
  81.0 0.1 pad_maximum_fusion.own
  81.1 0.1 collective-permute-start.16
  81.2 2.0 %collective-permute-start.17 = (bf16[4,256,256]{2,1,0:T(8,128)(2,1)S(1)}, bf16[4,256,256]{2,1,0:T(8,128)(2,1)S(1)}, u32[]{:S(2)}, u32[]{:S(2)}) collective-permute-start(bf16[4,256,256]{2,1,0:T(8,128)(2,1)S(1)} %pad_maximum_fusion.own), channel_id=1, source_target_pairs={{0,124},{4,8},{8,4},{12,16},{16,12},{20,24},{24,20},{28,32},{32,28... | collective-permute-start | bytes 1572872 | tf_op jit(solution)/shard_map/ppermute | solution.py:234
  83.2 6.8 %shard_map.143.early = bf16[6144,256]{1,0:T(8,128)(2,1)S(1)} custom-call(s16[6144,128]{1,0:T(8,128)(2,1)S(1)} %shard_map.134.sources, bf16[6144,256]{1,0:T(8,128)(2,1)S(1)} %shard_map.142.before, bf16[4,256,256]{2,1,0:T(8,128)(2,1)S(1)} %pad_maximum_fusion.own, bf16[4,256,256]{2,1,0:T(8,128)(2,1)S(1)} %collective-permute-done.16.chip), custom_call_target="tpu_custom_call" | custom-call | flops 5637144576 | bytes 1048576 | tf_op jit(solution)/shard_map/pallas_call | solution.py:330
  90.0 3.3 %collective-permute-done.17.cross = bf16[4,256,256]{2,1,0:T(8,128)(2,1)S(1)} collective-permute-done((bf16[4,256,256]{2,1,0:T(8,128)(2,1)S(1)}, bf16[4,256,256]{2,1,0:T(8,128)(2,1)S(1)}, u32[]{:S(2)}, u32[]{:S(2)}) %collective-permute-start.17) | collective-permute-done | bytes 524320 | tf_op jit(solution)/shard_map/ppermute | solution.py:234
  93.4 6.7 %shard_map.144 = bf16[2048,256]{1,0:T(8,128)(2,1)} custom-call(s16[6144,128]{1,0:T(8,128)(2,1)S(1)} %shard_map.134.sources, bf16[6144,256]{1,0:T(8,128)(2,1)S(1)} %shard_map.143.early, bf16[4,256,256]{2,1,0:T(8,128)(2,1)S(1)} %collective-permute-done.17.cross, bf16[2048,256]{1,0:T(8,128)(2,1)S(1)} %copy-done.2, bf16[2048,256]{1,0:T(8,128)(2,1)S(1)} %shard_map.135.proj, ...), custom_call_target="tpu_custom_call" | custom-call | flops 1000000000 | bytes 1048576 | tf_op jit(solution)/shard_map/pallas_call | solution.py:337
  (36 shorter events, 0.3 us)
Async XLA Ops:
  0.6 10.3 %copy-start.2 = (bf16[2048,256]{1,0:T(8,128)(2,1)S(1)}, bf16[2048,256]{1,0:T(8,128)(2,1)}, u32[]{:S(2)}) copy-start(bf16[2048,256]{1,0:T(8,128)(2,1)} %grid.3) | copy-start | bytes 3145732
  0.6 10.3 %copy-start.11 = (s32[2048,3]{0,1:T(4,128)S(1)}, s32[2048,3]{0,1:T(4,128)}, u32[]{:S(2)}) copy-start(s32[2048,3]{0,1:T(4,128)} %param.19) | copy-start | bytes 73732
  0.7 10.3 %copy-start.1 = (bf16[4,256,256]{2,1,0:T(8,128)(2,1)S(1)}, bf16[4,256,256]{2,1,0:T(8,128)(2,1)}, u32[]{:S(2)}) copy-start(bf16[4,256,256]{2,1,0:T(8,128)(2,1)} %weights.17) | copy-start | bytes 1572868
  6.3 9.1 %collective-permute-start = (bf16[3,128,256]{2,1,0:T(8,128)(2,1)}, bf16[3,128,256]{2,1,0:T(8,128)(2,1)S(1)}, u32[]{:S(2)}, u32[]{:S(2)}) collective-permute-start(bf16[3,128,256]{2,1,0:T(8,128)(2,1)} %get-tuple-element.31), channel_id=1, source_target_pairs={{0,1},{1,0},{2,3},{3,2},{4,5},{5,4},{6,7},{7,6},{8,9},{9,8},{10,11... | collective-permute-start | bytes 589832 | tf_op jit(solution)/shard_map/ppermute | solution.py:226
  8.0 10.6 %collective-permute-start.1 = (bf16[3,128,256]{2,1,0:T(8,128)(2,1)}, bf16[3,128,256]{2,1,0:T(8,128)(2,1)S(1)}, u32[]{:S(2)}, u32[]{:S(2)}) collective-permute-start(bf16[3,128,256]{2,1,0:T(8,128)(2,1)} %get-tuple-element.32), channel_id=1, source_target_pairs={{0,3},{1,2},{2,1},{3,0},{4,7},{5,6},{6,5},{7,4},{8,11},{9,10},{10,... | collective-permute-start | bytes 589832 | tf_op jit(solution)/shard_map/ppermute | solution.py:226
  10.2 9.8 %collective-permute-start.2 = (bf16[3,128,256]{2,1,0:T(8,128)(2,1)}, bf16[3,128,256]{2,1,0:T(8,128)(2,1)S(1)}, u32[]{:S(2)}, u32[]{:S(2)}) collective-permute-start(bf16[3,128,256]{2,1,0:T(8,128)(2,1)} %get-tuple-element.33), channel_id=1, source_target_pairs={{0,2},{1,3},{2,0},{3,1},{4,6},{5,7},{6,4},{7,5},{8,10},{9,11},{10,... | collective-permute-start | bytes 589832 | tf_op jit(solution)/shard_map/ppermute | solution.py:226
  11.4 0.9 copy-start.8
  11.4 0.9 copy-start.9
  12.3 1.0 %copy-start.6 = (s32[4096]{0:T(1024)S(1)}, s32[4096]{0:T(1024)}, u32[]{:S(2)}) copy-start(s32[4096]{0:T(1024)} %param.15) | copy-start | bytes 49156
  12.3 1.0 %copy-start.7 = (s32[4096]{0:T(1024)S(1)}, s32[4096]{0:T(1024)}, u32[]{:S(2)}) copy-start(s32[4096]{0:T(1024)} %param.16) | copy-start | bytes 49156
  13.3 2.0 %copy-start.10 = (bf16[3,128,256]{2,1,0:T(8,128)(2,1)S(1)}, bf16[3,128,256]{2,1,0:T(8,128)(2,1)}, u32[]{:S(2)}) copy-start(bf16[3,128,256]{2,1,0:T(8,128)(2,1)} %get-tuple-element.30) | copy-start | bytes 589828
  15.3 11.3 %copy-start.3 = (bf16[4,256,256]{2,1,0:T(8,128)(2,1)S(1)}, bf16[4,256,256]{2,1,0:T(8,128)(2,1)}, u32[]{:S(2)}) copy-start(bf16[4,256,256]{2,1,0:T(8,128)(2,1)} %weights.12) | copy-start | bytes 1572868
  15.3 11.3 %copy-start.4 = (bf16[256,256]{1,0:T(8,128)(2,1)S(1)}, bf16[256,256]{1,0:T(8,128)(2,1)}, u32[]{:S(2)}) copy-start(bf16[256,256]{1,0:T(8,128)(2,1)} %latent.3) | copy-start | bytes 393220
  20.1 6.5 %collective-permute-start.3 = (bf16[4,128,256]{2,1,0:T(8,128)(2,1)S(1)}, bf16[4,128,256]{2,1,0:T(8,128)(2,1)S(1)}, u32[]{:S(2)}, u32[]{:S(2)}) collective-permute-start(bf16[4,128,256]{2,1,0:T(8,128)(2,1)S(1)} %get-tuple-element.45), channel_id=1, source_target_pairs={{0,4},{4,0},{8,12},{12,8},{16,20},{20,16},{24,28},{28,24},{32,36},... | collective-permute-start | bytes 786440 | tf_op jit(solution)/shard_map/ppermute | solution.py:230
  20.2 10.4 %collective-permute-start.4 = (bf16[4,128,256]{2,1,0:T(8,128)(2,1)S(1)}, bf16[4,128,256]{2,1,0:T(8,128)(2,1)S(1)}, u32[]{:S(2)}, u32[]{:S(2)}) collective-permute-start(bf16[4,128,256]{2,1,0:T(8,128)(2,1)S(1)} %get-tuple-element.46), channel_id=1, source_target_pairs={{0,124},{4,8},{8,4},{12,16},{16,12},{20,24},{24,20},{28,32},{32,28... | collective-permute-start | bytes 786440 | tf_op jit(solution)/shard_map/ppermute | solution.py:234
  26.6 4.0 %copy-start = (bf16[8,256,256]{2,1,0:T(8,128)(2,1)S(1)}, bf16[8,256,256]{2,1,0:T(8,128)(2,1)}, u32[]{:S(2)}) copy-start(bf16[8,256,256]{2,1,0:T(8,128)(2,1)} %weights.16) | copy-start | bytes 3145732
  26.6 4.0 %copy-start.5 = (bf16[4,256]{1,0:T(4,128)(2,1)S(1)}, bf16[4,256]{1,0:T(4,128)(2,1)}, u32[]{:S(2)}) copy-start(bf16[4,256]{1,0:T(4,128)(2,1)} %gain.1) | copy-start | bytes 6148
  33.3 6.4 %collective-permute-start.6 = (bf16[256,256]{1,0:T(8,128)(2,1)S(1)}, bf16[256,256]{1,0:T(8,128)(2,1)S(1)}, u32[]{:S(2)}, u32[]{:S(2)}) collective-permute-start(bf16[256,256]{1,0:T(8,128)(2,1)S(1)} %get-tuple-element.48), channel_id=1, source_target_pairs={{0,3},{1,2},{2,1},{3,0},{4,7},{5,6},{6,5},{7,4},{8,11},{9,10},{10,... | collective-permute-start | bytes 393224 | tf_op jit(solution)/shard_map/ppermute | solution.py:226
  35.8 5.0 %collective-permute-start.5 = (bf16[256,256]{1,0:T(8,128)(2,1)S(1)}, bf16[256,256]{1,0:T(8,128)(2,1)S(1)}, u32[]{:S(2)}, u32[]{:S(2)}) collective-permute-start(bf16[256,256]{1,0:T(8,128)(2,1)S(1)} %get-tuple-element.48), channel_id=1, source_target_pairs={{0,1},{1,0},{2,3},{3,2},{4,5},{5,4},{6,7},{7,6},{8,9},{9,8},{10,11... | collective-permute-start | bytes 393224 | tf_op jit(solution)/shard_map/ppermute | solution.py:226
  40.8 3.8 %collective-permute-start.7 = (bf16[3,256,256]{2,1,0:T(8,128)(2,1)S(1)}, bf16[3,256,256]{2,1,0:T(8,128)(2,1)S(1)}, u32[]{:S(2)}, u32[]{:S(2)}) collective-permute-start(bf16[3,256,256]{2,1,0:T(8,128)(2,1)S(1)} %pad_maximum_fusion.1.own), channel_id=1, source_target_pairs={{0,4},{4,0},{8,12},{12,8},{16,20},{20,16},{24,28},{28,24},{32,36},... | collective-permute-start | bytes 1179656 | tf_op jit(solution)/shard_map/ppermute | solution.py:230
  40.9 10.6 %collective-permute-start.8 = (bf16[3,256,256]{2,1,0:T(8,128)(2,1)S(1)}, bf16[3,256,256]{2,1,0:T(8,128)(2,1)S(1)}, u32[]{:S(2)}, u32[]{:S(2)}) collective-permute-start(bf16[3,256,256]{2,1,0:T(8,128)(2,1)S(1)} %pad_maximum_fusion.1.own), channel_id=1, source_target_pairs={{0,124},{4,8},{8,4},{12,16},{16,12},{20,24},{24,20},{28,32},{32,28... | collective-permute-start | bytes 1179656 | tf_op jit(solution)/shard_map/ppermute | solution.py:234
  53.5 6.3 %collective-permute-start.10 = (bf16[256,256]{1,0:T(8,128)(2,1)S(1)}, bf16[256,256]{1,0:T(8,128)(2,1)S(1)}, u32[]{:S(2)}, u32[]{:S(2)}) collective-permute-start(bf16[256,256]{1,0:T(8,128)(2,1)S(1)} %get-tuple-element.51), channel_id=1, source_target_pairs={{0,3},{1,2},{2,1},{3,0},{4,7},{5,6},{6,5},{7,4},{8,11},{9,10},{10,... | collective-permute-start | bytes 393224 | tf_op jit(solution)/shard_map/ppermute | solution.py:226
  54.8 5.0 %collective-permute-start.9 = (bf16[256,256]{1,0:T(8,128)(2,1)S(1)}, bf16[256,256]{1,0:T(8,128)(2,1)S(1)}, u32[]{:S(2)}, u32[]{:S(2)}) collective-permute-start(bf16[256,256]{1,0:T(8,128)(2,1)S(1)} %get-tuple-element.51), channel_id=1, source_target_pairs={{0,1},{1,0},{2,3},{3,2},{4,5},{5,4},{6,7},{7,6},{8,9},{9,8},{10,11... | collective-permute-start | bytes 393224 | tf_op jit(solution)/shard_map/ppermute | solution.py:226
  59.9 2.7 %collective-permute-start.11 = (bf16[3,256,256]{2,1,0:T(8,128)(2,1)S(1)}, bf16[3,256,256]{2,1,0:T(8,128)(2,1)S(1)}, u32[]{:S(2)}, u32[]{:S(2)}) collective-permute-start(bf16[3,256,256]{2,1,0:T(8,128)(2,1)S(1)} %pad_maximum_fusion.2.own), channel_id=1, source_target_pairs={{0,4},{4,0},{8,12},{12,8},{16,20},{20,16},{24,28},{28,24},{32,36},... | collective-permute-start | bytes 1179656 | tf_op jit(solution)/shard_map/ppermute | solution.py:230
  60.0 10.6 %collective-permute-start.12 = (bf16[3,256,256]{2,1,0:T(8,128)(2,1)S(1)}, bf16[3,256,256]{2,1,0:T(8,128)(2,1)S(1)}, u32[]{:S(2)}, u32[]{:S(2)}) collective-permute-start(bf16[3,256,256]{2,1,0:T(8,128)(2,1)S(1)} %pad_maximum_fusion.2.own), channel_id=1, source_target_pairs={{0,124},{4,8},{8,4},{12,16},{16,12},{20,24},{24,20},{28,32},{32,28... | collective-permute-start | bytes 1179656 | tf_op jit(solution)/shard_map/ppermute | solution.py:234
  73.1 6.5 %collective-permute-start.15 = (bf16[256,256]{1,0:T(8,128)(2,1)S(1)}, bf16[256,256]{1,0:T(8,128)(2,1)S(1)}, u32[]{:S(2)}, u32[]{:S(2)}) collective-permute-start(bf16[256,256]{1,0:T(8,128)(2,1)S(1)} %get-tuple-element.53.own), channel_id=1, source_target_pairs={{0,2},{1,3},{2,0},{3,1},{4,6},{5,7},{6,4},{7,5},{8,10},{9,11},{10,... | collective-permute-start | bytes 393224 | tf_op jit(solution)/shard_map/ppermute | solution.py:226
  74.6 6.4 %collective-permute-start.14 = (bf16[256,256]{1,0:T(8,128)(2,1)S(1)}, bf16[256,256]{1,0:T(8,128)(2,1)S(1)}, u32[]{:S(2)}, u32[]{:S(2)}) collective-permute-start(bf16[256,256]{1,0:T(8,128)(2,1)S(1)} %get-tuple-element.53.own), channel_id=1, source_target_pairs={{0,3},{1,2},{2,1},{3,0},{4,7},{5,6},{6,5},{7,4},{8,11},{9,10},{10,... | collective-permute-start | bytes 393224 | tf_op jit(solution)/shard_map/ppermute | solution.py:226
  75.8 5.2 %collective-permute-start.13 = (bf16[256,256]{1,0:T(8,128)(2,1)S(1)}, bf16[256,256]{1,0:T(8,128)(2,1)S(1)}, u32[]{:S(2)}, u32[]{:S(2)}) collective-permute-start(bf16[256,256]{1,0:T(8,128)(2,1)S(1)} %get-tuple-element.53.own), channel_id=1, source_target_pairs={{0,1},{1,0},{2,3},{3,2},{4,5},{5,4},{6,7},{7,6},{8,9},{9,8},{10,11... | collective-permute-start | bytes 393224 | tf_op jit(solution)/shard_map/ppermute | solution.py:226
  81.1 2.1 %collective-permute-start.16 = (bf16[4,256,256]{2,1,0:T(8,128)(2,1)S(1)}, bf16[4,256,256]{2,1,0:T(8,128)(2,1)S(1)}, u32[]{:S(2)}, u32[]{:S(2)}) collective-permute-start(bf16[4,256,256]{2,1,0:T(8,128)(2,1)S(1)} %pad_maximum_fusion.own), channel_id=1, source_target_pairs={{0,4},{4,0},{8,12},{12,8},{16,20},{20,16},{24,28},{28,24},{32,36},... | collective-permute-start | bytes 1572872 | tf_op jit(solution)/shard_map/ppermute | solution.py:230
  81.2 12.2 %collective-permute-start.17 = (bf16[4,256,256]{2,1,0:T(8,128)(2,1)S(1)}, bf16[4,256,256]{2,1,0:T(8,128)(2,1)S(1)}, u32[]{:S(2)}, u32[]{:S(2)}) collective-permute-start(bf16[4,256,256]{2,1,0:T(8,128)(2,1)S(1)} %pad_maximum_fusion.own), channel_id=1, source_target_pairs={{0,124},{4,8},{8,4},{12,16},{16,12},{20,24},{24,20},{28,32},{32,28... | collective-permute-start | bytes 1572872 | tf_op jit(solution)/shard_map/ppermute | solution.py:234

commit v5 on v4

--- a/solution.py
+++ b/solution.py
@@ -42,7 +42,9 @@
     return [lon] + [lax.rem(lon + by + 4, 4) for by in (step, -step, 2)]
 
 
-def send_kernel(lists, grid, weights, out0, out1, out2, out3, rows_in, weight, table, picked, wanted, sems):
+def send_kernel(
+    lists, grid, weights, out0, out1, out2, out3, rows_in, weight, table, picked, wanted, staged, sems, out_sems
+):
     odd, _ = position()
     slots = 128
     parts = 4
@@ -68,7 +70,8 @@
         table[here] = dot(rows_in[here, :], weight[...]).reshape(size, 2, 128)
     for copy in fetch[1 + parts :]:
         copy.wait()
-    for k, out in enumerate((out0, out1, out2, out3)):
+    sent = []
+    for k, out in ((1, out1), (2, out2), (3, out3), (0, out0)):
         for part in range(3):
             base = (3 * k + part) * slots
 
@@ -78,7 +81,11 @@
                 for u in range(32):
                     picked[base + i * 32 + u] = rows[u]
 
-            out[part] = picked[base : base + slots].reshape(slots, 256).astype(bf16)
+            staged[k, part] = picked[base : base + slots].reshape(slots, 256).astype(bf16)
+        sent.append(pltpu.make_async_copy(staged.at[k], out, out_sems.at[k]))
+        sent[-1].start()
+    for copy in sent:
+        copy.wait()
 
 
 def lane_copies(row):
@@ -158,9 +165,10 @@
     sent_out[...] = dot(new, following[4 * (stage % STEPS)]).astype(bf16)
 
 
-def own_grid_kernel(sources, own, out):
+def own_grid_kernel(sources, own, latent, out, latent_out):
     width = own.shape[0]
     starts = received_starts(width)[0][:1]
+    latent_out[...] = latent[...]
 
     @pl.loop(0, out.shape[0] // EDGE_BLOCK)
     def _(j):
@@ -181,7 +189,7 @@
         out[here, :] = (before[here, :].astype(f32) + found).astype(bf16)
 
 
-def late_grid_kernel(sources, early, cross, grid, proj, gain, weights, out):
+def late_grid_kernel(sources, early, cross, grid, proj, gain, weights, out, staged, sems):
     width = cross.shape[1]
     cross_starts = received_starts(width)[2]
     table = cross[...].reshape(-1, 256)
@@ -198,7 +206,12 @@
             late = dot(pointers(sources[rows, :], cross_starts, width), table)
             hidden += silu(late + early[rows, :].astype(f32) + base)
         summed = dot(hidden.astype(bf16), weights[2])
-        out[here, :] = node_update(grid[here, :], summed, gains, weights[3]).astype(bf16)
+        staged[here, :] = node_update(grid[here, :], summed, gains, weights[3]).astype(bf16)
+        pltpu.make_async_copy(staged.at[here], out.at[here], sems.at[j]).start()
+
+    for j in range(count // GRID_BLOCK):
+        here = pl.ds(j * GRID_BLOCK, GRID_BLOCK)
+        pltpu.make_async_copy(staged.at[here], out.at[here], sems.at[j]).wait()
 
 
 def project_kernel(rows, weights, out):
@@ -209,11 +222,11 @@
     return jax.ShapeDtypeStruct(dims, dtype)
 
 
-def call(kernel, specs, outs, scratch, cost, limit=20):
+def call(kernel, specs, outs, scratch, cost, limit=20, out_space=VMEM):
     return pl.pallas_call(
         kernel,
         in_specs=specs,
-        out_specs=tuple(VMEM for _ in outs),
+        out_specs=tuple(out_space for _ in outs),
         out_shape=tuple(outs),
         scratch_shapes=scratch,
         compiler_params=pltpu.CompilerParams(vmem_limit_bytes=limit * 2**20),
@@ -294,10 +307,13 @@
             pltpu.VMEM((grid_count, 2, 128), f32),
             pltpu.VMEM((1536, 2, 128), f32),
             pltpu.SMEM((1536,), jnp.int32),
+            pltpu.VMEM((4, 3, 128, latent), bf16),
             pltpu.SemaphoreType.DMA((17,)),
+            pltpu.SemaphoreType.DMA((4,)),
         ],
         10**9,
         SEND_VMEM,
+        HBM,
     )(encode_sends, grid_latent, encode_weights)
     encode_lanes = edge_lanes(encode_sources, encode_targets)
     mesh_lanes = edge_lanes(mesh_sources, mesh_targets)
@@ -317,13 +333,13 @@
         around = jnp.stack([along(sent, 1), sent, along(sent, 2)])
         mesh_now, sent = edge_pass(halo_starts, step + 1, mesh_lanes, mesh_now, around, around, around)
     beside = [along(sent, k) for k in (1, 2, 3)]
-    (before,) = call(
+    before, mesh_out = call(
         own_grid_kernel,
-        [VMEM] * 2,
-        [shape(3 * grid_count, latent)],
+        [VMEM] * 3,
+        [shape(3 * grid_count, latent), shape(nodes, latent)],
         [],
         2 * 3 * grid_count * nodes * latent,
-    )(grid_lanes, sent)
+    )(grid_lanes, sent, mesh_now)
     band = jnp.stack([sent] + beside)
     band, before = lax.optimization_barrier((band, before))
     chip, cross = swap_chip(band), swap_cross(band)
@@ -338,10 +354,12 @@
         late_grid_kernel,
         [VMEM] * 7,
         [shape(grid_count, latent)],
-        [],
+        [pltpu.VMEM((grid_count, latent), bf16), pltpu.SemaphoreType.DMA((grid_count // GRID_BLOCK,))],
         10**9,
+        20,
+        HBM,
     )(grid_lanes, early, cross, grid_latent, grid_proj, norm_gains, decode_weights)
-    return grid_out, mesh_now
+    return grid_out, mesh_out
 
 
 def solution(mesh):

time: 100 us -> 100 us (level)
  transfers between devices with their start and end apart: 18 -> 18, of which waited for: 11 -> 11; matrix products, arithmetic and copies ran while one was open for 0% -> 0% of each run, Pallas kernels for 20% -> 21%
where the time goes in v5:
time: 100 us; the launch traced here: 99.8 us
  Pallas kernels  39.7 us (40%)
  waiting for transfers between devices  31.6 us (32%)
  starting transfers between devices  27 us (27%)
  between operations  1.18 us (1%)
    ppermute x10, waiting for transfers between devices, along(): return lax.ppermute(x, 'lon', list(enumerate(to)))  16.5 us
    ppermute x4, waiting for transfers between devices, swap_cross(): lax.ppermute(x, 'lat', [(i, (i + 1 ^ 1) - 1) if 0 < i < 31 else (i, 31 -...  15 us
    ppermute x4, starting transfers between devices, swap_cross(): lax.ppermute(x, 'lat', [(i, (i + 1 ^ 1) - 1) if 0 < i < 31 else (i, 31 -...  14.7 us
    ppermute x10, starting transfers between devices, along(): return lax.ppermute(x, 'lon', list(enumerate(to)))  12 us
    pallas_call x3, Pallas kernels, edge_pass(): call(partial(early_edges_kernel, starts, set_index), [VMEM] * 6, [shape(e...  7.11 us
    pallas_call x1, Pallas kernels, shards(): call(early_grid_kernel, [VMEM] * 4, [shape(3 * grid_count, latent)], [],...  6.91 us
    pallas_call x3, Pallas kernels, edge_pass(): call(partial(late_edges_kernel, starts, set_index, stage), [VMEM] * 8, [s...  6.85 us
    pallas_call x1, Pallas kernels, shards(): call(late_grid_kernel, [VMEM] * 7, [shape(grid_count, latent)], [pltpu.VM...  6.74 us
  transfers between devices with their start and end apart: 18, of which 11 were waited for; matrix products, arithmetic and copies ran while one was open for 0% of the time, Pallas kernels for 21%

profile of v5, /device:TPU:0, one launch (start us, length us, event | category | flops | bytes accessed | tf_op | source)
XLA Modules:
  0.0 99.8 jit_solution(259133569045433592)
XLA Ops:
  0.7 5.5 %shard_map.131 = (bf16[3,128,256]{2,1,0:T(8,128)(2,1)}, bf16[3,128,256]{2,1,0:T(8,128)(2,1)}, bf16[3,128,256]{2,1,0:T(8,128)(2,1)}, bf16[3,128,256]{2,1,0:T(8,128)(2,1)}) custom-call(s32[3,4,128]{2,1,0:T(4,128)} %lists.1, bf16[2048,256]{1,0:T(8,128)(2,1)} %grid.3, bf16[4,256,256]{2,1,0:T(8,128)(2,1)} %weights.12), custom_call_target="tpu_custom_call" | custom-call | flops 1000000000 | bytes 1048576 | tf_op jit(solution)/shard_map/pallas_call | solution.py:300
  6.2 1.7 %collective-permute-start = (bf16[3,128,256]{2,1,0:T(8,128)(2,1)}, bf16[3,128,256]{2,1,0:T(8,128)(2,1)S(1)}, u32[]{:S(2)}, u32[]{:S(2)}) collective-permute-start(bf16[3,128,256]{2,1,0:T(8,128)(2,1)} %get-tuple-element.33), channel_id=1, source_target_pairs={{0,1},{1,0},{2,3},{3,2},{4,5},{5,4},{6,7},{7,6},{8,9},{9,8},{10,11... | collective-permute-start | bytes 589832 | tf_op jit(solution)/shard_map/ppermute | solution.py:239
  7.9 2.2 %collective-permute-start.1 = (bf16[3,128,256]{2,1,0:T(8,128)(2,1)}, bf16[3,128,256]{2,1,0:T(8,128)(2,1)S(1)}, u32[]{:S(2)}, u32[]{:S(2)}) collective-permute-start(bf16[3,128,256]{2,1,0:T(8,128)(2,1)} %get-tuple-element.34), channel_id=1, source_target_pairs={{0,3},{1,2},{2,1},{3,0},{4,7},{5,6},{6,5},{7,4},{8,11},{9,10},{10,... | collective-permute-start | bytes 589832 | tf_op jit(solution)/shard_map/ppermute | solution.py:239
  10.1 0.7 collective-permute-start.2
  10.8 0.4 shard_map.135.proj
  11.3 0.0 copy-start.8
  11.3 0.0 copy-start.9
  11.3 0.9 shard_map.134.sources
  12.2 0.0 copy-start.6
  12.2 1.0 shard_map.133
  13.2 0.0 copy-start.10
  13.2 2.0 %shard_map.132 = (s16[4096,128]{1,0:T(8,128)(2,1)S(1)}, s16[4096,128]{1,0:T(8,128)(2,1)S(1)}, bf16[256,4096]{1,0:T(8,128)(2,1)S(1)}) custom-call(s32[32,128]{1,0:T(8,128)S(1)} %bitcast.18, s32[32,128]{1,0:T(8,128)S(1)} %bitcast.19), custom_call_target="tpu_custom_call" | custom-call | flops 1000000000 | bytes 1048576 | tf_op jit(solution)/shard_map/pallas_call | solution.py:269
  15.3 3.2 %collective-permute-done.1 = bf16[3,128,256]{2,1,0:T(8,128)(2,1)S(1)} collective-permute-done((bf16[3,128,256]{2,1,0:T(8,128)(2,1)}, bf16[3,128,256]{2,1,0:T(8,128)(2,1)S(1)}, u32[]{:S(2)}, u32[]{:S(2)}) %collective-permute-start.1) | collective-permute-done | bytes 196640 | tf_op jit(solution)/shard_map/ppermute | solution.py:239
  18.5 1.4 %collective-permute-done.2 = bf16[3,128,256]{2,1,0:T(8,128)(2,1)S(1)} collective-permute-done((bf16[3,128,256]{2,1,0:T(8,128)(2,1)}, bf16[3,128,256]{2,1,0:T(8,128)(2,1)S(1)}, u32[]{:S(2)}, u32[]{:S(2)}) %collective-permute-start.2) | collective-permute-done | bytes 196640 | tf_op jit(solution)/shard_map/ppermute | solution.py:239
  19.9 0.1 pad_maximum_fusion.3
  20.0 0.1 collective-permute-start.3
  20.1 6.3 %collective-permute-start.4 = (bf16[4,128,256]{2,1,0:T(8,128)(2,1)S(1)}, bf16[4,128,256]{2,1,0:T(8,128)(2,1)S(1)}, u32[]{:S(2)}, u32[]{:S(2)}) collective-permute-start(bf16[4,128,256]{2,1,0:T(8,128)(2,1)S(1)} %get-tuple-element.48), channel_id=1, source_target_pairs={{0,124},{4,8},{8,4},{12,16},{16,12},{20,24},{24,20},{28,32},{32,28... | collective-permute-start | bytes 786440 | tf_op jit(solution)/shard_map/ppermute | solution.py:247
  26.5 0.0 copy-start.5
  26.5 2.9 %shard_map.136.early = bf16[4096,256]{1,0:T(8,128)(2,1)S(1)} custom-call(s16[4096,128]{1,0:T(8,128)(2,1)S(1)} %get-tuple-element.45.sources, s16[4096,128]{1,0:T(8,128)(2,1)S(1)} %get-tuple-element.46.targets, bf16[4,128,256]{2,1,0:T(8,128)(2,1)S(1)} %pad_maximum_fusion.5.own, bf16[4,128,256]{2,1,0:T(8,128)(2,1)S(1)} %collective-permute-done.3.chip, ...), custom_call_target="tpu_custom_call" | custom-call | flops 2147483648 | bytes 1048576 | tf_op jit(solution)/shard_map/pallas_call | solution.py:285
  29.4 1.0 %collective-permute-done.4.cross = bf16[4,128,256]{2,1,0:T(8,128)(2,1)S(1)} collective-permute-done((bf16[4,128,256]{2,1,0:T(8,128)(2,1)S(1)}, bf16[4,128,256]{2,1,0:T(8,128)(2,1)S(1)}, u32[]{:S(2)}, u32[]{:S(2)}) %collective-permute-start.4) | collective-permute-done | bytes 262176 | tf_op jit(solution)/shard_map/ppermute | solution.py:247
  30.5 2.8 %shard_map.137 = (bf16[256,256]{1,0:T(8,128)(2,1)S(1)}, bf16[256,256]{1,0:T(8,128)(2,1)S(1)}) custom-call(s16[4096,128]{1,0:T(8,128)(2,1)S(1)} %get-tuple-element.45.sources, bf16[4096,256]{1,0:T(8,128)(2,1)S(1)} %shard_map.136.early, bf16[4,128,256]{2,1,0:T(8,128)(2,1)S(1)} %collective-permute-done.4.cross, ...), custom_call_target="tpu_custom_call" | custom-call | flops 1073741824 | bytes 1048576 | tf_op jit(solution)/shard_map/pallas_call | solution.py:292
  33.3 2.5 %collective-permute-start.6 = (bf16[256,256]{1,0:T(8,128)(2,1)S(1)}, bf16[256,256]{1,0:T(8,128)(2,1)S(1)}, u32[]{:S(2)}, u32[]{:S(2)}) collective-permute-start(bf16[256,256]{1,0:T(8,128)(2,1)S(1)} %get-tuple-element.50), channel_id=1, source_target_pairs={{0,3},{1,2},{2,1},{3,0},{4,7},{5,6},{6,5},{7,4},{8,11},{9,10},{10,... | collective-permute-start | bytes 393224 | tf_op jit(solution)/shard_map/ppermute | solution.py:239
  35.8 4.0 %collective-permute-done.6 = bf16[256,256]{1,0:T(8,128)(2,1)S(1)} collective-permute-done((bf16[256,256]{1,0:T(8,128)(2,1)S(1)}, bf16[256,256]{1,0:T(8,128)(2,1)S(1)}, u32[]{:S(2)}, u32[]{:S(2)}) %collective-permute-start.6) | collective-permute-done | bytes 131104 | tf_op jit(solution)/shard_map/ppermute | solution.py:239
  39.8 1.0 %collective-permute-done.5 = bf16[256,256]{1,0:T(8,128)(2,1)S(1)} collective-permute-done((bf16[256,256]{1,0:T(8,128)(2,1)S(1)}, bf16[256,256]{1,0:T(8,128)(2,1)S(1)}, u32[]{:S(2)}, u32[]{:S(2)}) %collective-permute-start.5) | collective-permute-done | bytes 131104 | tf_op jit(solution)/shard_map/ppermute | solution.py:239
  40.8 0.1 collective-permute-start.7
  40.9 3.7 %collective-permute-start.8 = (bf16[3,256,256]{2,1,0:T(8,128)(2,1)S(1)}, bf16[3,256,256]{2,1,0:T(8,128)(2,1)S(1)}, u32[]{:S(2)}, u32[]{:S(2)}) collective-permute-start(bf16[3,256,256]{2,1,0:T(8,128)(2,1)S(1)} %pad_maximum_fusion.1.own), channel_id=1, source_target_pairs={{0,124},{4,8},{8,4},{12,16},{16,12},{20,24},{24,20},{28,32},{32,28... | collective-permute-start | bytes 1179656 | tf_op jit(solution)/shard_map/ppermute | solution.py:247
  44.6 2.1 %shard_map.138.early = bf16[2048,256]{1,0:T(8,128)(2,1)S(1)} custom-call(s16[2048,128]{1,0:T(8,128)(2,1)S(1)} %get-tuple-element.43.sources, s16[2048,128]{1,0:T(8,128)(2,1)S(1)} %get-tuple-element.44.targets, bf16[3,256,256]{2,1,0:T(8,128)(2,1)S(1)} %pad_maximum_fusion.1.own, bf16[3,256,256]{2,1,0:T(8,128)(2,1)S(1)} %collective-permute-done.7.chip, ...), custom_call_target="tpu_custom_call" | custom-call | flops 1610612736 | bytes 1048576 | tf_op jit(solution)/shard_map/pallas_call | solution.py:285
  46.7 4.8 %collective-permute-done.8.cross = bf16[3,256,256]{2,1,0:T(8,128)(2,1)S(1)} collective-permute-done((bf16[3,256,256]{2,1,0:T(8,128)(2,1)S(1)}, bf16[3,256,256]{2,1,0:T(8,128)(2,1)S(1)}, u32[]{:S(2)}, u32[]{:S(2)}) %collective-permute-start.8) | collective-permute-done | bytes 393248 | tf_op jit(solution)/shard_map/ppermute | solution.py:247
  51.5 2.0 %shard_map.139 = (bf16[256,256]{1,0:T(8,128)(2,1)S(1)}, bf16[256,256]{1,0:T(8,128)(2,1)S(1)}) custom-call(s16[2048,128]{1,0:T(8,128)(2,1)S(1)} %get-tuple-element.43.sources, bf16[2048,256]{1,0:T(8,128)(2,1)S(1)} %shard_map.138.early, bf16[3,256,256]{2,1,0:T(8,128)(2,1)S(1)} %collective-permute-done.8.cross, ...), custom_call_target="tpu_custom_call" | custom-call | flops 805306368 | bytes 1048576 | tf_op jit(solution)/shard_map/pallas_call | solution.py:292
  53.5 1.3 %collective-permute-start.10 = (bf16[256,256]{1,0:T(8,128)(2,1)S(1)}, bf16[256,256]{1,0:T(8,128)(2,1)S(1)}, u32[]{:S(2)}, u32[]{:S(2)}) collective-permute-start(bf16[256,256]{1,0:T(8,128)(2,1)S(1)} %get-tuple-element.53), channel_id=1, source_target_pairs={{0,3},{1,2},{2,1},{3,0},{4,7},{5,6},{6,5},{7,4},{8,11},{9,10},{10,... | collective-permute-start | bytes 393224 | tf_op jit(solution)/shard_map/ppermute | solution.py:239
  54.8 5.0 %collective-permute-done.10 = bf16[256,256]{1,0:T(8,128)(2,1)S(1)} collective-permute-done((bf16[256,256]{1,0:T(8,128)(2,1)S(1)}, bf16[256,256]{1,0:T(8,128)(2,1)S(1)}, u32[]{:S(2)}, u32[]{:S(2)}) %collective-permute-start.10) | collective-permute-done | bytes 131104 | tf_op jit(solution)/shard_map/ppermute | solution.py:239
  59.8 0.1 collective-permute-start.11
  59.9 2.6 %collective-permute-start.12 = (bf16[3,256,256]{2,1,0:T(8,128)(2,1)S(1)}, bf16[3,256,256]{2,1,0:T(8,128)(2,1)S(1)}, u32[]{:S(2)}, u32[]{:S(2)}) collective-permute-start(bf16[3,256,256]{2,1,0:T(8,128)(2,1)S(1)} %pad_maximum_fusion.2.own), channel_id=1, source_target_pairs={{0,124},{4,8},{8,4},{12,16},{16,12},{20,24},{24,20},{28,32},{32,28... | collective-permute-start | bytes 1179656 | tf_op jit(solution)/shard_map/ppermute | solution.py:247
  62.5 2.1 %shard_map.140.early = bf16[2048,256]{1,0:T(8,128)(2,1)S(1)} custom-call(s16[2048,128]{1,0:T(8,128)(2,1)S(1)} %get-tuple-element.43.sources, s16[2048,128]{1,0:T(8,128)(2,1)S(1)} %get-tuple-element.44.targets, bf16[3,256,256]{2,1,0:T(8,128)(2,1)S(1)} %pad_maximum_fusion.2.own, bf16[3,256,256]{2,1,0:T(8,128)(2,1)S(1)} %collective-permute-done.11.chip, ...), custom_call_target="tpu_custom_call" | custom-call | flops 1610612736 | bytes 1048576 | tf_op jit(solution)/shard_map/pallas_call | solution.py:285
  64.6 5.9 %collective-permute-done.12.cross = bf16[3,256,256]{2,1,0:T(8,128)(2,1)S(1)} collective-permute-done((bf16[3,256,256]{2,1,0:T(8,128)(2,1)S(1)}, bf16[3,256,256]{2,1,0:T(8,128)(2,1)S(1)}, u32[]{:S(2)}, u32[]{:S(2)}) %collective-permute-start.12) | collective-permute-done | bytes 393248 | tf_op jit(solution)/shard_map/ppermute | solution.py:247
  70.5 2.0 %shard_map.141 = (bf16[256,256]{1,0:T(8,128)(2,1)S(1)}, bf16[256,256]{1,0:T(8,128)(2,1)S(1)}) custom-call(s16[2048,128]{1,0:T(8,128)(2,1)S(1)} %get-tuple-element.43.sources, bf16[2048,256]{1,0:T(8,128)(2,1)S(1)} %shard_map.140.early, bf16[3,256,256]{2,1,0:T(8,128)(2,1)S(1)} %collective-permute-done.12.cross, ...), custom_call_target="tpu_custom_call" | custom-call | flops 805306368 | bytes 1048576 | tf_op jit(solution)/shard_map/pallas_call | solution.py:292
  72.5 1.5 %collective-permute-start.15 = (bf16[256,256]{1,0:T(8,128)(2,1)S(1)}, bf16[256,256]{1,0:T(8,128)(2,1)S(1)}, u32[]{:S(2)}, u32[]{:S(2)}) collective-permute-start(bf16[256,256]{1,0:T(8,128)(2,1)S(1)} %get-tuple-element.55.own), channel_id=1, source_target_pairs={{0,2},{1,3},{2,0},{3,1},{4,6},{5,7},{6,4},{7,5},{8,10},{9,11},{10,... | collective-permute-start | bytes 393224 | tf_op jit(solution)/shard_map/ppermute | solution.py:239
  74.1 1.2 %collective-permute-start.14 = (bf16[256,256]{1,0:T(8,128)(2,1)S(1)}, bf16[256,256]{1,0:T(8,128)(2,1)S(1)}, u32[]{:S(2)}, u32[]{:S(2)}) collective-permute-start(bf16[256,256]{1,0:T(8,128)(2,1)S(1)} %get-tuple-element.55.own), channel_id=1, source_target_pairs={{0,3},{1,2},{2,1},{3,0},{4,7},{5,6},{6,5},{7,4},{8,11},{9,10},{10,... | collective-permute-start | bytes 393224 | tf_op jit(solution)/shard_map/ppermute | solution.py:239
  75.3 0.8 collective-permute-start.13
  76.1 2.4 %shard_map.142 = (bf16[6144,256]{1,0:T(8,128)(2,1)S(1)}, bf16[256,256]{1,0:T(8,128)(2,1)}) custom-call(s16[6144,128]{1,0:T(8,128)(2,1)S(1)} %shard_map.134.sources, bf16[256,256]{1,0:T(8,128)(2,1)S(1)} %get-tuple-element.55.own, bf16[256,256]{1,0:T(8,128)(2,1)S(1)} %get-tuple-element.56.latent), custom_call_target="tpu_custom_call" | custom-call | flops 805306368 | bytes 1048576 | tf_op jit(solution)/shard_map/pallas_call | solution.py:336
  78.5 0.7 collective-permute-done.15
  79.1 1.4 %collective-permute-done.14 = bf16[256,256]{1,0:T(8,128)(2,1)S(1)} collective-permute-done((bf16[256,256]{1,0:T(8,128)(2,1)S(1)}, bf16[256,256]{1,0:T(8,128)(2,1)S(1)}, u32[]{:S(2)}, u32[]{:S(2)}) %collective-permute-start.14) | collective-permute-done | bytes 131104 | tf_op jit(solution)/shard_map/ppermute | solution.py:239
  80.5 0.1 pad_maximum_fusion.own
  80.6 0.1 collective-permute-start.16
  80.7 2.0 %collective-permute-start.17 = (bf16[4,256,256]{2,1,0:T(8,128)(2,1)S(1)}, bf16[4,256,256]{2,1,0:T(8,128)(2,1)S(1)}, u32[]{:S(2)}, u32[]{:S(2)}) collective-permute-start(bf16[4,256,256]{2,1,0:T(8,128)(2,1)S(1)} %pad_maximum_fusion.own), channel_id=1, source_target_pairs={{0,124},{4,8},{8,4},{12,16},{16,12},{20,24},{24,20},{28,32},{32,28... | collective-permute-start | bytes 1572872 | tf_op jit(solution)/shard_map/ppermute | solution.py:247
  82.7 6.9 %shard_map.143.early = bf16[6144,256]{1,0:T(8,128)(2,1)S(1)} custom-call(s16[6144,128]{1,0:T(8,128)(2,1)S(1)} %shard_map.134.sources, bf16[6144,256]{1,0:T(8,128)(2,1)S(1)} %get-tuple-element.58.before, bf16[4,256,256]{2,1,0:T(8,128)(2,1)S(1)} %pad_maximum_fusion.own, bf16[4,256,256]{2,1,0:T(8,128)(2,1)S(1)} %collective-permute-done.16.chip), custom_call_target="tpu_custom_call" | custom-call | flops 5637144576 | bytes 1048576 | tf_op jit(solution)/shard_map/pallas_call | solution.py:346
  89.6 3.3 %collective-permute-done.17.cross = bf16[4,256,256]{2,1,0:T(8,128)(2,1)S(1)} collective-permute-done((bf16[4,256,256]{2,1,0:T(8,128)(2,1)S(1)}, bf16[4,256,256]{2,1,0:T(8,128)(2,1)S(1)}, u32[]{:S(2)}, u32[]{:S(2)}) %collective-permute-start.17) | collective-permute-done | bytes 524320 | tf_op jit(solution)/shard_map/ppermute | solution.py:247
  92.9 6.7 %shard_map.144 = bf16[2048,256]{1,0:T(8,128)(2,1)} custom-call(s16[6144,128]{1,0:T(8,128)(2,1)S(1)} %shard_map.134.sources, bf16[6144,256]{1,0:T(8,128)(2,1)S(1)} %shard_map.143.early, bf16[4,256,256]{2,1,0:T(8,128)(2,1)S(1)} %collective-permute-done.17.cross, bf16[2048,256]{1,0:T(8,128)(2,1)S(1)} %copy-done.2, bf16[2048,256]{1,0:T(8,128)(2,1)S(1)} %shard_map.135.proj, ...), custom_call_target="tpu_custom_call" | custom-call | flops 1000000000 | bytes 1048576 | tf_op jit(solution)/shard_map/pallas_call | solution.py:353
  (36 shorter events, 0.3 us)
Async XLA Ops:
  0.6 10.2 %copy-start.2 = (bf16[2048,256]{1,0:T(8,128)(2,1)S(1)}, bf16[2048,256]{1,0:T(8,128)(2,1)}, u32[]{:S(2)}) copy-start(bf16[2048,256]{1,0:T(8,128)(2,1)} %grid.3) | copy-start | bytes 3145732
  0.6 10.2 %copy-start.11 = (s32[2048,3]{0,1:T(4,128)S(1)}, s32[2048,3]{0,1:T(4,128)}, u32[]{:S(2)}) copy-start(s32[2048,3]{0,1:T(4,128)} %param.19) | copy-start | bytes 73732
  0.7 10.2 %copy-start.1 = (bf16[4,256,256]{2,1,0:T(8,128)(2,1)S(1)}, bf16[4,256,256]{2,1,0:T(8,128)(2,1)}, u32[]{:S(2)}) copy-start(bf16[4,256,256]{2,1,0:T(8,128)(2,1)} %weights.17) | copy-start | bytes 1572868
  6.2 9.1 %collective-permute-start = (bf16[3,128,256]{2,1,0:T(8,128)(2,1)}, bf16[3,128,256]{2,1,0:T(8,128)(2,1)S(1)}, u32[]{:S(2)}, u32[]{:S(2)}) collective-permute-start(bf16[3,128,256]{2,1,0:T(8,128)(2,1)} %get-tuple-element.33), channel_id=1, source_target_pairs={{0,1},{1,0},{2,3},{3,2},{4,5},{5,4},{6,7},{7,6},{8,9},{9,8},{10,11... | collective-permute-start | bytes 589832 | tf_op jit(solution)/shard_map/ppermute | solution.py:239
  7.9 10.6 %collective-permute-start.1 = (bf16[3,128,256]{2,1,0:T(8,128)(2,1)}, bf16[3,128,256]{2,1,0:T(8,128)(2,1)S(1)}, u32[]{:S(2)}, u32[]{:S(2)}) collective-permute-start(bf16[3,128,256]{2,1,0:T(8,128)(2,1)} %get-tuple-element.34), channel_id=1, source_target_pairs={{0,3},{1,2},{2,1},{3,0},{4,7},{5,6},{6,5},{7,4},{8,11},{9,10},{10,... | collective-permute-start | bytes 589832 | tf_op jit(solution)/shard_map/ppermute | solution.py:239
  10.1 9.8 %collective-permute-start.2 = (bf16[3,128,256]{2,1,0:T(8,128)(2,1)}, bf16[3,128,256]{2,1,0:T(8,128)(2,1)S(1)}, u32[]{:S(2)}, u32[]{:S(2)}) collective-permute-start(bf16[3,128,256]{2,1,0:T(8,128)(2,1)} %get-tuple-element.35), channel_id=1, source_target_pairs={{0,2},{1,3},{2,0},{3,1},{4,6},{5,7},{6,4},{7,5},{8,10},{9,11},{10,... | collective-permute-start | bytes 589832 | tf_op jit(solution)/shard_map/ppermute | solution.py:239
  11.3 0.9 copy-start.8
  11.3 0.9 copy-start.9
  12.2 1.0 %copy-start.6 = (s32[4096]{0:T(1024)S(1)}, s32[4096]{0:T(1024)}, u32[]{:S(2)}) copy-start(s32[4096]{0:T(1024)} %param.15) | copy-start | bytes 49156
  12.2 1.0 %copy-start.7 = (s32[4096]{0:T(1024)S(1)}, s32[4096]{0:T(1024)}, u32[]{:S(2)}) copy-start(s32[4096]{0:T(1024)} %param.16) | copy-start | bytes 49156
  13.2 2.0 %copy-start.10 = (bf16[3,128,256]{2,1,0:T(8,128)(2,1)S(1)}, bf16[3,128,256]{2,1,0:T(8,128)(2,1)}, u32[]{:S(2)}) copy-start(bf16[3,128,256]{2,1,0:T(8,128)(2,1)} %get-tuple-element.32) | copy-start | bytes 589828
  15.2 11.3 %copy-start.3 = (bf16[4,256,256]{2,1,0:T(8,128)(2,1)S(1)}, bf16[4,256,256]{2,1,0:T(8,128)(2,1)}, u32[]{:S(2)}) copy-start(bf16[4,256,256]{2,1,0:T(8,128)(2,1)} %weights.12) | copy-start | bytes 1572868
  15.2 11.3 %copy-start.4 = (bf16[256,256]{1,0:T(8,128)(2,1)S(1)}, bf16[256,256]{1,0:T(8,128)(2,1)}, u32[]{:S(2)}) copy-start(bf16[256,256]{1,0:T(8,128)(2,1)} %latent.3) | copy-start | bytes 393220
  20.0 6.5 %collective-permute-start.3 = (bf16[4,128,256]{2,1,0:T(8,128)(2,1)S(1)}, bf16[4,128,256]{2,1,0:T(8,128)(2,1)S(1)}, u32[]{:S(2)}, u32[]{:S(2)}) collective-permute-start(bf16[4,128,256]{2,1,0:T(8,128)(2,1)S(1)} %get-tuple-element.47), channel_id=1, source_target_pairs={{0,4},{4,0},{8,12},{12,8},{16,20},{20,16},{24,28},{28,24},{32,36},... | collective-permute-start | bytes 786440 | tf_op jit(solution)/shard_map/ppermute | solution.py:243
  20.1 10.4 %collective-permute-start.4 = (bf16[4,128,256]{2,1,0:T(8,128)(2,1)S(1)}, bf16[4,128,256]{2,1,0:T(8,128)(2,1)S(1)}, u32[]{:S(2)}, u32[]{:S(2)}) collective-permute-start(bf16[4,128,256]{2,1,0:T(8,128)(2,1)S(1)} %get-tuple-element.48), channel_id=1, source_target_pairs={{0,124},{4,8},{8,4},{12,16},{16,12},{20,24},{24,20},{28,32},{32,28... | collective-permute-start | bytes 786440 | tf_op jit(solution)/shard_map/ppermute | solution.py:247
  26.5 4.0 %copy-start = (bf16[8,256,256]{2,1,0:T(8,128)(2,1)S(1)}, bf16[8,256,256]{2,1,0:T(8,128)(2,1)}, u32[]{:S(2)}) copy-start(bf16[8,256,256]{2,1,0:T(8,128)(2,1)} %weights.16) | copy-start | bytes 3145732
  26.5 4.0 %copy-start.5 = (bf16[4,256]{1,0:T(4,128)(2,1)S(1)}, bf16[4,256]{1,0:T(4,128)(2,1)}, u32[]{:S(2)}) copy-start(bf16[4,256]{1,0:T(4,128)(2,1)} %gain.1) | copy-start | bytes 6148
  33.3 6.4 %collective-permute-start.6 = (bf16[256,256]{1,0:T(8,128)(2,1)S(1)}, bf16[256,256]{1,0:T(8,128)(2,1)S(1)}, u32[]{:S(2)}, u32[]{:S(2)}) collective-permute-start(bf16[256,256]{1,0:T(8,128)(2,1)S(1)} %get-tuple-element.50), channel_id=1, source_target_pairs={{0,3},{1,2},{2,1},{3,0},{4,7},{5,6},{6,5},{7,4},{8,11},{9,10},{10,... | collective-permute-start | bytes 393224 | tf_op jit(solution)/shard_map/ppermute | solution.py:239
  35.8 5.0 %collective-permute-start.5 = (bf16[256,256]{1,0:T(8,128)(2,1)S(1)}, bf16[256,256]{1,0:T(8,128)(2,1)S(1)}, u32[]{:S(2)}, u32[]{:S(2)}) collective-permute-start(bf16[256,256]{1,0:T(8,128)(2,1)S(1)} %get-tuple-element.50), channel_id=1, source_target_pairs={{0,1},{1,0},{2,3},{3,2},{4,5},{5,4},{6,7},{7,6},{8,9},{9,8},{10,11... | collective-permute-start | bytes 393224 | tf_op jit(solution)/shard_map/ppermute | solution.py:239
  40.8 3.8 %collective-permute-start.7 = (bf16[3,256,256]{2,1,0:T(8,128)(2,1)S(1)}, bf16[3,256,256]{2,1,0:T(8,128)(2,1)S(1)}, u32[]{:S(2)}, u32[]{:S(2)}) collective-permute-start(bf16[3,256,256]{2,1,0:T(8,128)(2,1)S(1)} %pad_maximum_fusion.1.own), channel_id=1, source_target_pairs={{0,4},{4,0},{8,12},{12,8},{16,20},{20,16},{24,28},{28,24},{32,36},... | collective-permute-start | bytes 1179656 | tf_op jit(solution)/shard_map/ppermute | solution.py:243
  40.9 10.6 %collective-permute-start.8 = (bf16[3,256,256]{2,1,0:T(8,128)(2,1)S(1)}, bf16[3,256,256]{2,1,0:T(8,128)(2,1)S(1)}, u32[]{:S(2)}, u32[]{:S(2)}) collective-permute-start(bf16[3,256,256]{2,1,0:T(8,128)(2,1)S(1)} %pad_maximum_fusion.1.own), channel_id=1, source_target_pairs={{0,124},{4,8},{8,4},{12,16},{16,12},{20,24},{24,20},{28,32},{32,28... | collective-permute-start | bytes 1179656 | tf_op jit(solution)/shard_map/ppermute | solution.py:247
  53.5 6.3 %collective-permute-start.10 = (bf16[256,256]{1,0:T(8,128)(2,1)S(1)}, bf16[256,256]{1,0:T(8,128)(2,1)S(1)}, u32[]{:S(2)}, u32[]{:S(2)}) collective-permute-start(bf16[256,256]{1,0:T(8,128)(2,1)S(1)} %get-tuple-element.53), channel_id=1, source_target_pairs={{0,3},{1,2},{2,1},{3,0},{4,7},{5,6},{6,5},{7,4},{8,11},{9,10},{10,... | collective-permute-start | bytes 393224 | tf_op jit(solution)/shard_map/ppermute | solution.py:239
  54.8 5.0 %collective-permute-start.9 = (bf16[256,256]{1,0:T(8,128)(2,1)S(1)}, bf16[256,256]{1,0:T(8,128)(2,1)S(1)}, u32[]{:S(2)}, u32[]{:S(2)}) collective-permute-start(bf16[256,256]{1,0:T(8,128)(2,1)S(1)} %get-tuple-element.53), channel_id=1, source_target_pairs={{0,1},{1,0},{2,3},{3,2},{4,5},{5,4},{6,7},{7,6},{8,9},{9,8},{10,11... | collective-permute-start | bytes 393224 | tf_op jit(solution)/shard_map/ppermute | solution.py:239
  59.8 2.7 %collective-permute-start.11 = (bf16[3,256,256]{2,1,0:T(8,128)(2,1)S(1)}, bf16[3,256,256]{2,1,0:T(8,128)(2,1)S(1)}, u32[]{:S(2)}, u32[]{:S(2)}) collective-permute-start(bf16[3,256,256]{2,1,0:T(8,128)(2,1)S(1)} %pad_maximum_fusion.2.own), channel_id=1, source_target_pairs={{0,4},{4,0},{8,12},{12,8},{16,20},{20,16},{24,28},{28,24},{32,36},... | collective-permute-start | bytes 1179656 | tf_op jit(solution)/shard_map/ppermute | solution.py:243
  59.9 10.6 %collective-permute-start.12 = (bf16[3,256,256]{2,1,0:T(8,128)(2,1)S(1)}, bf16[3,256,256]{2,1,0:T(8,128)(2,1)S(1)}, u32[]{:S(2)}, u32[]{:S(2)}) collective-permute-start(bf16[3,256,256]{2,1,0:T(8,128)(2,1)S(1)} %pad_maximum_fusion.2.own), channel_id=1, source_target_pairs={{0,124},{4,8},{8,4},{12,16},{16,12},{20,24},{24,20},{28,32},{32,28... | collective-permute-start | bytes 1179656 | tf_op jit(solution)/shard_map/ppermute | solution.py:247
  72.5 6.6 %collective-permute-start.15 = (bf16[256,256]{1,0:T(8,128)(2,1)S(1)}, bf16[256,256]{1,0:T(8,128)(2,1)S(1)}, u32[]{:S(2)}, u32[]{:S(2)}) collective-permute-start(bf16[256,256]{1,0:T(8,128)(2,1)S(1)} %get-tuple-element.55.own), channel_id=1, source_target_pairs={{0,2},{1,3},{2,0},{3,1},{4,6},{5,7},{6,4},{7,5},{8,10},{9,11},{10,... | collective-permute-start | bytes 393224 | tf_op jit(solution)/shard_map/ppermute | solution.py:239
  74.1 6.4 %collective-permute-start.14 = (bf16[256,256]{1,0:T(8,128)(2,1)S(1)}, bf16[256,256]{1,0:T(8,128)(2,1)S(1)}, u32[]{:S(2)}, u32[]{:S(2)}) collective-permute-start(bf16[256,256]{1,0:T(8,128)(2,1)S(1)} %get-tuple-element.55.own), channel_id=1, source_target_pairs={{0,3},{1,2},{2,1},{3,0},{4,7},{5,6},{6,5},{7,4},{8,11},{9,10},{10,... | collective-permute-start | bytes 393224 | tf_op jit(solution)/shard_map/ppermute | solution.py:239
  75.3 5.2 %collective-permute-start.13 = (bf16[256,256]{1,0:T(8,128)(2,1)S(1)}, bf16[256,256]{1,0:T(8,128)(2,1)S(1)}, u32[]{:S(2)}, u32[]{:S(2)}) collective-permute-start(bf16[256,256]{1,0:T(8,128)(2,1)S(1)} %get-tuple-element.55.own), channel_id=1, source_target_pairs={{0,1},{1,0},{2,3},{3,2},{4,5},{5,4},{6,7},{7,6},{8,9},{9,8},{10,11... | collective-permute-start | bytes 393224 | tf_op jit(solution)/shard_map/ppermute | solution.py:239
  80.6 2.1 %collective-permute-start.16 = (bf16[4,256,256]{2,1,0:T(8,128)(2,1)S(1)}, bf16[4,256,256]{2,1,0:T(8,128)(2,1)S(1)}, u32[]{:S(2)}, u32[]{:S(2)}) collective-permute-start(bf16[4,256,256]{2,1,0:T(8,128)(2,1)S(1)} %pad_maximum_fusion.own), channel_id=1, source_target_pairs={{0,4},{4,0},{8,12},{12,8},{16,20},{20,16},{24,28},{28,24},{32,36},... | collective-permute-start | bytes 1572872 | tf_op jit(solution)/shard_map/ppermute | solution.py:243
  80.7 12.2 %collective-permute-start.17 = (bf16[4,256,256]{2,1,0:T(8,128)(2,1)S(1)}, bf16[4,256,256]{2,1,0:T(8,128)(2,1)S(1)}, u32[]{:S(2)}, u32[]{:S(2)}) collective-permute-start(bf16[4,256,256]{2,1,0:T(8,128)(2,1)S(1)} %pad_maximum_fusion.own), channel_id=1, source_target_pairs={{0,124},{4,8},{8,4},{12,16},{16,12},{20,24},{24,20},{28,32},{32,28... | collective-permute-start | bytes 1572872 | tf_op jit(solution)/shard_map/ppermute | solution.py:247

commit v6 on v5

--- a/solution.py
+++ b/solution.py
@@ -75,11 +75,10 @@
         for part in range(3):
             base = (3 * k + part) * slots
 
-            @pl.loop(0, slots // 32)
-            def _(i):
-                rows = [table[wanted[base + i * 32 + u]] for u in range(32)]
+            for first in range(base, base + slots, 32):
+                rows = [table[wanted[first + u]] for u in range(32)]
                 for u in range(32):
-                    picked[base + i * 32 + u] = rows[u]
+                    picked[first + u] = rows[u]
 
             staged[k, part] = picked[base : base + slots].reshape(slots, 256).astype(bf16)
         sent.append(pltpu.make_async_copy(staged.at[k], out, out_sems.at[k]))
@@ -165,7 +164,7 @@
     sent_out[...] = dot(new, following[4 * (stage % STEPS)]).astype(bf16)
 
 
-def own_grid_kernel(sources, own, latent, out, latent_out):
+def own_grid_kernel(sources, own, proj, latent, out, latent_out):
     width = own.shape[0]
     starts = received_starts(width)[0][:1]
     latent_out[...] = latent[...]
@@ -173,7 +172,9 @@
     @pl.loop(0, out.shape[0] // EDGE_BLOCK)
     def _(j):
         here = pl.ds(pl.multiple_of(j * EDGE_BLOCK, EDGE_BLOCK), EDGE_BLOCK)
-        out[here, :] = dot(pointers(sources[here, :], starts, width), own[...]).astype(bf16)
+        first = lax.rem(j, proj.shape[0] // EDGE_BLOCK) * EDGE_BLOCK
+        base = proj[pl.ds(pl.multiple_of(first, EDGE_BLOCK), EDGE_BLOCK), :].astype(f32)
+        out[here, :] = (base + dot(pointers(sources[here, :], starts, width), own[...])).astype(bf16)
 
 
 def early_grid_kernel(sources, before, own, chip, out):
@@ -189,7 +190,7 @@
         out[here, :] = (before[here, :].astype(f32) + found).astype(bf16)
 
 
-def late_grid_kernel(sources, early, cross, grid, proj, gain, weights, out, staged, sems):
+def late_grid_kernel(sources, early, cross, grid, gain, weights, out, staged, sems):
     width = cross.shape[1]
     cross_starts = received_starts(width)[2]
     table = cross[...].reshape(-1, 256)
@@ -199,12 +200,11 @@
     def _(j):
         first = pl.multiple_of(j * GRID_BLOCK, GRID_BLOCK)
         here = pl.ds(first, GRID_BLOCK)
-        base = proj[here, :].astype(f32)
         hidden = jnp.zeros((GRID_BLOCK, 256), f32)
         for k in range(3):
             rows = pl.ds(pl.multiple_of(k * count + first, GRID_BLOCK), GRID_BLOCK)
             late = dot(pointers(sources[rows, :], cross_starts, width), table)
-            hidden += silu(late + early[rows, :].astype(f32) + base)
+            hidden += silu(late + early[rows, :].astype(f32))
         summed = dot(hidden.astype(bf16), weights[2])
         staged[here, :] = node_update(grid[here, :], summed, gains, weights[3]).astype(bf16)
         pltpu.make_async_copy(staged.at[here], out.at[here], sems.at[j]).start()
@@ -335,11 +335,11 @@
     beside = [along(sent, k) for k in (1, 2, 3)]
     before, mesh_out = call(
         own_grid_kernel,
-        [VMEM] * 3,
+        [VMEM] * 4,
         [shape(3 * grid_count, latent), shape(nodes, latent)],
         [],
         2 * 3 * grid_count * nodes * latent,
-    )(grid_lanes, sent, mesh_now)
+    )(grid_lanes, sent, grid_proj, mesh_now)
     band = jnp.stack([sent] + beside)
     band, before = lax.optimization_barrier((band, before))
     chip, cross = swap_chip(band), swap_cross(band)
@@ -352,13 +352,13 @@
     )(grid_lanes, before, band, chip)
     (grid_out,) = call(
         late_grid_kernel,
-        [VMEM] * 7,
+        [VMEM] * 6,
         [shape(grid_count, latent)],
         [pltpu.VMEM((grid_count, latent), bf16), pltpu.SemaphoreType.DMA((grid_count // GRID_BLOCK,))],
         10**9,
         20,
         HBM,
-    )(grid_lanes, early, cross, grid_latent, grid_proj, norm_gains, decode_weights)
+    )(grid_lanes, early, cross, grid_latent, norm_gains, decode_weights)
     return grid_out, mesh_out
 
 

time: 100 us -> 98.6 us (0.986)
  Pallas kernels: 39.7 us -> 38.5 us
  waiting for transfers between devices: 31.6 us -> 30.6 us
  transfers between devices with their start and end apart: 18 -> 18, of which waited for: 11 -> 11; matrix products, arithmetic and copies ran while one was open for 0% -> 1% of each run, Pallas kernels for 21% -> 21%
where the time goes in v6:
time: 98.6 us; the launch traced here: 98.5 us
  Pallas kernels  38.5 us (39%)
  waiting for transfers between devices  30.6 us (31%)
  starting transfers between devices  26.8 us (27%)
  between operations  1.17 us (1%)
  local copies, waits for them, and re-layouts  1.1 us (1%)
    ppermute x10, waiting for transfers between devices, along(): return lax.ppermute(x, 'lon', list(enumerate(to)))  15.6 us
    ppermute x4, waiting for transfers between devices, swap_cross(): lax.ppermute(x, 'lat', [(i, (i + 1 ^ 1) - 1) if 0 < i < 31 else (i, 31 -...  14.9 us
    ppermute x4, starting transfers between devices, swap_cross(): lax.ppermute(x, 'lat', [(i, (i + 1 ^ 1) - 1) if 0 < i < 31 else (i, 31 -...  14.7 us
    ppermute x10, starting transfers between devices, along(): return lax.ppermute(x, 'lon', list(enumerate(to)))  11.8 us
    pallas_call x3, Pallas kernels, edge_pass(): call(partial(early_edges_kernel, starts, set_index), [VMEM] * 6, [shape(e...  7.11 us
    pallas_call x1, Pallas kernels, shards(): call(early_grid_kernel, [VMEM] * 4, [shape(3 * grid_count, latent)], [],...  6.92 us
    pallas_call x3, Pallas kernels, edge_pass(): call(partial(late_edges_kernel, starts, set_index, stage), [VMEM] * 8, [s...  6.85 us
    pallas_call x1, Pallas kernels, shards(): call(late_grid_kernel, [VMEM] * 6, [shape(grid_count, latent)], [pltpu.VM...  6.52 us
  transfers between devices with their start and end apart: 18, of which 11 were waited for; matrix products, arithmetic and copies ran while one was open for 1% of the time, Pallas kernels for 21%

profile of v6, /device:TPU:0, one launch (start us, length us, event | category | flops | bytes accessed | tf_op | source)
XLA Modules:
  0.0 98.5 jit_solution(7641590702520249993)
XLA Ops:
  0.7 4.5 %shard_map.131 = (bf16[3,128,256]{2,1,0:T(8,128)(2,1)}, bf16[3,128,256]{2,1,0:T(8,128)(2,1)}, bf16[3,128,256]{2,1,0:T(8,128)(2,1)}, bf16[3,128,256]{2,1,0:T(8,128)(2,1)}) custom-call(s32[3,4,128]{2,1,0:T(4,128)} %lists.1, bf16[2048,256]{1,0:T(8,128)(2,1)} %grid.3, bf16[4,256,256]{2,1,0:T(8,128)(2,1)} %weights.12), custom_call_target="tpu_custom_call" | custom-call | flops 1000000000 | bytes 1048576 | tf_op jit(solution)/shard_map/pallas_call | solution.py:300
  5.2 1.7 %collective-permute-start = (bf16[3,128,256]{2,1,0:T(8,128)(2,1)}, bf16[3,128,256]{2,1,0:T(8,128)(2,1)}, u32[]{:S(2)}, u32[]{:S(2)}) collective-permute-start(bf16[3,128,256]{2,1,0:T(8,128)(2,1)} %get-tuple-element.33), channel_id=1, source_target_pairs={{0,1},{1,0},{2,3},{3,2},{4,5},{5,4},{6,7},{7,6},{8,9},{9,8},{10,11... | collective-permute-start | bytes 589832 | tf_op jit(solution)/shard_map/ppermute | solution.py:239
  6.9 2.2 %collective-permute-start.1 = (bf16[3,128,256]{2,1,0:T(8,128)(2,1)}, bf16[3,128,256]{2,1,0:T(8,128)(2,1)S(1)}, u32[]{:S(2)}, u32[]{:S(2)}) collective-permute-start(bf16[3,128,256]{2,1,0:T(8,128)(2,1)} %get-tuple-element.34), channel_id=1, source_target_pairs={{0,3},{1,2},{2,1},{3,0},{4,7},{5,6},{6,5},{7,4},{8,11},{9,10},{10,... | collective-permute-start | bytes 589832 | tf_op jit(solution)/shard_map/ppermute | solution.py:239
  9.1 0.7 collective-permute-start.2
  9.9 0.4 shard_map.135.proj
  10.3 0.0 copy-start.9
  10.4 0.9 shard_map.134.sources
  11.2 0.0 copy-start.6
  11.3 1.0 shard_map.133
  12.3 2.0 %shard_map.132 = (s16[4096,128]{1,0:T(8,128)(2,1)S(1)}, s16[4096,128]{1,0:T(8,128)(2,1)S(1)}, bf16[256,4096]{1,0:T(8,128)(2,1)S(1)}) custom-call(s32[32,128]{1,0:T(8,128)S(1)} %bitcast.18, s32[32,128]{1,0:T(8,128)S(1)} %bitcast.19), custom_call_target="tpu_custom_call" | custom-call | flops 1000000000 | bytes 1048576 | tf_op jit(solution)/shard_map/pallas_call | solution.py:269
  14.2 0.0 copy-start.3
  14.3 1.0 fusion.1
  15.3 2.2 %collective-permute-done.1 = bf16[3,128,256]{2,1,0:T(8,128)(2,1)S(1)} collective-permute-done((bf16[3,128,256]{2,1,0:T(8,128)(2,1)}, bf16[3,128,256]{2,1,0:T(8,128)(2,1)S(1)}, u32[]{:S(2)}, u32[]{:S(2)}) %collective-permute-start.1) | collective-permute-done | bytes 196640 | tf_op jit(solution)/shard_map/ppermute | solution.py:239
  17.5 1.4 %collective-permute-done.2 = bf16[3,128,256]{2,1,0:T(8,128)(2,1)S(1)} collective-permute-done((bf16[3,128,256]{2,1,0:T(8,128)(2,1)}, bf16[3,128,256]{2,1,0:T(8,128)(2,1)S(1)}, u32[]{:S(2)}, u32[]{:S(2)}) %collective-permute-start.2) | collective-permute-done | bytes 196640 | tf_op jit(solution)/shard_map/ppermute | solution.py:239
  19.0 0.1 pad_maximum_fusion.3
  19.0 0.1 collective-permute-start.3
  19.1 6.3 %collective-permute-start.4 = (bf16[4,128,256]{2,1,0:T(8,128)(2,1)S(1)}, bf16[4,128,256]{2,1,0:T(8,128)(2,1)S(1)}, u32[]{:S(2)}, u32[]{:S(2)}) collective-permute-start(bf16[4,128,256]{2,1,0:T(8,128)(2,1)S(1)} %get-tuple-element.48), channel_id=1, source_target_pairs={{0,124},{4,8},{8,4},{12,16},{16,12},{20,24},{24,20},{28,32},{32,28... | collective-permute-start | bytes 786440 | tf_op jit(solution)/shard_map/ppermute | solution.py:247
  25.6 2.9 %shard_map.136.early = bf16[4096,256]{1,0:T(8,128)(2,1)S(1)} custom-call(s16[4096,128]{1,0:T(8,128)(2,1)S(1)} %get-tuple-element.45.sources, s16[4096,128]{1,0:T(8,128)(2,1)S(1)} %get-tuple-element.46.targets, bf16[4,128,256]{2,1,0:T(8,128)(2,1)S(1)} %pad_maximum_fusion.5.own, bf16[4,128,256]{2,1,0:T(8,128)(2,1)S(1)} %collective-permute-done.3.chip, ...), custom_call_target="tpu_custom_call" | custom-call | flops 2147483648 | bytes 1048576 | tf_op jit(solution)/shard_map/pallas_call | solution.py:285
  28.5 1.0 %collective-permute-done.4.cross = bf16[4,128,256]{2,1,0:T(8,128)(2,1)S(1)} collective-permute-done((bf16[4,128,256]{2,1,0:T(8,128)(2,1)S(1)}, bf16[4,128,256]{2,1,0:T(8,128)(2,1)S(1)}, u32[]{:S(2)}, u32[]{:S(2)}) %collective-permute-start.4) | collective-permute-done | bytes 262176 | tf_op jit(solution)/shard_map/ppermute | solution.py:247
  29.5 2.8 %shard_map.137 = (bf16[256,256]{1,0:T(8,128)(2,1)S(1)}, bf16[256,256]{1,0:T(8,128)(2,1)S(1)}) custom-call(s16[4096,128]{1,0:T(8,128)(2,1)S(1)} %get-tuple-element.45.sources, bf16[4096,256]{1,0:T(8,128)(2,1)S(1)} %shard_map.136.early, bf16[4,128,256]{2,1,0:T(8,128)(2,1)S(1)} %collective-permute-done.4.cross, ...), custom_call_target="tpu_custom_call" | custom-call | flops 1073741824 | bytes 1048576 | tf_op jit(solution)/shard_map/pallas_call | solution.py:292
  32.4 2.3 %collective-permute-start.6 = (bf16[256,256]{1,0:T(8,128)(2,1)S(1)}, bf16[256,256]{1,0:T(8,128)(2,1)S(1)}, u32[]{:S(2)}, u32[]{:S(2)}) collective-permute-start(bf16[256,256]{1,0:T(8,128)(2,1)S(1)} %get-tuple-element.50), channel_id=1, source_target_pairs={{0,3},{1,2},{2,1},{3,0},{4,7},{5,6},{6,5},{7,4},{8,11},{9,10},{10,... | collective-permute-start | bytes 393224 | tf_op jit(solution)/shard_map/ppermute | solution.py:239
  34.7 4.0 %collective-permute-done.6 = bf16[256,256]{1,0:T(8,128)(2,1)S(1)} collective-permute-done((bf16[256,256]{1,0:T(8,128)(2,1)S(1)}, bf16[256,256]{1,0:T(8,128)(2,1)S(1)}, u32[]{:S(2)}, u32[]{:S(2)}) %collective-permute-start.6) | collective-permute-done | bytes 131104 | tf_op jit(solution)/shard_map/ppermute | solution.py:239
  38.6 1.0 %collective-permute-done.5 = bf16[256,256]{1,0:T(8,128)(2,1)S(1)} collective-permute-done((bf16[256,256]{1,0:T(8,128)(2,1)S(1)}, bf16[256,256]{1,0:T(8,128)(2,1)S(1)}, u32[]{:S(2)}, u32[]{:S(2)}) %collective-permute-start.5) | collective-permute-done | bytes 131104 | tf_op jit(solution)/shard_map/ppermute | solution.py:239
  39.7 0.1 collective-permute-start.7
  39.8 3.7 %collective-permute-start.8 = (bf16[3,256,256]{2,1,0:T(8,128)(2,1)S(1)}, bf16[3,256,256]{2,1,0:T(8,128)(2,1)S(1)}, u32[]{:S(2)}, u32[]{:S(2)}) collective-permute-start(bf16[3,256,256]{2,1,0:T(8,128)(2,1)S(1)} %pad_maximum_fusion.1.own), channel_id=1, source_target_pairs={{0,124},{4,8},{8,4},{12,16},{16,12},{20,24},{24,20},{28,32},{32,28... | collective-permute-start | bytes 1179656 | tf_op jit(solution)/shard_map/ppermute | solution.py:247
  43.5 2.1 %shard_map.138.early = bf16[2048,256]{1,0:T(8,128)(2,1)S(1)} custom-call(s16[2048,128]{1,0:T(8,128)(2,1)S(1)} %get-tuple-element.43.sources, s16[2048,128]{1,0:T(8,128)(2,1)S(1)} %get-tuple-element.44.targets, bf16[3,256,256]{2,1,0:T(8,128)(2,1)S(1)} %pad_maximum_fusion.1.own, bf16[3,256,256]{2,1,0:T(8,128)(2,1)S(1)} %collective-permute-done.7.chip, ...), custom_call_target="tpu_custom_call" | custom-call | flops 1610612736 | bytes 1048576 | tf_op jit(solution)/shard_map/pallas_call | solution.py:285
  45.6 4.8 %collective-permute-done.8.cross = bf16[3,256,256]{2,1,0:T(8,128)(2,1)S(1)} collective-permute-done((bf16[3,256,256]{2,1,0:T(8,128)(2,1)S(1)}, bf16[3,256,256]{2,1,0:T(8,128)(2,1)S(1)}, u32[]{:S(2)}, u32[]{:S(2)}) %collective-permute-start.8) | collective-permute-done | bytes 393248 | tf_op jit(solution)/shard_map/ppermute | solution.py:247
  50.4 2.0 %shard_map.139 = (bf16[256,256]{1,0:T(8,128)(2,1)S(1)}, bf16[256,256]{1,0:T(8,128)(2,1)S(1)}) custom-call(s16[2048,128]{1,0:T(8,128)(2,1)S(1)} %get-tuple-element.43.sources, bf16[2048,256]{1,0:T(8,128)(2,1)S(1)} %shard_map.138.early, bf16[3,256,256]{2,1,0:T(8,128)(2,1)S(1)} %collective-permute-done.8.cross, ...), custom_call_target="tpu_custom_call" | custom-call | flops 805306368 | bytes 1048576 | tf_op jit(solution)/shard_map/pallas_call | solution.py:292
  52.4 1.3 %collective-permute-start.10 = (bf16[256,256]{1,0:T(8,128)(2,1)S(1)}, bf16[256,256]{1,0:T(8,128)(2,1)S(1)}, u32[]{:S(2)}, u32[]{:S(2)}) collective-permute-start(bf16[256,256]{1,0:T(8,128)(2,1)S(1)} %get-tuple-element.53), channel_id=1, source_target_pairs={{0,3},{1,2},{2,1},{3,0},{4,7},{5,6},{6,5},{7,4},{8,11},{9,10},{10,... | collective-permute-start | bytes 393224 | tf_op jit(solution)/shard_map/ppermute | solution.py:239
  53.7 5.0 %collective-permute-done.10 = bf16[256,256]{1,0:T(8,128)(2,1)S(1)} collective-permute-done((bf16[256,256]{1,0:T(8,128)(2,1)S(1)}, bf16[256,256]{1,0:T(8,128)(2,1)S(1)}, u32[]{:S(2)}, u32[]{:S(2)}) %collective-permute-start.10) | collective-permute-done | bytes 131104 | tf_op jit(solution)/shard_map/ppermute | solution.py:239
  58.7 0.1 collective-permute-start.11
  58.8 2.8 %collective-permute-start.12 = (bf16[3,256,256]{2,1,0:T(8,128)(2,1)S(1)}, bf16[3,256,256]{2,1,0:T(8,128)(2,1)S(1)}, u32[]{:S(2)}, u32[]{:S(2)}) collective-permute-start(bf16[3,256,256]{2,1,0:T(8,128)(2,1)S(1)} %pad_maximum_fusion.2.own), channel_id=1, source_target_pairs={{0,124},{4,8},{8,4},{12,16},{16,12},{20,24},{24,20},{28,32},{32,28... | collective-permute-start | bytes 1179656 | tf_op jit(solution)/shard_map/ppermute | solution.py:247
  61.6 2.1 %shard_map.140.early = bf16[2048,256]{1,0:T(8,128)(2,1)S(1)} custom-call(s16[2048,128]{1,0:T(8,128)(2,1)S(1)} %get-tuple-element.43.sources, s16[2048,128]{1,0:T(8,128)(2,1)S(1)} %get-tuple-element.44.targets, bf16[3,256,256]{2,1,0:T(8,128)(2,1)S(1)} %pad_maximum_fusion.2.own, bf16[3,256,256]{2,1,0:T(8,128)(2,1)S(1)} %collective-permute-done.11.chip, ...), custom_call_target="tpu_custom_call" | custom-call | flops 1610612736 | bytes 1048576 | tf_op jit(solution)/shard_map/pallas_call | solution.py:285
  63.7 5.9 %collective-permute-done.12.cross = bf16[3,256,256]{2,1,0:T(8,128)(2,1)S(1)} collective-permute-done((bf16[3,256,256]{2,1,0:T(8,128)(2,1)S(1)}, bf16[3,256,256]{2,1,0:T(8,128)(2,1)S(1)}, u32[]{:S(2)}, u32[]{:S(2)}) %collective-permute-start.12) | collective-permute-done | bytes 393248 | tf_op jit(solution)/shard_map/ppermute | solution.py:247
  69.6 2.0 %shard_map.141 = (bf16[256,256]{1,0:T(8,128)(2,1)S(1)}, bf16[256,256]{1,0:T(8,128)(2,1)S(1)}) custom-call(s16[2048,128]{1,0:T(8,128)(2,1)S(1)} %get-tuple-element.43.sources, bf16[2048,256]{1,0:T(8,128)(2,1)S(1)} %shard_map.140.early, bf16[3,256,256]{2,1,0:T(8,128)(2,1)S(1)} %collective-permute-done.12.cross, ...), custom_call_target="tpu_custom_call" | custom-call | flops 805306368 | bytes 1048576 | tf_op jit(solution)/shard_map/pallas_call | solution.py:292
  71.6 1.5 %collective-permute-start.15 = (bf16[256,256]{1,0:T(8,128)(2,1)S(1)}, bf16[256,256]{1,0:T(8,128)(2,1)S(1)}, u32[]{:S(2)}, u32[]{:S(2)}) collective-permute-start(bf16[256,256]{1,0:T(8,128)(2,1)S(1)} %get-tuple-element.55.own), channel_id=1, source_target_pairs={{0,2},{1,3},{2,0},{3,1},{4,6},{5,7},{6,4},{7,5},{8,10},{9,11},{10,... | collective-permute-start | bytes 393224 | tf_op jit(solution)/shard_map/ppermute | solution.py:239
  73.2 1.2 %collective-permute-start.14 = (bf16[256,256]{1,0:T(8,128)(2,1)S(1)}, bf16[256,256]{1,0:T(8,128)(2,1)S(1)}, u32[]{:S(2)}, u32[]{:S(2)}) collective-permute-start(bf16[256,256]{1,0:T(8,128)(2,1)S(1)} %get-tuple-element.55.own), channel_id=1, source_target_pairs={{0,3},{1,2},{2,1},{3,0},{4,7},{5,6},{6,5},{7,4},{8,11},{9,10},{10,... | collective-permute-start | bytes 393224 | tf_op jit(solution)/shard_map/ppermute | solution.py:239
  74.4 0.8 collective-permute-start.13
  75.2 2.4 %shard_map.142 = (bf16[6144,256]{1,0:T(8,128)(2,1)S(1)}, bf16[256,256]{1,0:T(8,128)(2,1)}) custom-call(s16[6144,128]{1,0:T(8,128)(2,1)S(1)} %shard_map.134.sources, bf16[256,256]{1,0:T(8,128)(2,1)S(1)} %get-tuple-element.55.own, bf16[2048,256]{1,0:T(8,128)(2,1)S(1)} %shard_map.135.proj, bf16[256,256]{1,0:T(8,128)(2,1)S(1)} %get-tuple-element.57.latent), custom_call_target="tpu_custom_call" | custom-call | flops 805306368 | bytes 1048576 | tf_op jit(solution)/shard_map/pallas_call | solution.py:336
  77.6 0.6 collective-permute-done.15
  78.2 1.4 %collective-permute-done.14 = bf16[256,256]{1,0:T(8,128)(2,1)S(1)} collective-permute-done((bf16[256,256]{1,0:T(8,128)(2,1)S(1)}, bf16[256,256]{1,0:T(8,128)(2,1)S(1)}, u32[]{:S(2)}, u32[]{:S(2)}) %collective-permute-start.14) | collective-permute-done | bytes 131104 | tf_op jit(solution)/shard_map/ppermute | solution.py:239
  79.6 0.1 pad_maximum_fusion.own
  79.7 0.1 collective-permute-start.16
  79.8 1.9 %collective-permute-start.17 = (bf16[4,256,256]{2,1,0:T(8,128)(2,1)S(1)}, bf16[4,256,256]{2,1,0:T(8,128)(2,1)S(1)}, u32[]{:S(2)}, u32[]{:S(2)}) collective-permute-start(bf16[4,256,256]{2,1,0:T(8,128)(2,1)S(1)} %pad_maximum_fusion.own), channel_id=1, source_target_pairs={{0,124},{4,8},{8,4},{12,16},{16,12},{20,24},{24,20},{28,32},{32,28... | collective-permute-start | bytes 1572872 | tf_op jit(solution)/shard_map/ppermute | solution.py:247
  81.6 0.0 collective-permute-done.16.chip
  81.7 6.9 %shard_map.143.early = bf16[6144,256]{1,0:T(8,128)(2,1)S(1)} custom-call(s16[6144,128]{1,0:T(8,128)(2,1)S(1)} %shard_map.134.sources, bf16[6144,256]{1,0:T(8,128)(2,1)S(1)} %get-tuple-element.59.before, bf16[4,256,256]{2,1,0:T(8,128)(2,1)S(1)} %pad_maximum_fusion.own, bf16[4,256,256]{2,1,0:T(8,128)(2,1)S(1)} %collective-permute-done.16.chip), custom_call_target="tpu_custom_call" | custom-call | flops 5637144576 | bytes 1048576 | tf_op jit(solution)/shard_map/pallas_call | solution.py:346
  88.6 3.2 %collective-permute-done.17.cross = bf16[4,256,256]{2,1,0:T(8,128)(2,1)S(1)} collective-permute-done((bf16[4,256,256]{2,1,0:T(8,128)(2,1)S(1)}, bf16[4,256,256]{2,1,0:T(8,128)(2,1)S(1)}, u32[]{:S(2)}, u32[]{:S(2)}) %collective-permute-start.17) | collective-permute-done | bytes 524320 | tf_op jit(solution)/shard_map/ppermute | solution.py:247
  91.8 6.5 %shard_map.144 = bf16[2048,256]{1,0:T(8,128)(2,1)} custom-call(s16[6144,128]{1,0:T(8,128)(2,1)S(1)} %shard_map.134.sources, bf16[6144,256]{1,0:T(8,128)(2,1)S(1)} %shard_map.143.early, bf16[4,256,256]{2,1,0:T(8,128)(2,1)S(1)} %collective-permute-done.17.cross, bf16[2048,256]{1,0:T(8,128)(2,1)S(1)} %copy-done.2, bf16[4,256]{1,0:T(4,128)(2,1)S(1)} %copy-done.5, ...), custom_call_target="tpu_custom_call" | custom-call | flops 1000000000 | bytes 1048576 | tf_op jit(solution)/shard_map/pallas_call | solution.py:353
  (36 shorter events, 0.3 us)
Async XLA Ops:
  0.6 9.2 %copy-start.2 = (bf16[2048,256]{1,0:T(8,128)(2,1)S(1)}, bf16[2048,256]{1,0:T(8,128)(2,1)}, u32[]{:S(2)}) copy-start(bf16[2048,256]{1,0:T(8,128)(2,1)} %grid.3) | copy-start | bytes 3145732
  0.6 9.2 %copy-start.11 = (s32[2048,3]{0,1:T(4,128)S(1)}, s32[2048,3]{0,1:T(4,128)}, u32[]{:S(2)}) copy-start(s32[2048,3]{0,1:T(4,128)} %param.19) | copy-start | bytes 73732
  0.7 9.2 %copy-start.1 = (bf16[4,256,256]{2,1,0:T(8,128)(2,1)S(1)}, bf16[4,256,256]{2,1,0:T(8,128)(2,1)}, u32[]{:S(2)}) copy-start(bf16[4,256,256]{2,1,0:T(8,128)(2,1)} %weights.17) | copy-start | bytes 1572868
  5.2 9.1 %collective-permute-start = (bf16[3,128,256]{2,1,0:T(8,128)(2,1)}, bf16[3,128,256]{2,1,0:T(8,128)(2,1)}, u32[]{:S(2)}, u32[]{:S(2)}) collective-permute-start(bf16[3,128,256]{2,1,0:T(8,128)(2,1)} %get-tuple-element.33), channel_id=1, source_target_pairs={{0,1},{1,0},{2,3},{3,2},{4,5},{5,4},{6,7},{7,6},{8,9},{9,8},{10,11... | collective-permute-start | bytes 589832 | tf_op jit(solution)/shard_map/ppermute | solution.py:239
  6.9 10.6 %collective-permute-start.1 = (bf16[3,128,256]{2,1,0:T(8,128)(2,1)}, bf16[3,128,256]{2,1,0:T(8,128)(2,1)S(1)}, u32[]{:S(2)}, u32[]{:S(2)}) collective-permute-start(bf16[3,128,256]{2,1,0:T(8,128)(2,1)} %get-tuple-element.34), channel_id=1, source_target_pairs={{0,3},{1,2},{2,1},{3,0},{4,7},{5,6},{6,5},{7,4},{8,11},{9,10},{10,... | collective-permute-start | bytes 589832 | tf_op jit(solution)/shard_map/ppermute | solution.py:239
  9.1 9.8 %collective-permute-start.2 = (bf16[3,128,256]{2,1,0:T(8,128)(2,1)}, bf16[3,128,256]{2,1,0:T(8,128)(2,1)S(1)}, u32[]{:S(2)}, u32[]{:S(2)}) collective-permute-start(bf16[3,128,256]{2,1,0:T(8,128)(2,1)} %get-tuple-element.35), channel_id=1, source_target_pairs={{0,2},{1,3},{2,0},{3,1},{4,6},{5,7},{6,4},{7,5},{8,10},{9,11},{10,... | collective-permute-start | bytes 589832 | tf_op jit(solution)/shard_map/ppermute | solution.py:239
  10.3 0.9 copy-start.8
  10.3 0.9 copy-start.9
  11.2 1.0 %copy-start.6 = (s32[4096]{0:T(1024)S(1)}, s32[4096]{0:T(1024)}, u32[]{:S(2)}) copy-start(s32[4096]{0:T(1024)} %param.15) | copy-start | bytes 49156
  11.2 1.0 %copy-start.7 = (s32[4096]{0:T(1024)S(1)}, s32[4096]{0:T(1024)}, u32[]{:S(2)}) copy-start(s32[4096]{0:T(1024)} %param.16) | copy-start | bytes 49156
  12.2 2.0 %copy-start.10 = (bf16[3,128,256]{2,1,0:T(8,128)(2,1)S(1)}, bf16[3,128,256]{2,1,0:T(8,128)(2,1)}, u32[]{:S(2)}) copy-start(bf16[3,128,256]{2,1,0:T(8,128)(2,1)} %get-tuple-element.32) | copy-start | bytes 589828
  14.2 11.3 %copy-start.3 = (bf16[4,256,256]{2,1,0:T(8,128)(2,1)S(1)}, bf16[4,256,256]{2,1,0:T(8,128)(2,1)}, u32[]{:S(2)}) copy-start(bf16[4,256,256]{2,1,0:T(8,128)(2,1)} %weights.12) | copy-start | bytes 1572868
  14.3 11.3 %copy-start.4 = (bf16[256,256]{1,0:T(8,128)(2,1)S(1)}, bf16[256,256]{1,0:T(8,128)(2,1)}, u32[]{:S(2)}) copy-start(bf16[256,256]{1,0:T(8,128)(2,1)} %latent.3) | copy-start | bytes 393220
  19.0 6.5 %collective-permute-start.3 = (bf16[4,128,256]{2,1,0:T(8,128)(2,1)S(1)}, bf16[4,128,256]{2,1,0:T(8,128)(2,1)S(1)}, u32[]{:S(2)}, u32[]{:S(2)}) collective-permute-start(bf16[4,128,256]{2,1,0:T(8,128)(2,1)S(1)} %get-tuple-element.47), channel_id=1, source_target_pairs={{0,4},{4,0},{8,12},{12,8},{16,20},{20,16},{24,28},{28,24},{32,36},... | collective-permute-start | bytes 786440 | tf_op jit(solution)/shard_map/ppermute | solution.py:243
  19.1 10.4 %collective-permute-start.4 = (bf16[4,128,256]{2,1,0:T(8,128)(2,1)S(1)}, bf16[4,128,256]{2,1,0:T(8,128)(2,1)S(1)}, u32[]{:S(2)}, u32[]{:S(2)}) collective-permute-start(bf16[4,128,256]{2,1,0:T(8,128)(2,1)S(1)} %get-tuple-element.48), channel_id=1, source_target_pairs={{0,124},{4,8},{8,4},{12,16},{16,12},{20,24},{24,20},{28,32},{32,28... | collective-permute-start | bytes 786440 | tf_op jit(solution)/shard_map/ppermute | solution.py:247
  25.5 4.0 %copy-start = (bf16[8,256,256]{2,1,0:T(8,128)(2,1)S(1)}, bf16[8,256,256]{2,1,0:T(8,128)(2,1)}, u32[]{:S(2)}) copy-start(bf16[8,256,256]{2,1,0:T(8,128)(2,1)} %weights.16) | copy-start | bytes 3145732
  25.5 4.0 %copy-start.5 = (bf16[4,256]{1,0:T(4,128)(2,1)S(1)}, bf16[4,256]{1,0:T(4,128)(2,1)}, u32[]{:S(2)}) copy-start(bf16[4,256]{1,0:T(4,128)(2,1)} %gain.1) | copy-start | bytes 6148
  32.4 6.3 %collective-permute-start.6 = (bf16[256,256]{1,0:T(8,128)(2,1)S(1)}, bf16[256,256]{1,0:T(8,128)(2,1)S(1)}, u32[]{:S(2)}, u32[]{:S(2)}) collective-permute-start(bf16[256,256]{1,0:T(8,128)(2,1)S(1)} %get-tuple-element.50), channel_id=1, source_target_pairs={{0,3},{1,2},{2,1},{3,0},{4,7},{5,6},{6,5},{7,4},{8,11},{9,10},{10,... | collective-permute-start | bytes 393224 | tf_op jit(solution)/shard_map/ppermute | solution.py:239
  34.6 5.0 %collective-permute-start.5 = (bf16[256,256]{1,0:T(8,128)(2,1)S(1)}, bf16[256,256]{1,0:T(8,128)(2,1)S(1)}, u32[]{:S(2)}, u32[]{:S(2)}) collective-permute-start(bf16[256,256]{1,0:T(8,128)(2,1)S(1)} %get-tuple-element.50), channel_id=1, source_target_pairs={{0,1},{1,0},{2,3},{3,2},{4,5},{5,4},{6,7},{7,6},{8,9},{9,8},{10,11... | collective-permute-start | bytes 393224 | tf_op jit(solution)/shard_map/ppermute | solution.py:239
  39.7 3.8 %collective-permute-start.7 = (bf16[3,256,256]{2,1,0:T(8,128)(2,1)S(1)}, bf16[3,256,256]{2,1,0:T(8,128)(2,1)S(1)}, u32[]{:S(2)}, u32[]{:S(2)}) collective-permute-start(bf16[3,256,256]{2,1,0:T(8,128)(2,1)S(1)} %pad_maximum_fusion.1.own), channel_id=1, source_target_pairs={{0,4},{4,0},{8,12},{12,8},{16,20},{20,16},{24,28},{28,24},{32,36},... | collective-permute-start | bytes 1179656 | tf_op jit(solution)/shard_map/ppermute | solution.py:243
  39.8 10.6 %collective-permute-start.8 = (bf16[3,256,256]{2,1,0:T(8,128)(2,1)S(1)}, bf16[3,256,256]{2,1,0:T(8,128)(2,1)S(1)}, u32[]{:S(2)}, u32[]{:S(2)}) collective-permute-start(bf16[3,256,256]{2,1,0:T(8,128)(2,1)S(1)} %pad_maximum_fusion.1.own), channel_id=1, source_target_pairs={{0,124},{4,8},{8,4},{12,16},{16,12},{20,24},{24,20},{28,32},{32,28... | collective-permute-start | bytes 1179656 | tf_op jit(solution)/shard_map/ppermute | solution.py:247
  52.4 6.3 %collective-permute-start.10 = (bf16[256,256]{1,0:T(8,128)(2,1)S(1)}, bf16[256,256]{1,0:T(8,128)(2,1)S(1)}, u32[]{:S(2)}, u32[]{:S(2)}) collective-permute-start(bf16[256,256]{1,0:T(8,128)(2,1)S(1)} %get-tuple-element.53), channel_id=1, source_target_pairs={{0,3},{1,2},{2,1},{3,0},{4,7},{5,6},{6,5},{7,4},{8,11},{9,10},{10,... | collective-permute-start | bytes 393224 | tf_op jit(solution)/shard_map/ppermute | solution.py:239
  53.7 5.0 %collective-permute-start.9 = (bf16[256,256]{1,0:T(8,128)(2,1)S(1)}, bf16[256,256]{1,0:T(8,128)(2,1)S(1)}, u32[]{:S(2)}, u32[]{:S(2)}) collective-permute-start(bf16[256,256]{1,0:T(8,128)(2,1)S(1)} %get-tuple-element.53), channel_id=1, source_target_pairs={{0,1},{1,0},{2,3},{3,2},{4,5},{5,4},{6,7},{7,6},{8,9},{9,8},{10,11... | collective-permute-start | bytes 393224 | tf_op jit(solution)/shard_map/ppermute | solution.py:239
  58.7 2.9 %collective-permute-start.11 = (bf16[3,256,256]{2,1,0:T(8,128)(2,1)S(1)}, bf16[3,256,256]{2,1,0:T(8,128)(2,1)S(1)}, u32[]{:S(2)}, u32[]{:S(2)}) collective-permute-start(bf16[3,256,256]{2,1,0:T(8,128)(2,1)S(1)} %pad_maximum_fusion.2.own), channel_id=1, source_target_pairs={{0,4},{4,0},{8,12},{12,8},{16,20},{20,16},{24,28},{28,24},{32,36},... | collective-permute-start | bytes 1179656 | tf_op jit(solution)/shard_map/ppermute | solution.py:243
  58.8 10.8 %collective-permute-start.12 = (bf16[3,256,256]{2,1,0:T(8,128)(2,1)S(1)}, bf16[3,256,256]{2,1,0:T(8,128)(2,1)S(1)}, u32[]{:S(2)}, u32[]{:S(2)}) collective-permute-start(bf16[3,256,256]{2,1,0:T(8,128)(2,1)S(1)} %pad_maximum_fusion.2.own), channel_id=1, source_target_pairs={{0,124},{4,8},{8,4},{12,16},{16,12},{20,24},{24,20},{28,32},{32,28... | collective-permute-start | bytes 1179656 | tf_op jit(solution)/shard_map/ppermute | solution.py:247
  71.6 6.6 %collective-permute-start.15 = (bf16[256,256]{1,0:T(8,128)(2,1)S(1)}, bf16[256,256]{1,0:T(8,128)(2,1)S(1)}, u32[]{:S(2)}, u32[]{:S(2)}) collective-permute-start(bf16[256,256]{1,0:T(8,128)(2,1)S(1)} %get-tuple-element.55.own), channel_id=1, source_target_pairs={{0,2},{1,3},{2,0},{3,1},{4,6},{5,7},{6,4},{7,5},{8,10},{9,11},{10,... | collective-permute-start | bytes 393224 | tf_op jit(solution)/shard_map/ppermute | solution.py:239
  73.2 6.4 %collective-permute-start.14 = (bf16[256,256]{1,0:T(8,128)(2,1)S(1)}, bf16[256,256]{1,0:T(8,128)(2,1)S(1)}, u32[]{:S(2)}, u32[]{:S(2)}) collective-permute-start(bf16[256,256]{1,0:T(8,128)(2,1)S(1)} %get-tuple-element.55.own), channel_id=1, source_target_pairs={{0,3},{1,2},{2,1},{3,0},{4,7},{5,6},{6,5},{7,4},{8,11},{9,10},{10,... | collective-permute-start | bytes 393224 | tf_op jit(solution)/shard_map/ppermute | solution.py:239
  74.4 5.2 %collective-permute-start.13 = (bf16[256,256]{1,0:T(8,128)(2,1)S(1)}, bf16[256,256]{1,0:T(8,128)(2,1)S(1)}, u32[]{:S(2)}, u32[]{:S(2)}) collective-permute-start(bf16[256,256]{1,0:T(8,128)(2,1)S(1)} %get-tuple-element.55.own), channel_id=1, source_target_pairs={{0,1},{1,0},{2,3},{3,2},{4,5},{5,4},{6,7},{7,6},{8,9},{9,8},{10,11... | collective-permute-start | bytes 393224 | tf_op jit(solution)/shard_map/ppermute | solution.py:239
  79.7 2.0 %collective-permute-start.16 = (bf16[4,256,256]{2,1,0:T(8,128)(2,1)S(1)}, bf16[4,256,256]{2,1,0:T(8,128)(2,1)S(1)}, u32[]{:S(2)}, u32[]{:S(2)}) collective-permute-start(bf16[4,256,256]{2,1,0:T(8,128)(2,1)S(1)} %pad_maximum_fusion.own), channel_id=1, source_target_pairs={{0,4},{4,0},{8,12},{12,8},{16,20},{20,16},{24,28},{28,24},{32,36},... | collective-permute-start | bytes 1572872 | tf_op jit(solution)/shard_map/ppermute | solution.py:243
  79.8 12.0 %collective-permute-start.17 = (bf16[4,256,256]{2,1,0:T(8,128)(2,1)S(1)}, bf16[4,256,256]{2,1,0:T(8,128)(2,1)S(1)}, u32[]{:S(2)}, u32[]{:S(2)}) collective-permute-start(bf16[4,256,256]{2,1,0:T(8,128)(2,1)S(1)} %pad_maximum_fusion.own), channel_id=1, source_target_pairs={{0,124},{4,8},{8,4},{12,16},{16,12},{20,24},{24,20},{28,32},{32,28... | collective-permute-start | bytes 1572872 | tf_op jit(solution)/shard_map/ppermute | solution.py:247
